TPU v7x, 256 devices: a whole 4x4x8 slice. The times are simulated.
256 devices in a mesh: dom: 32 (over y, x, core), sub: 8 (over z).
Axes of the slice: x: 4, y: 4, z: 8, core: 2. Of those that a mesh axis runs over, the one named last changes fastest.
Arguments:
- interior_inverse: bfloat16 [80, 80, 32768], P(None, None, ('dom', 'sub'))
- coupling: bfloat16 [80, 48, 32768], P(None, None, ('dom', 'sub')), may hold values from -0.26953125 to 0.26953125
- trace_block: bfloat16 [48, 48, 32768], P(None, None, ('dom', 'sub'))
- interior_load: bfloat16 [80, 32768], P(None, ('dom', 'sub')), may hold values from -6 to 6
- trace_load: float32 [12, 65536], P(None, ('dom', 'sub'))
- face_shift: float32 [12, 65536], P(None, ('dom', 'sub')), may hold values from 0.2 to 2
- element_faces: int32 [4, 32768], P(None, ('dom', 'sub')), may hold values from 0 to 2175, as said below
- block_padding: int32 [256], P(('dom', 'sub')), may hold values from 0 to 96
Outputs:
- traces: float32 [12, 65536], P(None, ('dom', 'sub'))
- interior: float32 [80, 32768], P(None, ('dom', 'sub'))
Inputs may be any that keep to these rules, and one draw needn't show every extreme that they name: `element_faces`: within each partition the indices form one shuffled list: each of the partition's faces except its last 128 is named twice, each of its last 128 faces once, and each index below 128 once.
All inputs are finite; a program needn't handle non-finite values.
Results may differ from a plain program's by a relative error of at most 0.0029.
Values may be sent and summed in bfloat16 or wider, within the bound.
No kernel may reach another device: no remote copies, remote signals or barrier semaphores. Data moves between devices by JAX's collectives and lax.ppermute only.
A program may use at most 64 MiB of HBM per device.

v0:
```python
import jax
import jax.numpy as jnp
from jax import lax
from jax.sharding import PartitionSpec as P

BLOCK = 128
RIM = 128
ITERS = 3


def shifted(value, axis, steps):
    count = lax.axis_size(axis)
    first, last = (max(0, -steps), min(count, count - steps))
    return lax.ppermute(value, axis, [(source, source + steps) for source in range(first, last)])


def element_section(interior_inverse, coupling, trace_block, interior_load, living):
    coupled = jnp.einsum(
        "ijE,jkE->ikE", interior_inverse, coupling, preferred_element_type=jnp.float32
    ).astype(jnp.bfloat16)
    condensed = trace_block.astype(jnp.float32) + jnp.einsum(
        "jiE,jkE->ikE", coupling, coupled, preferred_element_type=jnp.float32
    )
    solved = jnp.einsum(
        "ijE,jE->iE", interior_inverse, interior_load, preferred_element_type=jnp.float32
    )
    pushed = jnp.einsum(
        "jiE,jE->iE", coupling, solved.astype(jnp.bfloat16), preferred_element_type=jnp.float32
    )
    return (coupled, condensed, solved, pushed * living)


def whole_partition(vector):
    return lax.all_gather(vector, "sub", axis=1, tiled=True)


def pick_faces(extended, element_faces, face_rows):
    picked = jnp.take(extended, element_faces.reshape(-1), axis=1)
    return picked.reshape(face_rows * element_faces.shape[0], element_faces.shape[1])


def spread(gathered, element_faces):
    rim_edge = shifted(gathered[:, -RIM:], "dom", 1)
    extended = jnp.concatenate([rim_edge, gathered], axis=1)
    return pick_faces(extended, element_faces, gathered.shape[0])


def spread_final(gathered, element_faces):
    rim_edge = shifted(gathered[:, -RIM:], "dom", 1)
    extended = jnp.concatenate([rim_edge, gathered], axis=1)
    return pick_faces(extended, element_faces, gathered.shape[0])


def collect(element_terms, element_faces, face_count):
    face_rows = element_terms.shape[0] // element_faces.shape[0]
    flattened = element_terms.reshape(face_rows, -1)
    summed = (
        jnp.zeros((face_rows, face_count + RIM), jnp.float32)
        .at[:, element_faces.reshape(-1)]
        .add(flattened)
    )
    returned = shifted(summed[:, :RIM], "dom", -1)
    partial_sums = summed[:, RIM:]
    return partial_sums.at[:, -RIM:].add(returned)


def conjugate(operate, right_side, own_part):

    def squares(vector):
        mine = own_part(vector)
        return lax.psum(jnp.sum(mine * mine), ("dom", "sub"))

    solution = jnp.zeros_like(right_side)
    residual = right_side
    direction = right_side
    norm_now = squares(residual)
    for iteration in range(ITERS):
        image = operate(direction)
        curving = lax.psum(jnp.sum(own_part(direction) * own_part(image)), ("dom", "sub"))
        step_size = norm_now / curving
        solution = solution + step_size * direction
        residual = residual - step_size * image
        norm_next = squares(residual)
        direction = residual + norm_next / norm_now * direction
        norm_now = norm_next
    return solution


def on_device(
    interior_inverse,
    coupling,
    trace_block,
    interior_load,
    trace_load,
    face_shift,
    element_faces,
    block_padding,
):
    elements = element_faces.shape[1]
    position = jnp.arange(elements, dtype=jnp.int32)
    padding_here = jnp.repeat(block_padding, BLOCK, total_repeat_length=elements)
    living = (position % BLOCK < BLOCK - padding_here).astype(jnp.float32)
    coupled, condensed, solved, pushed = element_section(
        interior_inverse, coupling, trace_block, interior_load, living
    )
    face_count = trace_load.shape[1]
    partition_faces = face_count * lax.axis_size("sub")

    def assemble(element_terms):
        partial_sums = collect(element_terms, element_faces, partition_faces)
        return lax.psum_scatter(partial_sums, "sub", scatter_dimension=1, tiled=True)

    def element_view(vector):
        return spread(whole_partition(vector), element_faces)

    def own_part(vector):
        return vector

    right_side = trace_load + assemble(pushed)

    def operate(vector):
        element_terms = (
            jnp.einsum(
                "ijE,jE->iE", condensed, element_view(vector), precision=lax.Precision.HIGHEST
            )
            * living
        )
        return assemble(element_terms) + face_shift * vector

    solution = conjugate(operate, right_side, own_part)
    solution_half = solution.astype(jnp.bfloat16)
    partition_half = lax.all_gather(solution_half, "sub", axis=1, tiled=True)
    traces_half = spread_final(partition_half, element_faces)
    lifted = jnp.einsum("ijE,jE->iE", coupled, traces_half, preferred_element_type=jnp.float32)
    interior = (solved - lifted) * living
    return (own_part(solution), interior)


def solution(mesh):
    placed = (
        P(None, None, ("dom", "sub")),
        P(None, None, ("dom", "sub")),
        P(None, None, ("dom", "sub")),
        P(None, ("dom", "sub")),
        P(None, ("dom", "sub")),
        P(None, ("dom", "sub")),
        P(None, ("dom", "sub")),
        P(("dom", "sub")),
    )
    return jax.shard_map(
        on_device,
        mesh=mesh,
        in_specs=placed,
        out_specs=(P(None, ("dom", "sub")), P(None, ("dom", "sub"))),
        check_vma=False,
    )
```

profile of v0, /device:TPU:1, one launch (start us, length us, event | category | flops | bytes accessed | tf_op | source)
XLA Modules:
  0.0 743.7 jit_solution(13571383672650835492)
XLA Ops:
  11.1 2.5 scatter_custom_fusion
  14.6 5.1 collective-permute-start
  19.8 2.3 copy.89
  22.1 3.9 copy.90
  26.0 4.4 convolution_convert_fusion
  32.7 31.8 %reduce-scatter.5.cloned.1.call-done = f32[12,256]{1,0:T(8,128)} async-done(((f32[12,2048]{1,0:T(8,128)}), f32[12,256]{1,0:T(8,128)}) %reduce-scatter.5.cloned.1.call-update) | async-done | bytes 12304 | tf_op jit(solution)/shard_map/reduce_scatter | solution.py:111
  65.3 18.2 %all_gather.12 = f32[12,2048]{1,0:T(8,128)S(1)} all-gather(f32[12,256]{1,0:T(8,128)S(1)} %add.144), channel_id=1, replica_groups=mesh['dom'=32,'sub'=8] {'sub'}, dimensions={1}, use_global_device_ids=true | all-gather | bytes 110592 | tf_op jit(solution)/shard_map/all_gather | solution.py:34
  83.5 15.4 %collective-permute-start.1 = (f32[12,128]{1,0:T(8,128)S(1)}, f32[12,128]{1,0:T(8,128)S(1)}, u32[]{:S(2)}, u32[]{:S(2)}) collective-permute-start(f32[12,128]{1,0:T(8,128)S(1)} %slice.161), channel_id=1, source_target_pairs={{0,8},{8,16},{16,24},{24,32},{32,40},{40,48},{48,56},{56,64},{64,7... | collective-permute-start | bytes 18440 | tf_op jit(solution)/shard_map/ppermute | solution.py:14
  102.7 3.4 multiply_reduce_fusion.4
  106.3 3.3 scatter_custom_fusion.1
  112.6 2.3 slice.162
  117.3 29.9 %reduce-scatter.7.cloned.1.call-done = f32[12,256]{1,0:T(8,128)} async-done(((f32[12,2048]{1,0:T(8,128)}), f32[12,256]{1,0:T(8,128)}) %reduce-scatter.7.cloned.1.call-update) | async-done | bytes 12304 | tf_op jit(solution)/shard_map/reduce_scatter | solution.py:111
  148.5 80.4 %all-reduce = (f32[]{:T(128)}, f32[]{:T(128)}) all-reduce(f32[]{:T(128)} %get-tuple-element.84, f32[]{:T(128)} %get-tuple-element.83), channel_id=1, replica_groups=mesh['dom'=32,'sub'=8] {'dom','sub'}, use_global_device_ids=true, to_apply=%region_3.4 | all-reduce | flops 2 | bytes 16 | tf_op jit(solution)/shard_map/psum | solution.py:71
  231.7 73.4 %psum.44 = f32[]{:T(128)} all-reduce(f32[]{:T(128)} %get-tuple-element.91), channel_id=1, replica_groups=mesh['dom'=32,'sub'=8] {'dom','sub'}, use_global_device_ids=true, to_apply=%region_9.11 | all-reduce | flops 1 | bytes 8 | tf_op jit(solution)/shard_map/psum | solution.py:71
  306.5 18.5 %all_gather.13 = f32[12,2048]{1,0:T(8,128)S(1)} all-gather(f32[12,256]{1,0:T(8,128)S(1)} %multiply_add_fusion.3), channel_id=1, replica_groups=mesh['dom'=32,'sub'=8] {'sub'}, dimensions={1}, use_global_device_ids=true | all-gather | bytes 110592 | tf_op jit(solution)/shard_map/all_gather | solution.py:34
  325.1 9.3 %collective-permute-start.3 = (f32[12,128]{1,0:T(8,128)S(1)}, f32[12,128]{1,0:T(8,128)S(1)}, u32[]{:S(2)}, u32[]{:S(2)}) collective-permute-start(f32[12,128]{1,0:T(8,128)S(1)} %slice.165), channel_id=1, source_target_pairs={{0,8},{8,16},{16,24},{24,32},{32,40},{40,48},{48,56},{56,64},{64,7... | collective-permute-start | bytes 18440 | tf_op jit(solution)/shard_map/ppermute | solution.py:14
  338.1 2.9 gather_fusion.2
  343.5 3.4 scatter_custom_fusion.2
  349.8 2.3 slice.166
  354.5 30.9 %reduce-scatter.9.cloned.1.call-done = f32[12,256]{1,0:T(8,128)} async-done(((f32[12,2048]{1,0:T(8,128)}), f32[12,256]{1,0:T(8,128)}) %reduce-scatter.9.cloned.1.call-update) | async-done | bytes 12304 | tf_op jit(solution)/shard_map/reduce_scatter | solution.py:111
  386.7 80.3 %psum.45 = f32[]{:T(128)} all-reduce(f32[]{:T(128)} %multiply_reduce_fusion.8), channel_id=1, replica_groups=mesh['dom'=32,'sub'=8] {'dom','sub'}, use_global_device_ids=true, to_apply=%region_13.15 | all-reduce | flops 1 | bytes 8 | tf_op jit(solution)/shard_map/psum | solution.py:79
  469.8 73.3 %psum.46 = f32[]{:T(128)} all-reduce(f32[]{:T(128)} %get-tuple-element.89), channel_id=1, replica_groups=mesh['dom'=32,'sub'=8] {'dom','sub'}, use_global_device_ids=true, to_apply=%region_15.17 | all-reduce | flops 1 | bytes 8 | tf_op jit(solution)/shard_map/psum | solution.py:71
  544.4 18.5 %all_gather.14 = f32[12,2048]{1,0:T(8,128)S(1)} all-gather(f32[12,256]{1,0:T(8,128)S(1)} %multiply_add_fusion.1), channel_id=1, replica_groups=mesh['dom'=32,'sub'=8] {'sub'}, dimensions={1}, use_global_device_ids=true | all-gather | bytes 110592 | tf_op jit(solution)/shard_map/all_gather | solution.py:34
  563.0 9.3 %collective-permute-start.5 = (f32[12,128]{1,0:T(8,128)S(1)}, f32[12,128]{1,0:T(8,128)S(1)}, u32[]{:S(2)}, u32[]{:S(2)}) collective-permute-start(f32[12,128]{1,0:T(8,128)S(1)} %slice.169), channel_id=1, source_target_pairs={{0,8},{8,16},{16,24},{24,32},{32,40},{40,48},{48,56},{56,64},{64,7... | collective-permute-start | bytes 18440 | tf_op jit(solution)/shard_map/ppermute | solution.py:14
  573.7 2.3 copy.102
  576.0 2.9 gather_fusion.3
  581.5 2.5 scatter_custom_fusion.3
  586.5 3.1 collective-permute-done.6
  590.3 31.2 %reduce-scatter.11.cloned.1.call-done = f32[12,256]{1,0:T(8,128)} async-done(((f32[12,2048]{1,0:T(8,128)}), f32[12,256]{1,0:T(8,128)}) %reduce-scatter.11.cloned.1.call-update) | async-done | bytes 12304 | tf_op jit(solution)/shard_map/reduce_scatter | solution.py:111
  622.8 80.4 %psum.47 = f32[]{:T(128)} all-reduce(f32[]{:T(128)} %multiply_reduce_fusion.6), channel_id=1, replica_groups=mesh['dom'=32,'sub'=8] {'dom','sub'}, use_global_device_ids=true, to_apply=%region_19.21 | all-reduce | flops 1 | bytes 8 | tf_op jit(solution)/shard_map/psum | solution.py:79
  705.1 18.5 %all_gather.15 = bf16[12,2048]{1,0:T(8,128)(2,1)S(1)} all-gather(bf16[12,256]{1,0:T(8,128)(2,1)S(1)} %get-tuple-element.87), channel_id=1, replica_groups=mesh['dom'=32,'sub'=8] {'sub'}, dimensions={1}, use_global_device_ids=true | all-gather | bytes 55296 | tf_op jit(solution)/shard_map/all_gather | solution.py:132
  723.6 9.2 %collective-permute-start.7 = (bf16[12,128]{1,0:T(8,128)(2,1)S(1)}, bf16[12,128]{1,0:T(8,128)(2,1)S(1)}, u32[]{:S(2)}, u32[]{:S(2)}) collective-permute-start(bf16[12,128]{1,0:T(8,128)(2,1)S(1)} %slice.173), channel_id=1, source_target_pairs={{0,8},{8,16},{16,24},{24,32},{32,40},{40,48},{48,56},{56,64},{64,7... | collective-permute-start | bytes 9224 | tf_op jit(solution)/shard_map/ppermute | solution.py:14
  (152 shorter events, 46.7 us)
Async XLA Ops:
  7.2 3.5 copy-start.4
  7.2 57.4 %reduce-scatter.5.cloned.1.call-start = ((), (), s32[]{:S(2)}) async-start(), calls=%async_computation.4 | async-start | bytes 147456 | tf_op jit(solution)/shard_map/reduce_scatter | solution.py:111
  8.0 98.2 %copy-start.13 = (f32[128]{0:T(128)}, f32[128]{0:T(128)S(1)}, u32[]{:S(2)}) copy-start(f32[128]{0:T(128)S(1)} %compare_convert_fusion) | copy-start | bytes 1540
  8.7 2.3 copy-start.11
  11.1 95.3 %copy-start.18 = (s32[512,1]{0,1:T(1,128)}, s32[512,1]{0,1:T(1,128)S(1)}, u32[]{:S(2)}) copy-start(s32[512,1]{0,1:T(1,128)S(1)} %compare_select_fusion) | copy-start | bytes 6148
  13.6 1.0 copy-start.3
  13.6 8.5 %copy-start.2 = (bf16[80,80,128]{2,1,0:T(8,128)(2,1)S(1)}, bf16[80,80,128]{2,1,0:T(8,128)(2,1)}, u32[]{:S(2)}) copy-start(bf16[80,80,128]{2,1,0:T(8,128)(2,1)} %param.22) | copy-start | bytes 4915204
  14.6 17.3 %collective-permute-start = (f32[12,128]{1,0:T(8,128)S(1)}, f32[12,128]{1,0:T(8,128)S(1)}, u32[]{:S(2)}, u32[]{:S(2)}) collective-permute-start(f32[12,128]{1,0:T(8,128)S(1)} %copy.147), channel_id=1, source_target_pairs={{8,0},{16,8},{24,16},{32,24},{40,32},{48,40},{56,48},{64,56},{72,6... | collective-permute-start | bytes 18440 | tf_op jit(solution)/shard_map/ppermute | solution.py:14
  22.1 3.9 copy-start
  30.4 1.2 slice-start
  30.4 34.1 %copy-start.12 = (f32[12,256]{1,0:T(8,128)S(1)}, f32[12,256]{1,0:T(8,128)}, u32[]{:S(2)}) copy-start(f32[12,256]{1,0:T(8,128)} %param.26) | copy-start | bytes 36868
  30.4 68.6 %copy-start.5 = (bf16[48,48,128]{2,1,0:T(8,128)(2,1)S(1)}, bf16[48,48,128]{2,1,0:T(8,128)(2,1)}, u32[]{:S(2)}) copy-start(bf16[48,48,128]{2,1,0:T(8,128)(2,1)} %param.24) | copy-start | bytes 1769476
  31.9 0.6 copy-start.8
  32.6 114.6 %reduce-scatter.7.cloned.1.call-start = ((), (), s32[]{:S(2)}) async-start(), calls=%async_computation.5 | async-start | bytes 147456 | tf_op jit(solution)/shard_map/reduce_scatter | solution.py:111
  32.7 308.3 %copy-start.16 = (pred[512]{0:T(512)(128)(4,1)}, pred[512]{0:T(512)(128)(4,1)S(1)}, u32[]{:S(2)}) copy-start(pred[512]{0:T(512)(128)(4,1)S(1)} %compare_and_fusion) | copy-start | bytes 1540
  83.5 17.4 %collective-permute-start.1 = (f32[12,128]{1,0:T(8,128)S(1)}, f32[12,128]{1,0:T(8,128)S(1)}, u32[]{:S(2)}, u32[]{:S(2)}) collective-permute-start(f32[12,128]{1,0:T(8,128)S(1)} %slice.161), channel_id=1, source_target_pairs={{0,8},{8,16},{16,24},{24,32},{32,40},{40,48},{48,56},{56,64},{64,7... | collective-permute-start | bytes 18440 | tf_op jit(solution)/shard_map/ppermute | solution.py:14
  110.5 36.7 %copy-start.10 = (f32[12,256]{1,0:T(8,128)S(1)}, f32[12,256]{1,0:T(8,128)}, u32[]{:S(2)}) copy-start(f32[12,256]{1,0:T(8,128)} %param.27) | copy-start | bytes 36868
  110.5 6.0 collective-permute-start.2
  116.6 0.6 copy-start.9
  117.2 268.1 %reduce-scatter.9.cloned.1.call-start = ((), (), s32[]{:S(2)}) async-start(), calls=%async_computation.6 | async-start | bytes 147456 | tf_op jit(solution)/shard_map/reduce_scatter | solution.py:111
  325.1 10.1 %collective-permute-start.3 = (f32[12,128]{1,0:T(8,128)S(1)}, f32[12,128]{1,0:T(8,128)S(1)}, u32[]{:S(2)}, u32[]{:S(2)}) collective-permute-start(f32[12,128]{1,0:T(8,128)S(1)} %slice.165), channel_id=1, source_target_pairs={{0,8},{8,16},{16,24},{24,32},{32,40},{40,48},{48,56},{56,64},{64,7... | collective-permute-start | bytes 18440 | tf_op jit(solution)/shard_map/ppermute | solution.py:14
  342.3 1.1 copy-start.14
  347.9 5.9 collective-permute-start.4
  352.1 226.8 %copy-start.17 = (pred[512]{0:T(512)(128)(4,1)S(1)}, pred[512]{0:T(512)(128)(4,1)}, u32[]{:S(2)}) copy-start(pred[512]{0:T(512)(128)(4,1)} %copy-done.16) | copy-start | bytes 1540
  353.7 0.6 copy-start.6
  354.4 267.1 %reduce-scatter.11.cloned.1.call-start = ((), (), s32[]{:S(2)}) async-start(), calls=%async_computation.7 | async-start | bytes 147456 | tf_op jit(solution)/shard_map/reduce_scatter | solution.py:111
  563.0 10.0 %collective-permute-start.5 = (f32[12,128]{1,0:T(8,128)S(1)}, f32[12,128]{1,0:T(8,128)S(1)}, u32[]{:S(2)}, u32[]{:S(2)}) collective-permute-start(f32[12,128]{1,0:T(8,128)S(1)} %slice.169), channel_id=1, source_target_pairs={{0,8},{8,16},{16,24},{24,32},{32,40},{40,48},{48,56},{56,64},{64,7... | collective-permute-start | bytes 18440 | tf_op jit(solution)/shard_map/ppermute | solution.py:14
  580.2 1.1 copy-start.15
  580.2 1.3 copy-start.19
  584.1 5.5 collective-permute-start.6
  586.1 149.4 %copy-start.1 = (bf16[128,48,80]{2,1,0:T(8,128)(2,1)S(1)}, bf16[128,48,80]{2,1,0:T(8,128)(2,1)}, u32[]{:S(2)}) copy-start(bf16[128,48,80]{2,1,0:T(8,128)(2,1)} %convolution_convert_fusion) | copy-start | bytes 2949124
  723.6 9.9 %collective-permute-start.7 = (bf16[12,128]{1,0:T(8,128)(2,1)S(1)}, bf16[12,128]{1,0:T(8,128)(2,1)S(1)}, u32[]{:S(2)}, u32[]{:S(2)}) collective-permute-start(bf16[12,128]{1,0:T(8,128)(2,1)S(1)} %slice.173), channel_id=1, source_target_pairs={{0,8},{8,16},{16,24},{24,32},{32,40},{40,48},{48,56},{56,64},{64,7... | collective-permute-start | bytes 9224 | tf_op jit(solution)/shard_map/ppermute | solution.py:14
  (1 other events, 0.6 us)
Sparse Core Ops, SparseCore 0:
  32.7 31.7 reduce-scatter.4
  117.4 29.7 reduce-scatter.6
  354.5 30.7 reduce-scatter.8
  590.4 31.0 reduce-scatter.10
where the time goes:
time: 747 us; the launch traced here: 744 us
  blocking collectives  462 us (62%)
  waiting for transfers between devices  129 us (17%)
  starting transfers between devices  54.4 us (7%)
  local copies, waits for them, and re-layouts  38.7 us (5%)
  other arithmetic  30.1 us (4%)
  between operations  21.9 us (3%)
  matrix products  7.72 us (1%)
    psum x3, blocking collectives, squares(): return lax.psum(jnp.sum(mine * mine), ('dom', 'sub'))  227 us
    psum x2, blocking collectives, conjugate(): lax.psum(jnp.sum(own_part(direction) * own_part(image)), ('dom', 'sub'))  161 us
    reduce_scatter x4, waiting for transfers between devices, assemble(): lax.psum_scatter(partial_sums, 'sub', scatter_dimension=1, tiled=True)  124 us
    all_gather x3, blocking collectives, whole_partition(): return lax.all_gather(vector, 'sub', axis=1, tiled=True)  55.3 us
    ppermute x8, starting transfers between devices, shifted(): lax.ppermute(value, axis, [(source, source + steps) for source in range(f...  54.2 us
    all_gather x1, blocking collectives, on_device(): partition_half = lax.all_gather(solution_half, 'sub', axis=1, tiled=True)  18.5 us
    unnamed x59, local copies, waits for them, and re-layouts  16.4 us
  transfers between devices with their start and end apart: 12, of which 8 were waited for; matrix products, arithmetic and copies ran while one was open for 3% of the time, Pallas kernels for 0%

commit v1 on v0

v1 whole, which is shorter than its diff:
```python
import functools

import jax
import jax.numpy as jnp
from jax import lax
from jax.experimental import pallas as pl
from jax.experimental.pallas import tpu as pltpu
from jax.sharding import PartitionSpec as P

NI = 80
FD = 12
NF = 48
LANES = 128
RIM = 128
SUB = 8
FACES_PART = 2048
F32 = jnp.float32
BF16 = jnp.bfloat16
VMEM_LIMIT = 24 * 1024 * 1024

PUSHED, UP, DOWN, LOADS, SHIFTS, NAMES, FIRST_ROWS = 0, 48, 72, 84, 108, 132, 136
LATER_UP, LATER_DOWN, LATER_ROWS = 48, 60, 72


def row_iota(rows):
    return lax.broadcasted_iota(jnp.int32, (rows, LANES), 0)


def lane_iota(rows):
    return lax.broadcasted_iota(jnp.int32, (rows, LANES), 1)


def eight_sums(parts):
    rows = row_iota(8)
    low = rows < 4
    parts = [
        jnp.where(low, parts[i], parts[i + 4])
        + pltpu.roll(jnp.where(low, parts[i + 4], parts[i]), 4, 0)
        for i in range(4)
    ]
    for step in (2, 1):
        low = (rows & step) == 0
        parts = [
            jnp.where(
                low,
                parts[i] + pltpu.roll(parts[i], 8 - step, 0),
                parts[i + step] + pltpu.roll(parts[i + step], step, 0),
            )
            for i in range(step)
        ]
    return parts[0]


def matrix_times(matrix_ref, vector):
    rows, depth, _ = matrix_ref.shape
    blocks = []
    for first in range(0, rows, 8):
        parts = [
            (matrix_ref[first + i].astype(F32) * vector)
            .reshape(depth // 8, 8, LANES)
            .sum(0)
            for i in range(8)
        ]
        blocks.append(eight_sums(parts))
    return jnp.concatenate(blocks, 0)


def transposed_times(matrix_ref, vector):
    depth = matrix_ref.shape[0]
    totals = [None, None]
    for i in range(depth):
        term = matrix_ref[i].astype(F32) * vector[i : i + 1]
        totals[i % 2] = term if totals[i % 2] is None else totals[i % 2] + term
    return totals[0] + totals[1]


def living_mask(padding_ref):
    return lane_iota(1) < LANES - padding_ref[0]


def element_operator(inverse_ref, coupling_ref, trace_ref, view, living):
    inner = matrix_times(inverse_ref, matrix_times(coupling_ref, view))
    terms = transposed_times(coupling_ref, inner) + matrix_times(trace_ref, view)
    return jnp.where(living, terms, 0.0)


def split3(value):
    high = value.astype(BF16)
    rest = value - high.astype(F32)
    middle = rest.astype(BF16)
    low = (rest - middle.astype(F32)).astype(BF16)
    return high, middle, low


def exact_pick(values, chosen):
    stacked = jnp.concatenate(split3(values), 0)
    sums = lax.dot_general(
        stacked, chosen, (((1,), (1,)), ((), ())), preferred_element_type=F32
    )
    rows = values.shape[0]
    return sums[:rows] + sums[rows : 2 * rows] + sums[2 * rows :]


def face_major(terms_ref):
    slots = []
    for j in range(4):
        part = terms_ref[pl.ds(j, FD, stride=4), :]
        slots.append(jnp.concatenate([part, jnp.zeros((4, LANES), F32)], 0))
    return jnp.concatenate(slots, 1)


def rim_lists(terms_ref, names_ref):
    wanted = lax.broadcasted_iota(jnp.int32, (2 * RIM, LANES), 0)
    wanted = jnp.where(wanted < RIM, wanted, wanted + FACES_PART - RIM)
    chosen = [
        jnp.where(wanted == names_ref[j : j + 1, :], 1.0, 0.0).astype(BF16)
        for j in range(4)
    ]
    lists = exact_pick(face_major(terms_ref), jnp.concatenate(chosen, 1))
    return lists[:FD, :RIM], lists[:FD, RIM:]


def first_kernel(
    ids_ref, padding_ref, inverse_ref, coupling_ref, interior_load_ref, trace_load_ref, shift_ref, names_ref,
    solved_ref, pushed_ref, up_ref, down_ref,
):
    living = living_mask(padding_ref)
    solved = matrix_times(inverse_ref, interior_load_ref[...].astype(F32))
    solved_ref[...] = solved
    pushed_ref[...] = jnp.where(living, transposed_times(coupling_ref, solved), 0.0)
    low, high = rim_lists(pushed_ref, names_ref)
    owner = ids_ref[1] == SUB - 1
    up_ref[:FD, :] = high + jnp.where(owner, trace_load_ref[:, RIM:], 0.0)
    up_ref[FD:, :] = jnp.where(owner, shift_ref[:, RIM:], 0.0)
    down_ref[...] = low


def spread_rows(values, block):
    a = jnp.broadcast_to(values[2 * block : 2 * block + 1], (8, LANES))
    b = jnp.broadcast_to(values[2 * block + 1 : 2 * block + 2], (8, LANES))
    return jnp.where(row_iota(8) < 4, a, b)


def turn(values, steps):
    if steps == 0:
        return values
    rows = row_iota(8) & 3
    return jnp.where(
        rows < 4 - steps, pltpu.roll(values, 8 - steps, 0), pltpu.roll(values, 4 - steps, 0)
    )


def take_lanes(values, lanes):
    return jnp.take_along_axis(values, lanes, axis=1, mode="promise_in_bounds")


def partner_terms(gathered_ref, chunk, lane, low_list, high_list):
    rows = row_iota(8) & 3
    found = [jnp.zeros((8, LANES), F32) for _ in range(6)]
    for t in range(4):
        chunk_t = turn(chunk, (4 - t) % 4)
        lane_t = turn(lane, (4 - t) % 4)
        part = [jnp.zeros((8, LANES), F32) for _ in range(6)]
        for s in range(SUB):
            here = chunk_t == 4 * s + rows
            for g in range(6):
                taken = take_lanes(gathered_ref[s, 8 * g : 8 * g + 8, :], lane_t)
                part[g] = jnp.where(here, taken, part[g])
        for g in range(6):
            found[g] = found[g] + turn(part[g], t)
    on_low = chunk == 4 * SUB
    on_high = chunk == 4 * SUB + 1
    for g in range(6):
        found[g] = jnp.where(on_low, take_lanes(spread_rows(low_list, g), lane), found[g])
        found[g] = jnp.where(on_high, take_lanes(spread_rows(high_list, g), lane), found[g])
    return jnp.concatenate(found, 0)


def twice(slots):
    return jnp.concatenate([slots, slots], 0)


def six_times(rows8):
    return jnp.concatenate([rows8] * 6, 0)


def summed(gathered_ref, first, last):
    total = gathered_ref[0, first:last, :]
    for s in range(1, SUB):
        total = total + gathered_ref[s, first:last, :]
    return total


def partner_places(names_ref, gathered_ref, sub):
    weights, columns = [], []
    high_rows = row_iota(24)
    low_rows = row_iota(LANES)
    for s in range(SUB):
        for j in range(4):
            names = gathered_ref[s, NAMES + j : NAMES + j + 1, :].astype(jnp.int32)
            row_hit = (names >> 7) == high_rows
            weights.append(
                jnp.concatenate(
                    [
                        jnp.where(row_hit, F32(4 * s + j), 0.0),
                        jnp.where(row_hit, lane_iota(24).astype(F32), 0.0),
                    ],
                    0,
                ).astype(BF16)
            )
            columns.append(jnp.where((names & 127) == low_rows, 1.0, 0.0).astype(BF16))
    table = lax.dot_general(
        jnp.concatenate(weights, 1),
        jnp.concatenate(columns, 1),
        (((1,), (1,)), ((), ())),
        preferred_element_type=F32,
    )
    chunks, lanes = [], []
    for j in range(4):
        name = names_ref[j : j + 1, :]
        low = jnp.broadcast_to(name & 127, (24, LANES))
        hit = high_rows == (name >> 7)
        chunk_sum = jnp.where(hit, take_lanes(table[:24], low), 0.0).sum(0, keepdims=True)
        lane_sum = jnp.where(hit, take_lanes(table[24:], low), 0.0).sum(0, keepdims=True)
        chunk = chunk_sum.astype(jnp.int32) - (4 * sub + j)
        lane = lane_sum.astype(jnp.int32) - lane_iota(1)
        below, above = name < RIM, name >= FACES_PART
        chunk = jnp.where(below, 4 * SUB, jnp.where(above, 4 * SUB + 1, chunk))
        lane = jnp.where(below | above, name & 127, lane)
        chunks.append(chunk)
        lanes.append(lane)
    return jnp.concatenate(chunks, 0), jnp.concatenate(lanes, 0) & 127


def face_values(names_ref, gathered_ref, up_list, loads_ref, shifts_ref):
    for j in range(4):
        name = names_ref[j : j + 1, :]
        high = jnp.broadcast_to(name >> 7, (24, LANES))
        low = jnp.broadcast_to(name & 127, (24, LANES))
        got = jnp.where(high == 0, take_lanes(up_list, low), 0.0)
        for s in range(SUB):
            for half in range(2):
                source = jnp.concatenate(
                    [
                        gathered_ref[s, LOADS + 12 * half : LOADS + 12 * half + 12, :],
                        gathered_ref[s, SHIFTS + 12 * half : SHIFTS + 12 * half + 12, :],
                    ],
                    0,
                )
                got = jnp.where(high == 2 * s + half + 1, take_lanes(source, low), got)
        loads_ref[pl.ds(j, FD, stride=4), :] = got[:FD]
        shifts_ref[pl.ds(j, FD, stride=4), :] = got[FD:]


def second_kernel(
    ids_ref, padding_ref, inverse_ref, coupling_ref, trace_ref, names_ref, pushed_ref, gathered_ref,
    chunk_ref, lane_ref, valid_ref, weight_ref, shifts_ref, view_ref, terms_ref, up_ref, down_ref,
    loads_ref,
):
    dom, sub = ids_ref[0], ids_ref[1]
    chunk, lane = partner_places(names_ref, gathered_ref, sub)
    chunk, lane = twice(chunk), twice(lane)
    names = twice(names_ref[...])
    valid = jnp.where((names < RIM) & (dom == 0), 0.0, 1.0)
    weight = jnp.where((names >= FACES_PART) & (dom == ids_ref[2] - 1), 1.0, 0.5)
    chunk_ref[...] = chunk
    lane_ref[...] = lane
    valid_ref[...] = valid
    weight_ref[...] = weight
    up_list = summed(gathered_ref, UP, UP + 24)
    down_list = summed(gathered_ref, DOWN, DOWN + 12)
    face_values(names_ref, gathered_ref, up_list, loads_ref, shifts_ref)
    own_load = jnp.where(six_times(names) < RIM, 0.0, loads_ref[...])
    partner = partner_terms(gathered_ref, chunk, lane, up_list[:FD], down_list)
    view = jnp.where(six_times(valid) > 0.0, own_load + (pushed_ref[...] + partner), 0.0)
    view_ref[...] = view
    terms_ref[...] = element_operator(
        inverse_ref, coupling_ref, trace_ref, view, living_mask(padding_ref)
    )
    low, high = rim_lists(terms_ref, names_ref)
    up_ref[...] = high
    down_ref[...] = low


def next_view(gathered_ref, chunk_ref, lane_ref, valid_ref, shifts_ref, view_ref, terms_ref):
    low_list = summed(gathered_ref, LATER_UP, LATER_UP + FD)
    high_list = summed(gathered_ref, LATER_DOWN, LATER_DOWN + FD)
    partner = partner_terms(gathered_ref, chunk_ref[...], lane_ref[...], low_list, high_list)
    image = terms_ref[...] + partner + shifts_ref[...] * view_ref[...]
    return jnp.where(six_times(valid_ref[...]) > 0.0, image, 0.0)


def third_kernel(
    padding_ref, inverse_ref, coupling_ref, trace_ref, names_ref, gathered_ref,
    chunk_ref, lane_ref, valid_ref, shifts_ref, view_ref, terms_ref,
    new_view_ref, new_terms_ref, up_ref, down_ref,
):
    view = next_view(gathered_ref, chunk_ref, lane_ref, valid_ref, shifts_ref, view_ref, terms_ref)
    new_view_ref[...] = view
    new_terms_ref[...] = element_operator(
        inverse_ref, coupling_ref, trace_ref, view, living_mask(padding_ref)
    )
    low, high = rim_lists(new_terms_ref, names_ref)
    up_ref[...] = high
    down_ref[...] = low


def fourth_kernel(
    padding_ref, inverse_ref, coupling_ref, trace_ref, gathered_ref,
    chunk_ref, lane_ref, valid_ref, weight_ref, shifts_ref, first_view_ref, view_ref, terms_ref,
    new_view_ref, sums_ref,
):
    first, second = first_view_ref[...], view_ref[...]
    third = next_view(gathered_ref, chunk_ref, lane_ref, valid_ref, shifts_ref, view_ref, terms_ref)
    new_view_ref[...] = third
    last = element_operator(inverse_ref, coupling_ref, trace_ref, third, living_mask(padding_ref))
    weight = six_times(weight_ref[...])
    last = last + weight * (shifts_ref[...] * third)
    views = (first, second, third)
    products = [weight * views[i] * views[j] for i in range(3) for j in range(i, 3)]
    products += [view * last for view in views]
    lane = lane_iota(1)
    sums = jnp.zeros((1, LANES), F32)
    for place, product in enumerate(products):
        total = product.reshape(6, 8, LANES).sum(0).sum(0, keepdims=True).sum(1, keepdims=True)
        sums = sums + jnp.where(lane == place, total, 0.0)
    sums_ref[...] = sums


def owner_kernel(
    ids_ref, first_ref, second_ref, third_ref, trace_load_ref, shift_ref,
    owned_ref, terms_ref, chosen_ref,
):
    sub = ids_ref[1]
    wanted = lax.broadcasted_iota(jnp.int32, (2 * RIM, LANES), 0) + (RIM + 2 * RIM * sub)
    sources = (first_ref, second_ref, third_ref)
    for s in range(SUB):
        for j in range(4):
            columns = slice((4 * s + j) * LANES, (4 * s + j + 1) * LANES)
            names = first_ref[s, NAMES + j : NAMES + j + 1, :].astype(jnp.int32)
            chosen_ref[:, columns] = jnp.where(wanted == names, 1.0, 0.0).astype(BF16)
            for v, source in enumerate(sources):
                part = source[s, pl.ds(j, FD, stride=4), :]
                part = jnp.concatenate([part, jnp.zeros((4, LANES), F32)], 0)
                for piece, value in enumerate(split3(part)):
                    first = 16 * (3 * v + piece)
                    terms_ref[first : first + 16, columns] = value
    sums = lax.dot_general(
        terms_ref[...], chosen_ref[...], (((1,), (1,)), ((), ())), preferred_element_type=F32
    )
    last = sub == SUB - 1
    downs = (
        summed(first_ref, DOWN, DOWN + FD),
        summed(second_ref, LATER_DOWN, LATER_DOWN + FD),
        summed(third_ref, LATER_DOWN, LATER_DOWN + FD),
    )
    current = None
    for v in range(3):
        rows = [sums[48 * v + 16 * piece : 48 * v + 16 * piece + FD] for piece in range(3)]
        total = rows[0] + rows[1] + rows[2]
        down = jnp.concatenate(
            [jnp.zeros((FD, RIM), F32), jnp.where(last, downs[v], 0.0)], 1
        )
        total = total + down
        if v == 0:
            current = total + trace_load_ref[...]
        else:
            current = total + shift_ref[...] * current
        owned_ref[v] = current


def coefficients(sums):
    lane = lane_iota(1)

    def entry(place):
        return jnp.where(lane == place, sums, 0.0).sum(1, keepdims=True)

    table = {}
    place = 0
    for i in range(3):
        for j in range(i, 3):
            table[i, j] = table[j, i] = entry(place)
            place += 1
    for i in range(3):
        table[i, 3] = entry(place)
        place += 1

    def form(left, right):
        total = None
        for i, a in enumerate(left):
            for j, b in enumerate(right):
                if a is None or b is None:
                    continue
                term = a * b * table[i, j]
                total = term if total is None else total + term
        return total

    def combine(left, factor, right):
        merged = []
        for i in range(max(len(left), len(right))):
            a = left[i] if i < len(left) else None
            b = right[i] if i < len(right) else None
            if b is None:
                merged.append(a)
            else:
                merged.append(factor * b if a is None else a + factor * b)
        return merged

    one = jnp.ones((1, 1), F32)
    residual, direction, result = [one], [one], []
    norm = table[0, 0]
    for iteration in range(3):
        image = [None] + direction
        step = norm / form(direction, image)
        result = combine(result, step, direction)
        if iteration < 2:
            residual = combine(residual, -step, image)
            new_norm = form(residual, residual)
            direction = combine(residual, new_norm / norm, direction)
            norm = new_norm
    return result


def last_kernel(
    padding_ref, inverse_ref, coupling_ref, all_sums_ref, first_view_ref, second_view_ref, third_view_ref,
    solved_ref, owned_ref,
    traces_ref, interior_ref,
):
    sums = all_sums_ref[...].reshape(-1, 8, LANES).sum(0).sum(0, keepdims=True)
    a, b, c = coefficients(sums)
    traces_ref[...] = a * owned_ref[0] + b * owned_ref[1] + c * owned_ref[2]
    view = a * first_view_ref[...] + b * second_view_ref[...] + c * third_view_ref[...]
    lifted = matrix_times(inverse_ref, matrix_times(coupling_ref, view))
    interior_ref[...] = jnp.where(living_mask(padding_ref), solved_ref[...] - lifted, 0.0)


def call(kernel, outputs, inputs, scalars=0, scratch=()):
    shape = [jax.ShapeDtypeStruct(s, d) for s, d in outputs]
    return pl.pallas_call(
        kernel,
        out_shape=shape,
        in_specs=[
            pl.BlockSpec(memory_space=pltpu.SMEM if i < scalars else pltpu.VMEM)
            for i in range(len(inputs))
        ],
        out_specs=[pl.BlockSpec(memory_space=pltpu.VMEM)] * len(shape),
        scratch_shapes=list(scratch),
        compiler_params=pltpu.CompilerParams(vmem_limit_bytes=VMEM_LIMIT),
    )(*inputs)


def to_all(value):
    copies = jnp.broadcast_to(value[None], (SUB,) + value.shape)
    return lax.all_to_all(copies, "sub", 0, 0, tiled=True)


def neighbours(up, down):
    count = lax.axis_size("dom")
    from_below = lax.ppermute(up, "dom", [(i, i + 1) for i in range(count - 1)])
    from_above = lax.ppermute(down, "dom", [(i + 1, i) for i in range(count - 1)])
    return from_below, from_above


def on_device(
    interior_inverse, coupling, trace_block, interior_load, trace_load, face_shift, element_faces, block_padding,
):
    ids = jnp.stack(
        [lax.axis_index("dom"), lax.axis_index("sub"), jnp.int32(lax.axis_size("dom"))]
    ).astype(jnp.int32)
    slab, lists = ((NF, LANES), F32), ((FD, LANES), F32)
    solved, pushed, up, down = call(
        first_kernel,
        [((NI, LANES), F32), slab, ((2 * FD, LANES), F32), lists],
        [ids, block_padding, interior_inverse, coupling, interior_load, trace_load, face_shift, element_faces],
        scalars=2,
    )
    from_below, from_above = neighbours(up, down)
    first = to_all(
        jnp.concatenate(
            [
                pushed, from_below, from_above,
                trace_load[:, :RIM], trace_load[:, RIM:], face_shift[:, :RIM], face_shift[:, RIM:],
                element_faces.astype(F32),
            ],
            0,
        )
    )
    eight_i, eight_f = ((8, LANES), jnp.int32), ((8, LANES), F32)
    chunk, lane, valid, weight, shifts, view0, terms, up, down = call(
        second_kernel,
        [eight_i, eight_i, eight_f, eight_f, slab, slab, slab, lists, lists],
        [ids, block_padding, interior_inverse, coupling, trace_block, element_faces, pushed, first],
        scalars=2,
        scratch=[pltpu.VMEM((NF, LANES), F32)],
    )
    second = to_all(jnp.concatenate([terms, *neighbours(up, down)], 0))
    view1, terms1, up, down = call(
        third_kernel,
        [slab, slab, lists, lists],
        [block_padding, interior_inverse, coupling, trace_block, element_faces, second, chunk, lane, valid, shifts, view0, terms],
        scalars=1,
    )
    third = to_all(jnp.concatenate([terms1, *neighbours(up, down)], 0))
    view2, sums = call(
        fourth_kernel,
        [slab, ((1, LANES), F32)],
        [block_padding, interior_inverse, coupling, trace_block, third, chunk, lane, valid, weight, shifts, view0, view1, terms1],
        scalars=1,
    )
    everyone = lax.axis_size("dom") * SUB
    all_sums = lax.all_to_all(
        jnp.broadcast_to(sums, (everyone, LANES)), ("dom", "sub"), 0, 0, tiled=True
    )
    (owned,) = call(
        owner_kernel,
        [((3, FD, 2 * RIM), F32)],
        [ids, first, second, third, trace_load, face_shift],
        scalars=1,
        scratch=[pltpu.VMEM((144, 32 * LANES), BF16), pltpu.VMEM((2 * RIM, 32 * LANES), BF16)],
    )
    traces, interior = call(
        last_kernel,
        [((FD, 2 * RIM), F32), ((NI, LANES), F32)],
        [block_padding, interior_inverse, coupling, all_sums, view0, view1, view2, solved, owned],
        scalars=1,
    )
    return traces, interior


def solution(mesh):
    last = ("dom", "sub")
    placed = (
        P(None, None, last), P(None, None, last), P(None, None, last),
        P(None, last), P(None, last), P(None, last), P(None, last), P(last),
    )
    return jax.shard_map(
        on_device,
        mesh=mesh,
        in_specs=placed,
        out_specs=(P(None, last), P(None, last)),
        check_vma=False,
    )
```

time: 747 us -> 119 us (0.16)
  blocking collectives: 462 us -> 53.3 us
  waiting for transfers between devices: 129 us -> 15.6 us
  other arithmetic: 30.1 us -> 0.09 us
  local copies, waits for them, and re-layouts: 38.7 us -> 9.86 us
  starting transfers between devices: 54.4 us -> 27.9 us
  between operations: 21.9 us -> 1.49 us
  Pallas kernels: 0 us -> 9.98 us
  matrix products: 7.72 us -> 0 us
    psum x5 -> x0, blocking collectives: 388 us -> none  [the longest x3 227 us: squares(): return lax.psum(jnp.sum(mine * mine), ('dom', 'sub'))]
    reduce_scatter x4 -> x0, waiting for transfers between devices: 124 us -> none  [assemble(): lax.psum_scatter(partial_sums, 'sub', scatter_dimension=1, tiled=True)]
    all_gather x4 -> x0, blocking collectives: 73.8 us -> none  [the longest x3 55.3 us: whole_partition(): return lax.all_gather(vector, 'sub', axis=1, tiled=True)]
    all_to_all x0 -> x3, blocking collectives: none -> 53.3 us  [to_all(): return lax.all_to_all(copies, 'sub', 0, 0, tiled=True)]
    ppermute x8 -> x6, starting transfers between devices: 54.2 us -> 18.6 us  [the longest x3 9.45 us: neighbours(): from_below = lax.ppermute(up, 'dom', [(i, i + 1) for i in range(count - 1)])]
    scatter-add x8 -> x0, other arithmetic: 11.7 us -> none  [the longest x4 11.7 us: collect(): summed = jnp.zeros((face_rows, face_count + RIM), jnp.float32).at[:, elem...]
    pallas_call x0 -> x6, Pallas kernels: none -> 9.98 us  [call(): pl.pallas_call(kernel, out_shape=shape, in_specs=[pl.BlockSpec(memory_spa...]
    all_to_all x0 -> x1, starting transfers between devices: none -> 9.35 us  [on_device(): lax.all_to_all(jnp.broadcast_to(sums, (everyone, LANES)), ('dom', 'sub'),...]
  transfers between devices with their start and end apart: 12 -> 7, of which waited for: 8 -> 4; matrix products, arithmetic and copies ran while one was open for 3% -> 0% of each run, Pallas kernels for 0% -> 2%
where the time goes in v1:
time: 119 us; the launch traced here: 118 us
  blocking collectives  53.3 us (45%)
  starting transfers between devices  27.9 us (23%)
  waiting for transfers between devices  15.6 us (13%)
  Pallas kernels  9.98 us (8%)
  local copies, waits for them, and re-layouts  9.86 us (8%)
  between operations  1.49 us (1%)
    all_to_all x3, blocking collectives, to_all(): return lax.all_to_all(copies, 'sub', 0, 0, tiled=True)  53.3 us
    pallas_call x6, Pallas kernels, call(): pl.pallas_call(kernel, out_shape=shape, in_specs=[pl.BlockSpec(memory_spa...  9.98 us
    ppermute x3, starting transfers between devices, neighbours(): from_below = lax.ppermute(up, 'dom', [(i, i + 1) for i in range(count - 1)])  9.45 us
    all_to_all x1, starting transfers between devices, on_device(): lax.all_to_all(jnp.broadcast_to(sums, (everyone, LANES)), ('dom', 'sub'),...  9.35 us
    ppermute x3, starting transfers between devices, neighbours(): lax.ppermute(down, 'dom', [(i + 1, i) for i in range(count - 1)])  9.12 us
    unnamed x44, local copies, waits for them, and re-layouts  8.85 us
    all_to_all x1, waiting for transfers between devices, on_device(): lax.all_to_all(jnp.broadcast_to(sums, (everyone, LANES)), ('dom', 'sub'),...  8.43 us
    ppermute x3, waiting for transfers between devices, neighbours(): lax.ppermute(down, 'dom', [(i + 1, i) for i in range(count - 1)])  6.06 us
  transfers between devices with their start and end apart: 7, of which 4 were waited for; matrix products, arithmetic and copies ran while one was open for 0% of the time, Pallas kernels for 2%

profile of v1, /device:TPU:1, one launch (start us, length us, event | category | flops | bytes accessed | tf_op | source)
XLA Modules:
  0.0 118.3 jit_solution(12882185821553369114)
XLA Ops:
  1.4 1.4 %copy-done = bf16[80,80,128]{2,1,0:T(8,128)(2,1)S(1)} copy-done((bf16[80,80,128]{2,1,0:T(8,128)(2,1)S(1)}, bf16[80,80,128]{2,1,0:T(8,128)(2,1)}, u32[]{:S(2)}) %copy-start) | copy-done | bytes 1638424
  2.8 1.2 %copy-done.2 = bf16[80,48,128]{2,1,0:T(8,128)(2,1)S(1)} copy-done((bf16[80,48,128]{2,1,0:T(8,128)(2,1)S(1)}, bf16[80,48,128]{2,1,0:T(8,128)(2,1)}, u32[]{:S(2)}) %copy-start.2) | copy-done | bytes 983064
  4.0 0.7 copy-done.9
  4.7 0.7 copy-done.11
  5.4 0.7 copy-done.17
  6.1 0.7 copy-done.21
  6.8 1.3 %shard_map.95 = (f32[80,128]{1,0:T(8,128)S(1)}, f32[48,128]{1,0:T(8,128)S(1)}, f32[24,128]{1,0:T(8,128)S(1)}, f32[12,128]{1,0:T(8,128)S(1)}) custom-call(s32[3]{0:T(128)S(1)} %pad_add_fusion.ids_ref, s32[1]{0:T(128)S(6)} %copy.10.padding_ref, bf16[80,80,128]{2,1,0:T(8,128)(2,1)S(1)} %copy-done, bf16[80,48,128]{2,1,0:T(8,128)(2,1)S(1)} %copy-done.2, ...), custom_call_target="tpu_custom_call" | custom-call | tf_op jit(solution)/shard_map/pallas_call | solution.py:439
  8.1 5.3 %collective-permute-start.1 = (f32[12,128]{1,0:T(8,128)S(1)}, f32[12,128]{1,0:T(8,128)S(1)}, u32[]{:S(2)}, u32[]{:S(2)}) collective-permute-start(f32[12,128]{1,0:T(8,128)S(1)} %get-tuple-element.23), channel_id=1, source_target_pairs={{8,0},{16,8},{24,16},{32,24},{40,32},{48,40},{56,48},{64,56},{72,6... | collective-permute-start | bytes 18440 | tf_op jit(solution)/shard_map/ppermute | solution.py:460
  13.4 1.9 %collective-permute-start = (f32[24,128]{1,0:T(8,128)S(1)}, f32[24,128]{1,0:T(8,128)S(1)}, u32[]{:S(2)}, u32[]{:S(2)}) collective-permute-start(f32[24,128]{1,0:T(8,128)S(1)} %get-tuple-element.22), channel_id=1, source_target_pairs={{0,8},{8,16},{16,24},{24,32},{32,40},{40,48},{48,56},{56,64},{64,7... | collective-permute-start | bytes 36872 | tf_op jit(solution)/shard_map/ppermute | solution.py:459
  15.4 1.1 collective-permute-done
  16.5 0.2 concatenate.9
  16.7 25.8 %all_to_all.23.gathered_ref.first_ref = f32[8,136,128]{2,1,0:T(8,128)S(1)} all-to-all(f32[8,136,128]{2,1,0:T(8,128)S(1)} %broadcast_in_dim.8), channel_id=1, replica_groups=mesh['dom'=32,'sub'=8] {'sub'}, dimensions={0} | all-to-all | bytes 1114112 | tf_op jit(solution)/shard_map/all_to_all | solution.py:454
  42.5 2.7 %shard_map.96 = (s32[8,128]{1,0:T(8,128)S(1)}, s32[8,128]{1,0:T(8,128)S(1)}, f32[8,128]{1,0:T(8,128)S(1)}, f32[8,128]{1,0:T(8,128)S(1)}, f32[48,128]{1,0:T(8,128...) custom-call(s32[3]{0:T(128)S(1)} %pad_add_fusion.ids_ref, ...), custom_call_target="tpu_custom_call" | custom-call | tf_op jit(solution)/shard_map/pallas_call | solution.py:439
  45.2 3.4 %collective-permute-start.2 = (f32[12,128]{1,0:T(8,128)S(1)}, f32[12,128]{1,0:T(8,128)S(1)}, u32[]{:S(2)}, u32[]{:S(2)}) collective-permute-start(f32[12,128]{1,0:T(8,128)S(1)} %get-tuple-element.25), channel_id=1, source_target_pairs={{0,8},{8,16},{16,24},{24,32},{32,40},{40,48},{48,56},{56,64},{64,7... | collective-permute-start | bytes 18440 | tf_op jit(solution)/shard_map/ppermute | solution.py:459
  48.7 1.9 %collective-permute-start.3 = (f32[12,128]{1,0:T(8,128)S(1)}, f32[12,128]{1,0:T(8,128)S(1)}, u32[]{:S(2)}, u32[]{:S(2)}) collective-permute-start(f32[12,128]{1,0:T(8,128)S(1)} %get-tuple-element.26), channel_id=1, source_target_pairs={{8,0},{16,8},{24,16},{32,24},{40,32},{48,40},{56,48},{64,56},{72,6... | collective-permute-start | bytes 18440 | tf_op jit(solution)/shard_map/ppermute | solution.py:460
  50.6 3.0 %collective-permute-done.3 = f32[12,128]{1,0:T(8,128)S(1)} collective-permute-done((f32[12,128]{1,0:T(8,128)S(1)}, f32[12,128]{1,0:T(8,128)S(1)}, u32[]{:S(2)}, u32[]{:S(2)}) %collective-permute-start.3) | collective-permute-done | bytes 6176 | tf_op jit(solution)/shard_map/ppermute | solution.py:460
  53.7 13.8 %all_to_all.24.gathered_ref.second_ref = f32[8,72,128]{2,1,0:T(8,128)S(1)} all-to-all(f32[8,72,128]{2,1,0:T(8,128)S(1)} %broadcast_in_dim.9), channel_id=1, replica_groups=mesh['dom'=32,'sub'=8] {'sub'}, dimensions={0} | all-to-all | bytes 589824 | tf_op jit(solution)/shard_map/all_to_all | solution.py:454
  67.4 1.4 %shard_map.97 = (f32[48,128]{1,0:T(8,128)S(1)}, f32[48,128]{1,0:T(8,128)S(1)}, f32[12,128]{1,0:T(8,128)S(1)}, f32[12,128]{1,0:T(8,128)S(1)}) custom-call(s32[1]{0:T(128)S(6)} %copy.10.padding_ref, bf16[80,80,128]{2,1,0:T(8,128)(2,1)S(1)} %copy-done.1, bf16[80,48,128]{2,1,0:T(8,128)(2,1)S(1)} %copy-done.3, bf16[48,48,128]{2,1,0:T(8,128)(2,1)S(1)} %copy-done.4, ...), custom_call_target="tpu_custom_call" | custom-call | tf_op jit(solution)/shard_map/pallas_call | solution.py:439
  68.9 4.1 %collective-permute-start.4 = (f32[12,128]{1,0:T(8,128)S(1)}, f32[12,128]{1,0:T(8,128)S(1)}, u32[]{:S(2)}, u32[]{:S(2)}) collective-permute-start(f32[12,128]{1,0:T(8,128)S(1)} %get-tuple-element.33), channel_id=1, source_target_pairs={{0,8},{8,16},{16,24},{24,32},{32,40},{40,48},{48,56},{56,64},{64,7... | collective-permute-start | bytes 18440 | tf_op jit(solution)/shard_map/ppermute | solution.py:459
  73.0 1.9 %collective-permute-start.5 = (f32[12,128]{1,0:T(8,128)S(1)}, f32[12,128]{1,0:T(8,128)S(1)}, u32[]{:S(2)}, u32[]{:S(2)}) collective-permute-start(f32[12,128]{1,0:T(8,128)S(1)} %get-tuple-element.34), channel_id=1, source_target_pairs={{8,0},{16,8},{24,16},{32,24},{40,32},{48,40},{56,48},{64,56},{72,6... | collective-permute-start | bytes 18440 | tf_op jit(solution)/shard_map/ppermute | solution.py:460
  74.9 3.0 %collective-permute-done.5 = f32[12,128]{1,0:T(8,128)S(1)} collective-permute-done((f32[12,128]{1,0:T(8,128)S(1)}, f32[12,128]{1,0:T(8,128)S(1)}, u32[]{:S(2)}, u32[]{:S(2)}) %collective-permute-start.5) | collective-permute-done | bytes 6176 | tf_op jit(solution)/shard_map/ppermute | solution.py:460
  78.0 13.8 %all_to_all.25.gathered_ref.third_ref = f32[8,72,128]{2,1,0:T(8,128)S(1)} all-to-all(f32[8,72,128]{2,1,0:T(8,128)S(1)} %broadcast_in_dim.10), channel_id=1, replica_groups=mesh['dom'=32,'sub'=8] {'sub'}, dimensions={0} | all-to-all | bytes 589824 | tf_op jit(solution)/shard_map/all_to_all | solution.py:454
  91.8 1.4 %shard_map.98 = (f32[48,128]{1,0:T(8,128)S(1)}, f32[1,128]{1,0:T(1,128)S(1)}) custom-call(s32[1]{0:T(128)S(6)} %copy.10.padding_ref, bf16[80,80,128]{2,1,0:T(8,128)(2,1)S(1)} %copy-done.1, bf16[80,48,128]{2,1,0:T(8,128)(2,1)S(1)} %copy-done.3, bf16[48,48,128]{2,1,0:T(8,128)(2,1)S(1)} %copy-done.4, f32[8,72,128]{2,1,0:T(8,128)S(1)} %all_to_all.25.gathered_ref.third_ref, ...), custom_call_target="tpu_custom_call" | custom-call | tf_op jit(solution)/shard_map/pallas_call | solution.py:439
  93.2 0.6 copy-done.19
  93.8 0.7 broadcast_in_dim.11
  94.5 9.3 %all-to-all-start.3 = ((f32[256,1,128]{2,1,0:T(1,128)}), f32[256,1,128]{2,1,0:T(1,128)S(1)}, u32[]{:S(2)}, u32[]{:S(2)}) async-start(f32[256,1,128]{2,1,0:T(1,128)} %broadcast_in_dim.11), calls=%async_computation.3 | async-start | bytes 262144 | tf_op jit(solution)/shard_map/all_to_all | solution.py:511
  103.9 1.0 copy-done.6
  104.9 1.0 copy-done.8
  105.9 0.7 copy-done.12
  106.6 1.8 %shard_map.99.owned_ref = f32[3,12,256]{2,1,0:T(8,128)S(1)} custom-call(s32[3]{0:T(128)S(1)} %pad_add_fusion.ids_ref, f32[8,136,128]{2,1,0:T(8,128)S(1)} %copy-done.6, f32[8,72,128]{2,1,0:T(8,128)S(1)} %all_to_all.24.gathered_ref.second_ref, f32[8,72,128]{2,1,0:T(8,128)S(1)} %copy-done.8, f32[12,256]{1,0:T(8,128)S(1)} %copy-done.10, f32[12,256]{1,0:T(8,128)S(1)} %copy-done.12), custom_call_target="tpu_custom_call" | custom-call | tf_op jit(solution)/shard_map/pallas_call | solution.py:439
  108.4 8.4 %all-to-all-done.3 = f32[256,1,128]{2,1,0:T(1,128)S(1)} async-done(((f32[256,1,128]{2,1,0:T(1,128)}), f32[256,1,128]{2,1,0:T(1,128)S(1)}, u32[]{:S(2)}, u32[]{:S(2)}) %all-to-all-start.3) | async-done | bytes 131104 | tf_op jit(solution)/shard_map/all_to_all | solution.py:511
  116.9 1.4 %shard_map.100 = (f32[12,256]{1,0:T(8,128)}, f32[80,128]{1,0:T(8,128)}) custom-call(s32[1]{0:T(128)S(6)} %copy.10.padding_ref, bf16[80,80,128]{2,1,0:T(8,128)(2,1)S(1)} %copy-done.1, bf16[80,48,128]{2,1,0:T(8,128)(2,1)S(1)} %copy-done.3, f32[256,128]{1,0:T(8,128)S(1)} %bitcast.4, f32[48,128]{1,0:T(8,128)S(1)} %get-tuple-element.31.view_ref.first_view_ref, ...), custom_call_target="tpu_custom_call" | custom-call | tf_op jit(solution)/shard_map/pallas_call | solution.py:439
  (45 shorter events, 0.3 us)
Async XLA Ops:
  1.4 1.4 %copy-start = (bf16[80,80,128]{2,1,0:T(8,128)(2,1)S(1)}, bf16[80,80,128]{2,1,0:T(8,128)(2,1)}, u32[]{:S(2)}) copy-start(bf16[80,80,128]{2,1,0:T(8,128)(2,1)} %inverse_ref.9) | copy-start | bytes 4915204
  2.8 1.2 %copy-start.2 = (bf16[80,48,128]{2,1,0:T(8,128)(2,1)S(1)}, bf16[80,48,128]{2,1,0:T(8,128)(2,1)}, u32[]{:S(2)}) copy-start(bf16[80,48,128]{2,1,0:T(8,128)(2,1)} %coupling_ref.9) | copy-start | bytes 2949124
  4.0 0.7 copy-start.9
  4.7 0.7 copy-start.11
  5.4 0.7 copy-start.17
  6.1 0.7 copy-start.21
  6.8 35.6 %copy-start.3 = (bf16[80,48,128]{2,1,0:T(8,128)(2,1)S(1)}, bf16[80,48,128]{2,1,0:T(8,128)(2,1)}, u32[]{:S(2)}) copy-start(bf16[80,48,128]{2,1,0:T(8,128)(2,1)} %coupling_ref.9) | copy-start | bytes 2949124
  6.8 35.6 %copy-start.4 = (bf16[48,48,128]{2,1,0:T(8,128)(2,1)S(1)}, bf16[48,48,128]{2,1,0:T(8,128)(2,1)}, u32[]{:S(2)}) copy-start(bf16[48,48,128]{2,1,0:T(8,128)(2,1)} %trace_ref.5) | copy-start | bytes 1769476
  8.1 7.3 %copy-start.15 = (f32[80,128]{1,0:T(8,128)}, f32[80,128]{1,0:T(8,128)S(1)}, u32[]{:S(2)}) copy-start(f32[80,128]{1,0:T(8,128)S(1)} %get-tuple-element.39.solved_ref) | copy-start | bytes 122884
  8.1 34.4 %copy-start.1 = (bf16[80,80,128]{2,1,0:T(8,128)(2,1)S(1)}, bf16[80,80,128]{2,1,0:T(8,128)(2,1)}, u32[]{:S(2)}) copy-start(bf16[80,80,128]{2,1,0:T(8,128)(2,1)} %inverse_ref.9) | copy-start | bytes 4915204
  8.1 34.4 %copy-start.18 = (s32[4,128]{1,0:T(4,128)S(1)}, s32[4,128]{1,0:T(4,128)}, u32[]{:S(2)}) copy-start(s32[4,128]{1,0:T(4,128)} %names_ref.5) | copy-start | bytes 6148
  8.1 7.3 %collective-permute-start.1 = (f32[12,128]{1,0:T(8,128)S(1)}, f32[12,128]{1,0:T(8,128)S(1)}, u32[]{:S(2)}, u32[]{:S(2)}) collective-permute-start(f32[12,128]{1,0:T(8,128)S(1)} %get-tuple-element.23), channel_id=1, source_target_pairs={{8,0},{16,8},{24,16},{32,24},{40,32},{48,40},{56,48},{64,56},{72,6... | collective-permute-start | bytes 18440 | tf_op jit(solution)/shard_map/ppermute | solution.py:460
  13.4 3.1 %collective-permute-start = (f32[24,128]{1,0:T(8,128)S(1)}, f32[24,128]{1,0:T(8,128)S(1)}, u32[]{:S(2)}, u32[]{:S(2)}) collective-permute-start(f32[24,128]{1,0:T(8,128)S(1)} %get-tuple-element.22), channel_id=1, source_target_pairs={{0,8},{8,16},{16,24},{24,32},{32,40},{40,48},{48,56},{56,64},{64,7... | collective-permute-start | bytes 36872 | tf_op jit(solution)/shard_map/ppermute | solution.py:459
  42.5 2.7 %copy-start.5 = (f32[8,136,128]{2,1,0:T(8,128)}, f32[8,136,128]{2,1,0:T(8,128)S(1)}, u32[]{:S(2)}) copy-start(f32[8,136,128]{2,1,0:T(8,128)S(1)} %all_to_all.23.gathered_ref.first_ref) | copy-start | bytes 1671172
  45.2 5.4 %collective-permute-start.2 = (f32[12,128]{1,0:T(8,128)S(1)}, f32[12,128]{1,0:T(8,128)S(1)}, u32[]{:S(2)}, u32[]{:S(2)}) collective-permute-start(f32[12,128]{1,0:T(8,128)S(1)} %get-tuple-element.25), channel_id=1, source_target_pairs={{0,8},{8,16},{16,24},{24,32},{32,40},{40,48},{48,56},{56,64},{64,7... | collective-permute-start | bytes 18440 | tf_op jit(solution)/shard_map/ppermute | solution.py:459
  48.7 5.0 %collective-permute-start.3 = (f32[12,128]{1,0:T(8,128)S(1)}, f32[12,128]{1,0:T(8,128)S(1)}, u32[]{:S(2)}, u32[]{:S(2)}) collective-permute-start(f32[12,128]{1,0:T(8,128)S(1)} %get-tuple-element.26), channel_id=1, source_target_pairs={{8,0},{16,8},{24,16},{32,24},{40,32},{48,40},{56,48},{64,56},{72,6... | collective-permute-start | bytes 18440 | tf_op jit(solution)/shard_map/ppermute | solution.py:460
  68.9 24.3 %copy-start.13 = (f32[48,128]{1,0:T(8,128)}, f32[48,128]{1,0:T(8,128)S(1)}, u32[]{:S(2)}) copy-start(f32[48,128]{1,0:T(8,128)S(1)} %get-tuple-element.36.view_ref.second_view_ref) | copy-start | bytes 73732
  68.9 6.0 %collective-permute-start.4 = (f32[12,128]{1,0:T(8,128)S(1)}, f32[12,128]{1,0:T(8,128)S(1)}, u32[]{:S(2)}, u32[]{:S(2)}) collective-permute-start(f32[12,128]{1,0:T(8,128)S(1)} %get-tuple-element.33), channel_id=1, source_target_pairs={{0,8},{8,16},{16,24},{24,32},{32,40},{40,48},{48,56},{56,64},{64,7... | collective-permute-start | bytes 18440 | tf_op jit(solution)/shard_map/ppermute | solution.py:459
  73.0 5.0 %collective-permute-start.5 = (f32[12,128]{1,0:T(8,128)S(1)}, f32[12,128]{1,0:T(8,128)S(1)}, u32[]{:S(2)}, u32[]{:S(2)}) collective-permute-start(f32[12,128]{1,0:T(8,128)S(1)} %get-tuple-element.34), channel_id=1, source_target_pairs={{8,0},{16,8},{24,16},{32,24},{40,32},{48,40},{56,48},{64,56},{72,6... | collective-permute-start | bytes 18440 | tf_op jit(solution)/shard_map/ppermute | solution.py:460
  91.8 1.4 %copy-start.7 = (f32[8,72,128]{2,1,0:T(8,128)}, f32[8,72,128]{2,1,0:T(8,128)S(1)}, u32[]{:S(2)}) copy-start(f32[8,72,128]{2,1,0:T(8,128)S(1)} %all_to_all.25.gathered_ref.third_ref) | copy-start | bytes 884740
  91.8 12.1 %copy-start.10 = (f32[12,256]{1,0:T(8,128)S(1)}, f32[12,256]{1,0:T(8,128)}, u32[]{:S(2)}) copy-start(f32[12,256]{1,0:T(8,128)} %trace_load_ref.3) | copy-start | bytes 36868
  93.2 0.6 copy-start.19
  93.8 23.1 %copy-start.16 = (f32[80,128]{1,0:T(8,128)S(1)}, f32[80,128]{1,0:T(8,128)}, u32[]{:S(2)}) copy-start(f32[80,128]{1,0:T(8,128)} %copy-done.15) | copy-start | bytes 122884
  93.8 23.1 %copy-start.14 = (f32[48,128]{1,0:T(8,128)S(1)}, f32[48,128]{1,0:T(8,128)}, u32[]{:S(2)}) copy-start(f32[48,128]{1,0:T(8,128)} %copy-done.13) | copy-start | bytes 73732
  93.8 23.1 %copy-start.20 = (f32[48,128]{1,0:T(8,128)S(1)}, f32[48,128]{1,0:T(8,128)}, u32[]{:S(2)}) copy-start(f32[48,128]{1,0:T(8,128)} %copy-done.19) | copy-start | bytes 73732
  94.5 22.3 %all-to-all-start.3 = ((f32[256,1,128]{2,1,0:T(1,128)}), f32[256,1,128]{2,1,0:T(1,128)S(1)}, u32[]{:S(2)}, u32[]{:S(2)}) async-start(f32[256,1,128]{2,1,0:T(1,128)} %broadcast_in_dim.11), calls=%async_computation.3 | async-start | bytes 262144 | tf_op jit(solution)/shard_map/all_to_all | solution.py:511
  103.9 1.1 copy-start.6
  104.9 1.0 copy-start.8
  105.9 0.7 copy-start.12

commit v2 on v1

--- a/solution.py
+++ b/solution.py
@@ -16,10 +16,15 @@
 FACES_PART = 2048
 F32 = jnp.float32
 BF16 = jnp.bfloat16
-VMEM_LIMIT = 24 * 1024 * 1024
-
-PUSHED, UP, DOWN, LOADS, SHIFTS, NAMES, FIRST_ROWS = 0, 48, 72, 84, 108, 132, 136
-LATER_UP, LATER_DOWN, LATER_ROWS = 48, 60, 72
+MIB = 1024 * 1024
+PARTS = 5
+
+I16 = jnp.int16
+
+PUSHED, LOADS, SHIFTS, NAMES, SCALES, UP, UP_SHIFT, DOWN, FIRST_END, FIRST_ROWS = (
+    0, 48, 72, 96, 100, 103, 116, 129, 142, 144,
+)
+LATER_UP, LATER_DOWN, LATER_END, LATER_ROWS = 49, 62, 75, 80
 
 
 def row_iota(rows):
@@ -74,14 +79,79 @@
     return totals[0] + totals[1]
 
 
-def living_mask(padding_ref):
-    return lane_iota(1) < LANES - padding_ref[0]
-
-
-def element_operator(inverse_ref, coupling_ref, trace_ref, view, living):
+def coded(value):
+    top = jnp.abs(value).max(0, keepdims=True).max(1, keepdims=True)
+    exponent = jnp.floor(jnp.log2(jnp.maximum(top, 2.0**-100))) + 1.0
+    whole = jnp.floor(value * jnp.exp2(15.0 - exponent) + 0.5)
+    return jnp.clip(whole, -32767.0, 32767.0), exponent
+
+
+def spread_row(exponent):
+    return jnp.broadcast_to(exponent, (1, LANES))
+
+
+def as_sent(value):
+    return value.astype(jnp.int32).astype(I16)
+
+
+def with_exponent(value):
+    whole, exponent = coded(value)
+    return [whole, spread_row(exponent)]
+
+
+def put_lists(on_ref, off_ref, up, down, dom):
+    even = dom % 2 == 0
+    rest = [jnp.zeros((on_ref.shape[0] - sum(len(x) for x in up), LANES), F32)]
+    up, down = jnp.concatenate(up + rest, 0), jnp.concatenate(down + rest, 0)
+    on_ref[...] = as_sent(jnp.where(even, up, down))
+    off_ref[...] = as_sent(jnp.where(even, down, up))
+
+
+def decode(sent_ref, terms_ref, sections):
+    rows = sent_ref.shape[1]
+    row = row_iota(rows)
+    for s in range(SUB):
+        values = sent_ref[s].astype(jnp.int32).astype(F32)
+        terms_ref[s] = values
+        factors = jnp.ones((1, LANES), F32)
+        for end, exponent in reversed(sections):
+            if exponent is None:
+                factor = jnp.ones((1, LANES), F32)
+            else:
+                factor = jnp.exp2(terms_ref[s, exponent : exponent + 1, :] - 15.0)
+            factors = jnp.where(row < end, factor, factors)
+        terms_ref[s] = values * factors
+
+
+def decode_first(sent_ref, terms_ref):
+    decode(
+        sent_ref,
+        terms_ref,
+        [
+            (LOADS, SCALES), (SHIFTS, SCALES + 1), (NAMES, SCALES + 2), (UP, None),
+            (UP + FD, UP + FD), (UP_SHIFT, None), (UP_SHIFT + FD, UP_SHIFT + FD), (DOWN, None),
+            (FIRST_END, DOWN + FD),
+        ],
+    )
+
+
+def decode_later(sent_ref, terms_ref):
+    decode(
+        sent_ref,
+        terms_ref,
+        [(NF, NF), (LATER_UP, None), (LATER_UP + FD, LATER_UP + FD), (LATER_DOWN, None), (LATER_END, LATER_DOWN + FD)],
+    )
+
+
+def ids():
+    return lax.axis_index("dom"), lax.axis_index("sub")
+
+
+def element_operator(inverse_ref, coupling_ref, trace_ref, view, living_ref, keep):
     inner = matrix_times(inverse_ref, matrix_times(coupling_ref, view))
+    keep(inner)
     terms = transposed_times(coupling_ref, inner) + matrix_times(trace_ref, view)
-    return jnp.where(living, terms, 0.0)
+    return jnp.where(six_times(living_ref[...]) > 0.0, terms, 0.0)
 
 
 def split3(value):
@@ -92,13 +162,14 @@
     return high, middle, low
 
 
-def exact_pick(values, chosen):
-    stacked = jnp.concatenate(split3(values), 0)
+def whole_pick(values, chosen):
+    high = jnp.floor(values * (1.0 / 256.0))
+    stacked = jnp.concatenate([high, values - 256.0 * high], 0).astype(BF16)
     sums = lax.dot_general(
         stacked, chosen, (((1,), (1,)), ((), ())), preferred_element_type=F32
     )
     rows = values.shape[0]
-    return sums[:rows] + sums[rows : 2 * rows] + sums[2 * rows :]
+    return 256.0 * sums[:rows] + sums[rows:]
 
 
 def face_major(terms_ref):
@@ -116,23 +187,70 @@
         jnp.where(wanted == names_ref[j : j + 1, :], 1.0, 0.0).astype(BF16)
         for j in range(4)
     ]
-    lists = exact_pick(face_major(terms_ref), jnp.concatenate(chosen, 1))
+    lists = whole_pick(face_major(terms_ref), jnp.concatenate(chosen, 1))
     return lists[:FD, :RIM], lists[:FD, RIM:]
 
 
 def first_kernel(
-    ids_ref, padding_ref, inverse_ref, coupling_ref, interior_load_ref, trace_load_ref, shift_ref, names_ref,
-    solved_ref, pushed_ref, up_ref, down_ref,
+    inverse_hbm, coupling_hbm, interior_load_hbm, trace_load_hbm, shift_hbm, names_hbm, padding_hbm,
+    living_ref, own_ref, on_ref, off_ref, solved_hbm,
+    solved_ref, inverse_ref, coupling_ref, interior_load_ref, trace_load_ref, shift_ref, names_ref, padding_ref, stage_ref, sems,
 ):
-    living = living_mask(padding_ref)
-    solved = matrix_times(inverse_ref, interior_load_ref[...].astype(F32))
+    rows = NI // PARTS
+    copies = [pltpu.make_async_copy(interior_load_hbm, interior_load_ref, sems.at[0])]
+    for part in range(PARTS):
+        block = pl.ds(part * rows, rows)
+        copies.append(
+            pltpu.make_async_copy(inverse_hbm.at[block], inverse_ref.at[block], sems.at[1 + part])
+        )
+    rest = [
+        (coupling_hbm, coupling_ref), (names_hbm, names_ref),
+        (trace_load_hbm, trace_load_ref), (shift_hbm, shift_ref), (padding_hbm, padding_ref),
+    ]
+    for place, (source, target) in enumerate(rest):
+        copies.append(pltpu.make_async_copy(source, target, sems.at[1 + PARTS + place]))
+    for copy in copies:
+        copy.start()
+    dom, sub = ids()
+    for copy in copies[2 + PARTS :]:
+        copy.wait()
+    padding = jnp.broadcast_to(padding_ref[:, :1], (1, LANES))
+    living = lane_iota(1) < LANES - padding
+    living_ref[...] = jnp.broadcast_to(jnp.where(living, 1.0, 0.0), (8, LANES))
+    stage_ref[NAMES:, :] = jnp.zeros((stage_ref.shape[0] - NAMES, LANES), F32)
+    loads, load_exponent = coded(trace_load_ref[...])
+    shifts, shift_exponent = coded(shift_ref[...])
+    for half in range(2):
+        columns = slice(half * RIM, half * RIM + RIM)
+        stage_ref[LOADS + FD * half : LOADS + FD * half + FD, :] = loads[:, columns]
+        stage_ref[SHIFTS + FD * half : SHIFTS + FD * half + FD, :] = shifts[:, columns]
+    stage_ref[NAMES : NAMES + 4, :] = names_ref[...].astype(F32)
+    stage_ref[SCALES + 1 : SCALES + 2, :] = spread_row(load_exponent)
+    stage_ref[SCALES + 2 : SCALES + 3, :] = spread_row(shift_exponent)
+    copies[0].wait()
+    load = interior_load_ref[...].astype(F32)
+    solved = []
+    for part in range(PARTS):
+        copies[1 + part].wait()
+        solved.append(matrix_times(inverse_ref.at[pl.ds(part * rows, rows)], load))
+    solved = jnp.concatenate(solved, 0)
     solved_ref[...] = solved
-    pushed_ref[...] = jnp.where(living, transposed_times(coupling_ref, solved), 0.0)
-    low, high = rim_lists(pushed_ref, names_ref)
-    owner = ids_ref[1] == SUB - 1
-    up_ref[:FD, :] = high + jnp.where(owner, trace_load_ref[:, RIM:], 0.0)
-    up_ref[FD:, :] = jnp.where(owner, shift_ref[:, RIM:], 0.0)
-    down_ref[...] = low
+    keep = pltpu.make_async_copy(solved_ref, solved_hbm, sems.at[PARTS + 6])
+    keep.start()
+    copies[1 + PARTS].wait()
+    whole, exponent = coded(jnp.where(living, transposed_times(coupling_ref, solved), 0.0))
+    stage_ref[:NF, :] = whole
+    stage_ref[SCALES : SCALES + 1, :] = spread_row(exponent)
+    low, high = rim_lists(stage_ref, names_ref)
+    owner = sub == SUB - 1
+    up = with_exponent(
+        high * jnp.exp2(exponent - 15.0) + jnp.where(owner, trace_load_ref[:, RIM:], 0.0)
+    )
+    up += [jnp.where(owner, shifts[:, RIM:], 0.0), spread_row(shift_exponent)]
+    down = [low, spread_row(exponent), jnp.zeros((FD + 1, LANES), F32)]
+    put_lists(on_ref, off_ref, up, down, dom)
+    own_ref[...] = as_sent(stage_ref[...])
+    keep.wait()
 
 
 def spread_rows(values, block):
@@ -252,34 +370,47 @@
         shifts_ref[pl.ds(j, FD, stride=4), :] = got[FD:]
 
 
+def put_terms(terms, names_ref, own_ref, on_ref, off_ref, stage_ref, dom):
+    whole, exponent = coded(terms)
+    stage_ref[:NF, :] = whole
+    stage_ref[NF:, :] = jnp.broadcast_to(exponent, (stage_ref.shape[0] - NF, LANES))
+    own_ref[...] = as_sent(stage_ref[...])
+    low, high = rim_lists(stage_ref, names_ref)
+    put_lists(on_ref, off_ref, [high, spread_row(exponent)], [low, spread_row(exponent)], dom)
+
+
 def second_kernel(
-    ids_ref, padding_ref, inverse_ref, coupling_ref, trace_ref, names_ref, pushed_ref, gathered_ref,
-    chunk_ref, lane_ref, valid_ref, weight_ref, shifts_ref, view_ref, terms_ref, up_ref, down_ref,
-    loads_ref,
+    inverse_ref, coupling_ref, trace_ref, names_ref, living_ref, sent_ref,
+    chunk_ref, lane_ref, valid_ref, weight_ref, shifts_ref, view_ref, terms_ref, own_ref, on_ref, off_ref, inner_ref,
+    loads_ref, stage_ref, gathered_ref,
 ):
-    dom, sub = ids_ref[0], ids_ref[1]
+    dom, sub = ids()
+    count = lax.axis_size("dom")
+    decode_first(sent_ref, gathered_ref)
     chunk, lane = partner_places(names_ref, gathered_ref, sub)
     chunk, lane = twice(chunk), twice(lane)
     names = twice(names_ref[...])
     valid = jnp.where((names < RIM) & (dom == 0), 0.0, 1.0)
-    weight = jnp.where((names >= FACES_PART) & (dom == ids_ref[2] - 1), 1.0, 0.5)
+    weight = jnp.where((names >= FACES_PART) & (dom == count - 1), 1.0, 0.5)
     chunk_ref[...] = chunk
     lane_ref[...] = lane
     valid_ref[...] = valid
     weight_ref[...] = weight
-    up_list = summed(gathered_ref, UP, UP + 24)
-    down_list = summed(gathered_ref, DOWN, DOWN + 12)
+    up_list = jnp.concatenate(
+        [summed(gathered_ref, UP, UP + FD), summed(gathered_ref, UP_SHIFT, UP_SHIFT + FD)], 0
+    )
+    down_list = summed(gathered_ref, DOWN, DOWN + FD)
     face_values(names_ref, gathered_ref, up_list, loads_ref, shifts_ref)
     own_load = jnp.where(six_times(names) < RIM, 0.0, loads_ref[...])
     partner = partner_terms(gathered_ref, chunk, lane, up_list[:FD], down_list)
-    view = jnp.where(six_times(valid) > 0.0, own_load + (pushed_ref[...] + partner), 0.0)
+    view = jnp.where(six_times(valid) > 0.0, own_load + (gathered_ref[sub, :NF, :] + partner), 0.0)
     view_ref[...] = view
-    terms_ref[...] = element_operator(
-        inverse_ref, coupling_ref, trace_ref, view, living_mask(padding_ref)
-    )
-    low, high = rim_lists(terms_ref, names_ref)
-    up_ref[...] = high
-    down_ref[...] = low
+    def keep(inner):
+        inner_ref[...] = inner
+
+    terms = element_operator(inverse_ref, coupling_ref, trace_ref, view, living_ref, keep)
+    terms_ref[...] = terms
+    put_terms(terms, names_ref, own_ref, on_ref, off_ref, stage_ref, dom)
 
 
 def next_view(gathered_ref, chunk_ref, lane_ref, valid_ref, shifts_ref, view_ref, terms_ref):
@@ -291,29 +422,45 @@
 
 
 def third_kernel(
-    padding_ref, inverse_ref, coupling_ref, trace_ref, names_ref, gathered_ref,
-    chunk_ref, lane_ref, valid_ref, shifts_ref, view_ref, terms_ref,
-    new_view_ref, new_terms_ref, up_ref, down_ref,
+    inverse_ref, coupling_ref, trace_ref, names_ref, living_ref, sent_ref,
+    chunk_ref, lane_ref, valid_ref, shifts_ref, view_ref, terms_ref, before_ref,
+    new_view_ref, new_terms_ref, own_ref, on_ref, off_ref, inner_ref,
+    stage_ref, gathered_ref,
 ):
+    dom, _ = ids()
+    decode_later(sent_ref, gathered_ref)
     view = next_view(gathered_ref, chunk_ref, lane_ref, valid_ref, shifts_ref, view_ref, terms_ref)
     new_view_ref[...] = view
-    new_terms_ref[...] = element_operator(
-        inverse_ref, coupling_ref, trace_ref, view, living_mask(padding_ref)
-    )
-    low, high = rim_lists(new_terms_ref, names_ref)
-    up_ref[...] = high
-    down_ref[...] = low
+    inner_ref[0] = before_ref[...]
+
+    def keep(inner):
+        inner_ref[1] = inner
+
+    terms = element_operator(inverse_ref, coupling_ref, trace_ref, view, living_ref, keep)
+    new_terms_ref[...] = terms
+    put_terms(terms, names_ref, own_ref, on_ref, off_ref, stage_ref, dom)
 
 
 def fourth_kernel(
-    padding_ref, inverse_ref, coupling_ref, trace_ref, gathered_ref,
-    chunk_ref, lane_ref, valid_ref, weight_ref, shifts_ref, first_view_ref, view_ref, terms_ref,
-    new_view_ref, sums_ref,
+    inverse_ref, coupling_ref, trace_ref, living_ref, sent_ref,
+    chunk_ref, lane_ref, valid_ref, weight_ref, shifts_ref, first_view_ref, view_ref, terms_ref, before_ref,
+    inner_hbm, sums_hbm,
+    inner_ref, sums_ref, gathered_ref, sems,
 ):
+    copies = [
+        pltpu.make_async_copy(before_ref, inner_hbm.at[pl.ds(0, 2)], sems.at[0]),
+        pltpu.make_async_copy(inner_ref, inner_hbm.at[2], sems.at[1]),
+    ]
+    copies[0].start()
+
+    def keep(inner):
+        inner_ref[...] = inner
+        copies[1].start()
+
+    decode_later(sent_ref, gathered_ref)
     first, second = first_view_ref[...], view_ref[...]
     third = next_view(gathered_ref, chunk_ref, lane_ref, valid_ref, shifts_ref, view_ref, terms_ref)
-    new_view_ref[...] = third
-    last = element_operator(inverse_ref, coupling_ref, trace_ref, third, living_mask(padding_ref))
+    last = element_operator(inverse_ref, coupling_ref, trace_ref, third, living_ref, keep)
     weight = six_times(weight_ref[...])
     last = last + weight * (shifts_ref[...] * third)
     views = (first, second, third)
@@ -324,14 +471,32 @@
     for place, product in enumerate(products):
         total = product.reshape(6, 8, LANES).sum(0).sum(0, keepdims=True).sum(1, keepdims=True)
         sums = sums + jnp.where(lane == place, total, 0.0)
-    sums_ref[...] = sums
+    sums_ref[...] = jnp.broadcast_to(sums, sums_ref.shape)
+    send = pltpu.make_async_copy(sums_ref, sums_hbm, sems.at[2])
+    send.start()
+    for copy in copies:
+        copy.wait()
+    send.wait()
 
 
 def owner_kernel(
-    ids_ref, first_ref, second_ref, third_ref, trace_load_ref, shift_ref,
-    owned_ref, terms_ref, chosen_ref,
+    first_sent_ref, second_sent_ref, third_sent_ref, trace_load_hbm, shift_hbm, *rest,
 ):
-    sub = ids_ref[1]
+    solved_hbm, inner_hbm = rest[:2]
+    owned_ref, kept_ref, terms_ref, chosen_ref, first_ref, second_ref, third_ref = rest[2:9]
+    trace_load_ref, shift_ref, sems = rest[9:]
+    copies = [
+        pltpu.make_async_copy(trace_load_hbm, trace_load_ref, sems.at[0]),
+        pltpu.make_async_copy(shift_hbm, shift_ref, sems.at[1]),
+        pltpu.make_async_copy(solved_hbm, kept_ref.at[0], sems.at[2]),
+        pltpu.make_async_copy(inner_hbm, kept_ref.at[pl.ds(1, 3)], sems.at[3]),
+    ]
+    for copy in copies:
+        copy.start()
+    decode_first(first_sent_ref, first_ref)
+    decode_later(second_sent_ref, second_ref)
+    decode_later(third_sent_ref, third_ref)
+    _, sub = ids()
     wanted = lax.broadcasted_iota(jnp.int32, (2 * RIM, LANES), 0) + (RIM + 2 * RIM * sub)
     sources = (first_ref, second_ref, third_ref)
     for s in range(SUB):
@@ -348,6 +513,8 @@
     sums = lax.dot_general(
         terms_ref[...], chosen_ref[...], (((1,), (1,)), ((), ())), preferred_element_type=F32
     )
+    for copy in copies:
+        copy.wait()
     last = sub == SUB - 1
     downs = (
         summed(first_ref, DOWN, DOWN + FD),
@@ -422,107 +589,126 @@
 
 
 def last_kernel(
-    padding_ref, inverse_ref, coupling_ref, all_sums_ref, first_view_ref, second_view_ref, third_view_ref,
-    solved_ref, owned_ref,
+    living_ref, all_sums_ref, inner_ref, owned_ref,
     traces_ref, interior_ref,
 ):
     sums = all_sums_ref[...].reshape(-1, 8, LANES).sum(0).sum(0, keepdims=True)
     a, b, c = coefficients(sums)
     traces_ref[...] = a * owned_ref[0] + b * owned_ref[1] + c * owned_ref[2]
-    view = a * first_view_ref[...] + b * second_view_ref[...] + c * third_view_ref[...]
-    lifted = matrix_times(inverse_ref, matrix_times(coupling_ref, view))
-    interior_ref[...] = jnp.where(living_mask(padding_ref), solved_ref[...] - lifted, 0.0)
-
-
-def call(kernel, outputs, inputs, scalars=0, scratch=()):
-    shape = [jax.ShapeDtypeStruct(s, d) for s, d in outputs]
+    lifted = a * inner_ref[1] + b * inner_ref[2] + c * inner_ref[3]
+    living = jnp.broadcast_to(living_ref[:1, :], (NI, LANES)) > 0.0
+    interior_ref[...] = jnp.where(living, inner_ref[0] - lifted, 0.0)
+
+
+def call(kernel, outputs, inputs, scratch=(), limit=6, from_hbm=(), to_hbm=()):
+    held = [pltpu.with_memory_space_constraint(x, pltpu.HBM) for x in from_hbm]
+    near, far = pl.BlockSpec(memory_space=pltpu.VMEM), pl.BlockSpec(memory_space=pltpu.HBM)
     return pl.pallas_call(
         kernel,
-        out_shape=shape,
-        in_specs=[
-            pl.BlockSpec(memory_space=pltpu.SMEM if i < scalars else pltpu.VMEM)
-            for i in range(len(inputs))
-        ],
-        out_specs=[pl.BlockSpec(memory_space=pltpu.VMEM)] * len(shape),
+        out_shape=[jax.ShapeDtypeStruct(s, d) for s, d in outputs]
+        + [pltpu.HBM(s, d) for s, d in to_hbm],
+        in_specs=[near] * len(inputs) + [far] * len(held),
+        out_specs=[near] * len(outputs) + [far] * len(to_hbm),
         scratch_shapes=list(scratch),
-        compiler_params=pltpu.CompilerParams(vmem_limit_bytes=VMEM_LIMIT),
-    )(*inputs)
-
-
-def to_all(value):
+        compiler_params=pltpu.CompilerParams(vmem_limit_bytes=limit * MIB),
+    )(*inputs, *held)
+
+
+def to_all(blocks, rows):
+    rest = rows - sum(len(block) for block in blocks)
+    value = jnp.concatenate(blocks + [jnp.zeros((rest, LANES), I16)], 0)
     copies = jnp.broadcast_to(value[None], (SUB,) + value.shape)
     return lax.all_to_all(copies, "sub", 0, 0, tiled=True)
 
 
-def neighbours(up, down):
+def neighbours(on, off):
     count = lax.axis_size("dom")
-    from_below = lax.ppermute(up, "dom", [(i, i + 1) for i in range(count - 1)])
-    from_above = lax.ppermute(down, "dom", [(i + 1, i) for i in range(count - 1)])
-    return from_below, from_above
+    pairs = [(i, i + 1) for i in range(1, count - 1, 2)]
+    from_off = lax.ppermute(off, "dom", pairs + [(j, i) for i, j in pairs])
+    from_on = lax.ppermute(on, "dom", [(i, i ^ 1) for i in range(count)])
+    even = lax.axis_index("dom") % 2 == 0
+    return jnp.where(even, from_off, from_on), jnp.where(even, from_on, from_off)
+
+
+def later(own, on, off):
+    from_below, from_above = neighbours(on, off)
+    return to_all([own[:LATER_UP], from_below[: FD + 1], from_above[: FD + 1]], LATER_ROWS)
 
 
 def on_device(
     interior_inverse, coupling, trace_block, interior_load, trace_load, face_shift, element_faces, block_padding,
 ):
-    ids = jnp.stack(
-        [lax.axis_index("dom"), lax.axis_index("sub"), jnp.int32(lax.axis_size("dom"))]
-    ).astype(jnp.int32)
-    slab, lists = ((NF, LANES), F32), ((FD, LANES), F32)
-    solved, pushed, up, down = call(
+    slab, rows8 = ((NF, LANES), F32), ((8, LANES), F32)
+    places = ((8, LANES), jnp.int32)
+    sent = [((64, LANES), I16), ((16, LANES), I16), ((16, LANES), I16)]
+    stage = pltpu.VMEM((64, LANES), F32)
+    decoded = pltpu.VMEM((SUB, LATER_ROWS, LANES), F32)
+    decoded_first = pltpu.VMEM((SUB, FIRST_ROWS, LANES), F32)
+    matrices = [interior_inverse, coupling, trace_block]
+
+    inner = ((NI, LANES), F32)
+
+    living, own, on, off, solved = call(
         first_kernel,
-        [((NI, LANES), F32), slab, ((2 * FD, LANES), F32), lists],
-        [ids, block_padding, interior_inverse, coupling, interior_load, trace_load, face_shift, element_faces],
-        scalars=2,
-    )
-    from_below, from_above = neighbours(up, down)
-    first = to_all(
-        jnp.concatenate(
-            [
-                pushed, from_below, from_above,
-                trace_load[:, :RIM], trace_load[:, RIM:], face_shift[:, :RIM], face_shift[:, RIM:],
-                element_faces.astype(F32),
-            ],
-            0,
-        )
-    )
-    eight_i, eight_f = ((8, LANES), jnp.int32), ((8, LANES), F32)
-    chunk, lane, valid, weight, shifts, view0, terms, up, down = call(
+        [rows8, ((112, LANES), I16), ((32, LANES), I16), ((32, LANES), I16)],
+        [],
+        from_hbm=[
+            interior_inverse, coupling, interior_load, trace_load, face_shift, element_faces,
+            jnp.pad(block_padding, (0, LANES - 1))[None],
+        ],
+        to_hbm=[inner],
+        scratch=[
+            pltpu.VMEM((NI, LANES), F32), pltpu.VMEM((NI, NI, LANES), BF16), pltpu.VMEM((NI, NF, LANES), BF16),
+            pltpu.VMEM((NI, LANES), BF16), pltpu.VMEM((FD, 2 * RIM), F32), pltpu.VMEM((FD, 2 * RIM), F32),
+            pltpu.VMEM((4, LANES), jnp.int32), pltpu.VMEM((1, LANES), jnp.int32), pltpu.VMEM((112, LANES), F32),
+            pltpu.SemaphoreType.DMA((PARTS + 7,)),
+        ],
+        limit=10,
+    )
+    from_below, from_above = neighbours(on, off)
+    first = to_all([own[:UP], from_below[: DOWN - UP], from_above[: FD + 1]], FIRST_ROWS)
+    chunk, lane, valid, weight, shifts, view0, terms, own, on, off, kept = call(
         second_kernel,
-        [eight_i, eight_i, eight_f, eight_f, slab, slab, slab, lists, lists],
-        [ids, block_padding, interior_inverse, coupling, trace_block, element_faces, pushed, first],
-        scalars=2,
-        scratch=[pltpu.VMEM((NF, LANES), F32)],
-    )
-    second = to_all(jnp.concatenate([terms, *neighbours(up, down)], 0))
-    view1, terms1, up, down = call(
+        [places, places, rows8, rows8, slab, slab, slab, *sent, inner],
+        [*matrices, element_faces, living, first],
+        scratch=[pltpu.VMEM((NF, LANES), F32), stage, decoded_first],
+    )
+    second = later(own, on, off)
+    view1, terms1, own, on, off, kept = call(
         third_kernel,
-        [slab, slab, lists, lists],
-        [block_padding, interior_inverse, coupling, trace_block, element_faces, second, chunk, lane, valid, shifts, view0, terms],
-        scalars=1,
-    )
-    third = to_all(jnp.concatenate([terms1, *neighbours(up, down)], 0))
-    view2, sums = call(
+        [slab, slab, *sent, ((2, NI, LANES), F32)],
+        [*matrices, element_faces, living, second, chunk, lane, valid, shifts, view0, terms, kept],
+        scratch=[stage, decoded],
+    )
+    third = later(own, on, off)
+    everyone = lax.axis_size("dom") * SUB
+    kept, sums = call(
         fourth_kernel,
-        [slab, ((1, LANES), F32)],
-        [block_padding, interior_inverse, coupling, trace_block, third, chunk, lane, valid, weight, shifts, view0, view1, terms1],
-        scalars=1,
-    )
-    everyone = lax.axis_size("dom") * SUB
-    all_sums = lax.all_to_all(
-        jnp.broadcast_to(sums, (everyone, LANES)), ("dom", "sub"), 0, 0, tiled=True
-    )
-    (owned,) = call(
+        [],
+        [*matrices, living, third, chunk, lane, valid, weight, shifts, view0, view1, terms1, kept],
+        to_hbm=[((3, NI, LANES), F32), ((everyone, LANES), F32)],
+        scratch=[
+            pltpu.VMEM((NI, LANES), F32), pltpu.VMEM((everyone, LANES), F32), decoded,
+            pltpu.SemaphoreType.DMA((3,)),
+        ],
+    )
+    all_sums = lax.all_to_all(sums, ("dom", "sub"), 0, 0, tiled=True)
+    owned, kept = call(
         owner_kernel,
-        [((3, FD, 2 * RIM), F32)],
-        [ids, first, second, third, trace_load, face_shift],
-        scalars=1,
-        scratch=[pltpu.VMEM((144, 32 * LANES), BF16), pltpu.VMEM((2 * RIM, 32 * LANES), BF16)],
+        [((3, FD, 2 * RIM), F32), ((4, NI, LANES), F32)],
+        [first, second, third],
+        from_hbm=[trace_load, face_shift, solved, kept],
+        scratch=[
+            pltpu.VMEM((144, 32 * LANES), BF16), pltpu.VMEM((2 * RIM, 32 * LANES), BF16),
+            decoded_first, decoded, decoded,
+            pltpu.VMEM((FD, 2 * RIM), F32), pltpu.VMEM((FD, 2 * RIM), F32), pltpu.SemaphoreType.DMA((4,)),
+        ],
+        limit=14,
     )
     traces, interior = call(
         last_kernel,
         [((FD, 2 * RIM), F32), ((NI, LANES), F32)],
-        [block_padding, interior_inverse, coupling, all_sums, view0, view1, view2, solved, owned],
-        scalars=1,
+        [living, all_sums, kept, owned],
     )
     return traces, interior
 

time: 119 us -> 97.8 us (0.82)
  blocking collectives: 53.3 us -> 42 us
  local copies, waits for them, and re-layouts: 9.86 us -> 2.61 us
  waiting for transfers between devices: 15.6 us -> 13.2 us
  starting transfers between devices: 27.9 us -> 25.8 us
  Pallas kernels: 9.98 us -> 12 us
    all_to_all x3, blocking collectives: 53.3 us -> 42 us  [to_all(): return lax.all_to_all(copies, 'sub', 0, 0, tiled=True)]
    unnamed x44 -> x16, local copies, waits for them, and re-layouts: 8.85 us -> 1.85 us
    ppermute x6, starting transfers between devices: 18.6 us -> 14.6 us  [the longest x3 13.4 us: neighbours(): from_off = lax.ppermute(off, 'dom', pairs + [(j, i) for i, j in pairs])]
    ppermute x6, waiting for transfers between devices: 7.17 us -> 4.24 us  [the longest x3 4.23 us: neighbours(): from_off = lax.ppermute(off, 'dom', pairs + [(j, i) for i, j in pairs])]
    pallas_call x6, Pallas kernels: 9.98 us -> 12 us  [call(): pl.pallas_call(kernel, out_shape=[jax.ShapeDtypeStruct(s, d) for s, d in...]
    all_to_all x1, starting transfers between devices: 9.35 us -> 11.2 us  [on_device(): all_sums = lax.all_to_all(sums, ('dom', 'sub'), 0, 0, tiled=True)]
where the time goes in v2:
time: 97.8 us; the launch traced here: 97.4 us
  blocking collectives  42 us (43%)
  starting transfers between devices  25.8 us (26%)
  waiting for transfers between devices  13.2 us (13%)
  Pallas kernels  12 us (12%)
  local copies, waits for them, and re-layouts  2.61 us (3%)
  between operations  1.51 us (2%)
    all_to_all x3, blocking collectives, to_all(): return lax.all_to_all(copies, 'sub', 0, 0, tiled=True)  42 us
    ppermute x3, starting transfers between devices, neighbours(): from_off = lax.ppermute(off, 'dom', pairs + [(j, i) for i, j in pairs])  13.4 us
    pallas_call x6, Pallas kernels, call(): pl.pallas_call(kernel, out_shape=[jax.ShapeDtypeStruct(s, d) for s, d in...  12 us
    all_to_all x1, starting transfers between devices, on_device(): all_sums = lax.all_to_all(sums, ('dom', 'sub'), 0, 0, tiled=True)  11.2 us
    all_to_all x1, waiting for transfers between devices, on_device(): all_sums = lax.all_to_all(sums, ('dom', 'sub'), 0, 0, tiled=True)  8.93 us
    ppermute x3, waiting for transfers between devices, neighbours(): from_off = lax.ppermute(off, 'dom', pairs + [(j, i) for i, j in pairs])  4.23 us
  transfers between devices with their start and end apart: 7, of which 4 were waited for; matrix products, arithmetic and copies ran while one was open for 0% of the time, Pallas kernels for 2%

profile of v2, /device:TPU:1, one launch (start us, length us, event | category | flops | bytes accessed | tf_op | source)
XLA Modules:
  0.0 97.4 jit_solution(13022139705912395867)
XLA Ops:
  1.3 0.5 pad_bitcast_fusion.padding_hbm
  1.8 2.9 %shard_map.95 = (f32[8,128]{1,0:T(8,128)S(1)}, s16[112,128]{1,0:T(8,128)(2,1)S(1)}, s16[32,128]{1,0:T(8,128)(2,1)S(1)}, s16[32,128]{1,0:T(8,128)(2,1)S(1)}, f32[80,128]{1,0:T(8,128)}) custom-call(bf16[80,80,128]{2,1,0:T(8,128)(2,1)} %inverse_ref.5, bf16[80,48,128]{2,1,0:T(8,128)(2,1)} %coupling_ref.5, bf16[80,128]{1,0:T(8,128)(2,1)} %interior_load_hbm.1, ...), custom_call_target="tpu_custom_call" | custom-call | tf_op jit(solution)/shard_map/pallas_call | solution.py:606
  4.7 4.5 %collective-permute-start = (s16[32,128]{1,0:T(8,128)(2,1)S(1)}, s16[32,128]{1,0:T(8,128)(2,1)S(1)}, u32[]{:S(2)}, u32[]{:S(2)}) collective-permute-start(s16[32,128]{1,0:T(8,128)(2,1)S(1)} %get-tuple-element.30), channel_id=1, source_target_pairs={{8,16},{24,32},{40,48},{56,64},{72,80},{88,96},{104,112},{120,128}... | collective-permute-start | bytes 24584 | tf_op jit(solution)/shard_map/ppermute | solution.py:627
  9.2 0.1 collective-permute-start.1
  9.4 0.1 pad.16.clone
  9.5 1.1 %collective-permute-done = s16[32,128]{1,0:T(8,128)(2,1)S(1)} collective-permute-done((s16[32,128]{1,0:T(8,128)(2,1)S(1)}, s16[32,128]{1,0:T(8,128)(2,1)S(1)}, u32[]{:S(2)}, u32[]{:S(2)}) %collective-permute-start) | collective-permute-done | bytes 8224 | tf_op jit(solution)/shard_map/ppermute | solution.py:627
  10.6 0.0 collective-permute-done.1
  10.6 0.1 add_add_fusion
  10.7 20.7 %all_to_all.26.sent_ref.first_sent_ref = s16[8,144,128]{2,1,0:T(8,128)(2,1)S(1)} all-to-all(s16[8,144,128]{2,1,0:T(8,128)(2,1)S(1)} %broadcast_in_dim.12), channel_id=1, replica_groups=mesh['dom'=32,'sub'=8] {'sub'}, dimensions={0} | all-to-all | bytes 589824 | tf_op jit(solution)/shard_map/all_to_all | solution.py:621
  31.4 0.0 copy-done
  31.4 2.4 %shard_map.96 = (s32[8,128]{1,0:T(8,128)S(1)}, s32[8,128]{1,0:T(8,128)S(1)}, f32[8,128]{1,0:T(8,128)S(1)}, f32[8,128]{1,0:T(8,128)S(1)}, f32[48,128]{1,0:T(8,128...) custom-call(bf16[80,80,128]{2,1,0:T(8,128)(2,1)S(1)} %copy-done, ...), custom_call_target="tpu_custom_call" | custom-call | tf_op jit(solution)/shard_map/pallas_call | solution.py:606
  33.8 0.9 collective-permute-start.3
  34.7 3.2 %collective-permute-start.2 = (s16[16,128]{1,0:T(8,128)(2,1)S(1)}, s16[16,128]{1,0:T(8,128)(2,1)S(1)}, u32[]{:S(2)}, u32[]{:S(2)}) collective-permute-start(s16[16,128]{1,0:T(8,128)(2,1)S(1)} %get-tuple-element.33), channel_id=1, source_target_pairs={{8,16},{24,32},{40,48},{56,64},{72,80},{88,96},{104,112},{120,128}... | collective-permute-start | bytes 12296 | tf_op jit(solution)/shard_map/ppermute | solution.py:627
  38.0 0.1 pad.12.clone
  38.1 0.0 collective-permute-done.3
  38.1 1.6 %collective-permute-done.2 = s16[16,128]{1,0:T(8,128)(2,1)S(1)} collective-permute-done((s16[16,128]{1,0:T(8,128)(2,1)S(1)}, s16[16,128]{1,0:T(8,128)(2,1)S(1)}, u32[]{:S(2)}, u32[]{:S(2)}) %collective-permute-start.2) | collective-permute-done | bytes 4128 | tf_op jit(solution)/shard_map/ppermute | solution.py:627
  39.7 0.1 add_add_fusion.1
  39.8 10.7 %all_to_all.27.sent_ref.second_sent_ref = s16[8,80,128]{2,1,0:T(8,128)(2,1)S(1)} all-to-all(s16[8,80,128]{2,1,0:T(8,128)(2,1)S(1)} %broadcast_in_dim.13), channel_id=1, replica_groups=mesh['dom'=32,'sub'=8] {'sub'}, dimensions={0} | all-to-all | bytes 327680 | tf_op jit(solution)/shard_map/all_to_all | solution.py:621
  50.4 1.6 %shard_map.97 = (f32[48,128]{1,0:T(8,128)S(1)}, f32[48,128]{1,0:T(8,128)S(1)}, s16[64,128]{1,0:T(8,128)(2,1)S(1)}, s16[16,128]{1,0:T(8,128)(2,1)S(1)}, s16[16,12...) custom-call(bf16[80,80,128]{2,1,0:T(8,128)(2,1)S(1)} %copy-done, bf16[80,48,128]{2,1,0:T(8,128)(2,1)S(1)} %copy-done.1, ...), custom_call_target="tpu_custom_call" | custom-call | tf_op jit(solution)/shard_map/pallas_call | solution.py:606
  52.1 0.1 collective-permute-start.5
  52.2 5.7 %collective-permute-start.4 = (s16[16,128]{1,0:T(8,128)(2,1)S(1)}, s16[16,128]{1,0:T(8,128)(2,1)S(1)}, u32[]{:S(2)}, u32[]{:S(2)}) collective-permute-start(s16[16,128]{1,0:T(8,128)(2,1)S(1)} %get-tuple-element.43), channel_id=1, source_target_pairs={{8,16},{24,32},{40,48},{56,64},{72,80},{88,96},{104,112},{120,128}... | collective-permute-start | bytes 12296 | tf_op jit(solution)/shard_map/ppermute | solution.py:627
  57.9 0.0 collective-permute-done.5
  57.9 1.5 %collective-permute-done.4 = s16[16,128]{1,0:T(8,128)(2,1)S(1)} collective-permute-done((s16[16,128]{1,0:T(8,128)(2,1)S(1)}, s16[16,128]{1,0:T(8,128)(2,1)S(1)}, u32[]{:S(2)}, u32[]{:S(2)}) %collective-permute-start.4) | collective-permute-done | bytes 4128 | tf_op jit(solution)/shard_map/ppermute | solution.py:627
  59.4 0.1 add_add_fusion.2
  59.5 10.7 %all_to_all.28.sent_ref.third_sent_ref = s16[8,80,128]{2,1,0:T(8,128)(2,1)S(1)} all-to-all(s16[8,80,128]{2,1,0:T(8,128)(2,1)S(1)} %broadcast_in_dim.28), channel_id=1, replica_groups=mesh['dom'=32,'sub'=8] {'sub'}, dimensions={0} | all-to-all | bytes 327680 | tf_op jit(solution)/shard_map/all_to_all | solution.py:621
  70.2 2.1 %shard_map.98 = (f32[3,80,128]{2,1,0:T(8,128)}, f32[256,128]{1,0:T(8,128)}) custom-call(bf16[80,80,128]{2,1,0:T(8,128)(2,1)S(1)} %copy-done, bf16[80,48,128]{2,1,0:T(8,128)(2,1)S(1)} %copy-done.1, bf16[48,48,128]{2,1,0:T(8,128)(2,1)S(1)} %copy-done.2, f32[8,128]{1,0:T(8,128)S(1)} %get-tuple-element.28.living_ref, ...), custom_call_target="tpu_custom_call" | custom-call | tf_op jit(solution)/shard_map/pallas_call | solution.py:606
  72.3 11.2 %all-to-all-start.3 = ((f32[256,1,128]{2,1,0:T(1,128)}), f32[256,1,128]{2,1,0:T(1,128)S(1)}, u32[]{:S(2)}, u32[]{:S(2)}) async-start(f32[256,1,128]{2,1,0:T(1,128)} %bitcast.7), calls=%async_computation.3 | async-start | bytes 262144 | tf_op jit(solution)/shard_map/all_to_all | solution.py:695
  83.6 0.9 copy-done.4
  84.5 0.9 copy-done.6
  85.4 2.3 %shard_map.99 = (f32[3,12,256]{2,1,0:T(8,128)S(1)}, f32[4,80,128]{2,1,0:T(8,128)S(1)}) custom-call(s16[8,144,128]{2,1,0:T(8,128)(2,1)S(1)} %all_to_all.26.sent_ref.first_sent_ref, s16[8,80,128]{2,1,0:T(8,128)(2,1)S(1)} %copy-done.4, s16[8,80,128]{2,1,0:T(8,128)(2,1)S(1)} %copy-done.6, f32[12,256]{1,0:T(8,128)} %trace_load_hbm.3, f32[12,256]{1,0:T(8,128)} %shift_hbm.3, ...), custom_call_target="tpu_custom_call" | custom-call | tf_op jit(solution)/shard_map/pallas_call | solution.py:606
  87.6 8.9 %all-to-all-done.3 = f32[256,1,128]{2,1,0:T(1,128)S(1)} async-done(((f32[256,1,128]{2,1,0:T(1,128)}), f32[256,1,128]{2,1,0:T(1,128)S(1)}, u32[]{:S(2)}, u32[]{:S(2)}) %all-to-all-start.3) | async-done | bytes 131104 | tf_op jit(solution)/shard_map/all_to_all | solution.py:695
  96.6 0.8 shard_map.100
  (25 shorter events, 0.1 us)
Async XLA Ops:
  1.8 29.6 %copy-start = (bf16[80,80,128]{2,1,0:T(8,128)(2,1)S(1)}, bf16[80,80,128]{2,1,0:T(8,128)(2,1)}, u32[]{:S(2)}) copy-start(bf16[80,80,128]{2,1,0:T(8,128)(2,1)} %inverse_ref.5) | copy-start | bytes 4915204
  1.8 29.6 %copy-start.1 = (bf16[80,48,128]{2,1,0:T(8,128)(2,1)S(1)}, bf16[80,48,128]{2,1,0:T(8,128)(2,1)}, u32[]{:S(2)}) copy-start(bf16[80,48,128]{2,1,0:T(8,128)(2,1)} %coupling_ref.5) | copy-start | bytes 2949124
  1.8 29.6 %copy-start.2 = (bf16[48,48,128]{2,1,0:T(8,128)(2,1)S(1)}, bf16[48,48,128]{2,1,0:T(8,128)(2,1)}, u32[]{:S(2)}) copy-start(bf16[48,48,128]{2,1,0:T(8,128)(2,1)} %trace_ref.5) | copy-start | bytes 1769476
  1.8 29.6 %copy-start.7 = (s32[4,128]{1,0:T(4,128)S(1)}, s32[4,128]{1,0:T(4,128)}, u32[]{:S(2)}) copy-start(s32[4,128]{1,0:T(4,128)} %names_ref.3) | copy-start | bytes 6148
  4.7 5.8 %collective-permute-start = (s16[32,128]{1,0:T(8,128)(2,1)S(1)}, s16[32,128]{1,0:T(8,128)(2,1)S(1)}, u32[]{:S(2)}, u32[]{:S(2)}) collective-permute-start(s16[32,128]{1,0:T(8,128)(2,1)S(1)} %get-tuple-element.30), channel_id=1, source_target_pairs={{8,16},{24,32},{40,48},{56,64},{72,80},{88,96},{104,112},{120,128}... | collective-permute-start | bytes 24584 | tf_op jit(solution)/shard_map/ppermute | solution.py:627
  9.2 1.3 %collective-permute-start.1 = (s16[32,128]{1,0:T(8,128)(2,1)S(1)}, s16[32,128]{1,0:T(8,128)(2,1)S(1)}, u32[]{:S(2)}, u32[]{:S(2)}) collective-permute-start(s16[32,128]{1,0:T(8,128)(2,1)S(1)} %get-tuple-element.31), channel_id=1, source_target_pairs={{0,8},{8,0},{16,24},{24,16},{32,40},{40,32},{48,56},{56,48},{64,72... | collective-permute-start | bytes 24584 | tf_op jit(solution)/shard_map/ppermute | solution.py:628
  33.8 4.3 %collective-permute-start.3 = (s16[16,128]{1,0:T(8,128)(2,1)S(1)}, s16[16,128]{1,0:T(8,128)(2,1)S(1)}, u32[]{:S(2)}, u32[]{:S(2)}) collective-permute-start(s16[16,128]{1,0:T(8,128)(2,1)S(1)} %get-tuple-element.34), channel_id=1, source_target_pairs={{0,8},{8,0},{16,24},{24,16},{32,40},{40,32},{48,56},{56,48},{64,72... | collective-permute-start | bytes 12296 | tf_op jit(solution)/shard_map/ppermute | solution.py:628
  34.7 4.9 %collective-permute-start.2 = (s16[16,128]{1,0:T(8,128)(2,1)S(1)}, s16[16,128]{1,0:T(8,128)(2,1)S(1)}, u32[]{:S(2)}, u32[]{:S(2)}) collective-permute-start(s16[16,128]{1,0:T(8,128)(2,1)S(1)} %get-tuple-element.33), channel_id=1, source_target_pairs={{8,16},{24,32},{40,48},{56,64},{72,80},{88,96},{104,112},{120,128}... | collective-permute-start | bytes 12296 | tf_op jit(solution)/shard_map/ppermute | solution.py:627
  50.4 1.6 %copy-start.3 = (s16[8,80,128]{2,1,0:T(8,128)(2,1)}, s16[8,80,128]{2,1,0:T(8,128)(2,1)S(1)}, u32[]{:S(2)}) copy-start(s16[8,80,128]{2,1,0:T(8,128)(2,1)S(1)} %all_to_all.27.sent_ref.second_sent_ref) | copy-start | bytes 491524
  52.1 5.8 %collective-permute-start.5 = (s16[16,128]{1,0:T(8,128)(2,1)S(1)}, s16[16,128]{1,0:T(8,128)(2,1)S(1)}, u32[]{:S(2)}, u32[]{:S(2)}) collective-permute-start(s16[16,128]{1,0:T(8,128)(2,1)S(1)} %get-tuple-element.44), channel_id=1, source_target_pairs={{0,8},{8,0},{16,24},{24,16},{32,40},{40,32},{48,56},{56,48},{64,72... | collective-permute-start | bytes 12296 | tf_op jit(solution)/shard_map/ppermute | solution.py:628
  52.2 7.3 %collective-permute-start.4 = (s16[16,128]{1,0:T(8,128)(2,1)S(1)}, s16[16,128]{1,0:T(8,128)(2,1)S(1)}, u32[]{:S(2)}, u32[]{:S(2)}) collective-permute-start(s16[16,128]{1,0:T(8,128)(2,1)S(1)} %get-tuple-element.43), channel_id=1, source_target_pairs={{8,16},{24,32},{40,48},{56,64},{72,80},{88,96},{104,112},{120,128}... | collective-permute-start | bytes 12296 | tf_op jit(solution)/shard_map/ppermute | solution.py:627
  70.2 2.1 %copy-start.5 = (s16[8,80,128]{2,1,0:T(8,128)(2,1)}, s16[8,80,128]{2,1,0:T(8,128)(2,1)S(1)}, u32[]{:S(2)}) copy-start(s16[8,80,128]{2,1,0:T(8,128)(2,1)S(1)} %all_to_all.28.sent_ref.third_sent_ref) | copy-start | bytes 491524
  72.3 24.2 %all-to-all-start.3 = ((f32[256,1,128]{2,1,0:T(1,128)}), f32[256,1,128]{2,1,0:T(1,128)S(1)}, u32[]{:S(2)}, u32[]{:S(2)}) async-start(f32[256,1,128]{2,1,0:T(1,128)} %bitcast.7), calls=%async_computation.3 | async-start | bytes 262144 | tf_op jit(solution)/shard_map/all_to_all | solution.py:695
  83.5 0.9 copy-start.4
  84.5 0.9 copy-start.6

commit v3 on v2

--- a/solution.py
+++ b/solution.py
@@ -21,6 +21,8 @@
 
 I16 = jnp.int16
 
+BIAS = 16384.0
+SCALE_LANE = 64
 PUSHED, LOADS, SHIFTS, NAMES, SCALES, UP, UP_SHIFT, DOWN, FIRST_END, FIRST_ROWS = (
     0, 48, 72, 96, 100, 103, 116, 129, 142, 144,
 )
@@ -87,7 +89,7 @@
 
 
 def spread_row(exponent):
-    return jnp.broadcast_to(exponent, (1, LANES))
+    return jnp.broadcast_to(exponent + BIAS, (1, LANES))
 
 
 def as_sent(value):
@@ -107,39 +109,52 @@
     off_ref[...] = as_sent(jnp.where(even, down, up))
 
 
-def decode(sent_ref, terms_ref, sections):
+def decode(sent_ref, terms_ref, sections, scale_rows, least=None):
     rows = sent_ref.shape[1]
     row = row_iota(rows)
     for s in range(SUB):
-        values = sent_ref[s].astype(jnp.int32).astype(F32)
-        terms_ref[s] = values
+        terms_ref[s] = sent_ref[s].astype(jnp.int32).astype(F32)
+    base = least
+    for s in range(SUB):
+        for place in scale_rows:
+            exponent = terms_ref[s, place : place + 1, :] - BIAS
+            base = exponent if base is None else jnp.maximum(base, exponent)
+    for s in range(SUB):
         factors = jnp.ones((1, LANES), F32)
-        for end, exponent in reversed(sections):
+        for end, exponent, scaled in reversed(sections):
             if exponent is None:
                 factor = jnp.ones((1, LANES), F32)
             else:
-                factor = jnp.exp2(terms_ref[s, exponent : exponent + 1, :] - 15.0)
+                power = terms_ref[s, exponent : exponent + 1, :] - (BIAS + 15.0)
+                factor = jnp.exp2(power - base if scaled else power)
             factors = jnp.where(row < end, factor, factors)
-        terms_ref[s] = values * factors
+        terms_ref[s] = terms_ref[s] * factors
+    return base
 
 
 def decode_first(sent_ref, terms_ref):
-    decode(
+    return decode(
         sent_ref,
         terms_ref,
         [
-            (LOADS, SCALES), (SHIFTS, SCALES + 1), (NAMES, SCALES + 2), (UP, None),
-            (UP + FD, UP + FD), (UP_SHIFT, None), (UP_SHIFT + FD, UP_SHIFT + FD), (DOWN, None),
-            (FIRST_END, DOWN + FD),
+            (LOADS, SCALES, True), (SHIFTS, SCALES + 1, True), (NAMES, SCALES + 2, False), (UP, None, False),
+            (UP + FD, UP + FD, True), (UP_SHIFT, None, False), (UP_SHIFT + FD, UP_SHIFT + FD, False),
+            (DOWN, None, False), (FIRST_END, DOWN + FD, True),
         ],
-    )
-
-
-def decode_later(sent_ref, terms_ref):
-    decode(
+        (SCALES, SCALES + 1, UP + FD, DOWN + FD),
+    )
+
+
+def decode_later(sent_ref, terms_ref, before):
+    return decode(
         sent_ref,
         terms_ref,
-        [(NF, NF), (LATER_UP, None), (LATER_UP + FD, LATER_UP + FD), (LATER_DOWN, None), (LATER_END, LATER_DOWN + FD)],
+        [
+            (NF, NF, True), (LATER_UP, None, False), (LATER_UP + FD, LATER_UP + FD, True),
+            (LATER_DOWN, None, False), (LATER_END, LATER_DOWN + FD, True),
+        ],
+        (NF, LATER_UP + FD, LATER_DOWN + FD),
+        before + 3.0,
     )
 
 
@@ -192,9 +207,9 @@
 
 
 def first_kernel(
-    inverse_hbm, coupling_hbm, interior_load_hbm, trace_load_hbm, shift_hbm, names_hbm, padding_hbm,
+    padding_ref, inverse_hbm, coupling_hbm, interior_load_hbm, trace_load_hbm, shift_hbm, names_hbm,
     living_ref, own_ref, on_ref, off_ref, solved_hbm,
-    solved_ref, inverse_ref, coupling_ref, interior_load_ref, trace_load_ref, shift_ref, names_ref, padding_ref, stage_ref, sems,
+    solved_ref, inverse_ref, coupling_ref, interior_load_ref, trace_load_ref, shift_ref, names_ref, stage_ref, sems,
 ):
     rows = NI // PARTS
     copies = [pltpu.make_async_copy(interior_load_hbm, interior_load_ref, sems.at[0])]
@@ -205,7 +220,7 @@
         )
     rest = [
         (coupling_hbm, coupling_ref), (names_hbm, names_ref),
-        (trace_load_hbm, trace_load_ref), (shift_hbm, shift_ref), (padding_hbm, padding_ref),
+        (trace_load_hbm, trace_load_ref), (shift_hbm, shift_ref),
     ]
     for place, (source, target) in enumerate(rest):
         copies.append(pltpu.make_async_copy(source, target, sems.at[1 + PARTS + place]))
@@ -214,8 +229,7 @@
     dom, sub = ids()
     for copy in copies[2 + PARTS :]:
         copy.wait()
-    padding = jnp.broadcast_to(padding_ref[:, :1], (1, LANES))
-    living = lane_iota(1) < LANES - padding
+    living = lane_iota(1) < LANES - padding_ref[0]
     living_ref[...] = jnp.broadcast_to(jnp.where(living, 1.0, 0.0), (8, LANES))
     stage_ref[NAMES:, :] = jnp.zeros((stage_ref.shape[0] - NAMES, LANES), F32)
     loads, load_exponent = coded(trace_load_ref[...])
@@ -235,7 +249,7 @@
         solved.append(matrix_times(inverse_ref.at[pl.ds(part * rows, rows)], load))
     solved = jnp.concatenate(solved, 0)
     solved_ref[...] = solved
-    keep = pltpu.make_async_copy(solved_ref, solved_hbm, sems.at[PARTS + 6])
+    keep = pltpu.make_async_copy(solved_ref, solved_hbm, sems.at[PARTS + 5])
     keep.start()
     copies[1 + PARTS].wait()
     whole, exponent = coded(jnp.where(living, transposed_times(coupling_ref, solved), 0.0))
@@ -370,10 +384,11 @@
         shifts_ref[pl.ds(j, FD, stride=4), :] = got[FD:]
 
 
-def put_terms(terms, names_ref, own_ref, on_ref, off_ref, stage_ref, dom):
+def put_terms(terms, base, names_ref, own_ref, on_ref, off_ref, stage_ref, dom):
     whole, exponent = coded(terms)
+    exponent = exponent + base
     stage_ref[:NF, :] = whole
-    stage_ref[NF:, :] = jnp.broadcast_to(exponent, (stage_ref.shape[0] - NF, LANES))
+    stage_ref[NF:, :] = jnp.broadcast_to(exponent + BIAS, (stage_ref.shape[0] - NF, LANES))
     own_ref[...] = as_sent(stage_ref[...])
     low, high = rim_lists(stage_ref, names_ref)
     put_lists(on_ref, off_ref, [high, spread_row(exponent)], [low, spread_row(exponent)], dom)
@@ -381,12 +396,13 @@
 
 def second_kernel(
     inverse_ref, coupling_ref, trace_ref, names_ref, living_ref, sent_ref,
-    chunk_ref, lane_ref, valid_ref, weight_ref, shifts_ref, view_ref, terms_ref, own_ref, on_ref, off_ref, inner_ref,
+    chunk_ref, lane_ref, valid_ref, weight_ref, shifts_ref, view_ref, terms_ref, own_ref, on_ref, off_ref, inner_ref, scale_ref,
     loads_ref, stage_ref, gathered_ref,
 ):
     dom, sub = ids()
     count = lax.axis_size("dom")
-    decode_first(sent_ref, gathered_ref)
+    base = decode_first(sent_ref, gathered_ref)
+    scale_ref[...] = jnp.broadcast_to(base, (8, LANES))
     chunk, lane = partner_places(names_ref, gathered_ref, sub)
     chunk, lane = twice(chunk), twice(lane)
     names = twice(names_ref[...])
@@ -410,26 +426,29 @@
 
     terms = element_operator(inverse_ref, coupling_ref, trace_ref, view, living_ref, keep)
     terms_ref[...] = terms
-    put_terms(terms, names_ref, own_ref, on_ref, off_ref, stage_ref, dom)
-
-
-def next_view(gathered_ref, chunk_ref, lane_ref, valid_ref, shifts_ref, view_ref, terms_ref):
+    put_terms(terms, base, names_ref, own_ref, on_ref, off_ref, stage_ref, dom)
+
+
+def next_view(factor, gathered_ref, chunk_ref, lane_ref, valid_ref, shifts_ref, view_ref, terms_ref):
     low_list = summed(gathered_ref, LATER_UP, LATER_UP + FD)
     high_list = summed(gathered_ref, LATER_DOWN, LATER_DOWN + FD)
     partner = partner_terms(gathered_ref, chunk_ref[...], lane_ref[...], low_list, high_list)
-    image = terms_ref[...] + partner + shifts_ref[...] * view_ref[...]
+    image = factor * (terms_ref[...] + shifts_ref[...] * view_ref[...]) + partner
     return jnp.where(six_times(valid_ref[...]) > 0.0, image, 0.0)
 
 
 def third_kernel(
     inverse_ref, coupling_ref, trace_ref, names_ref, living_ref, sent_ref,
-    chunk_ref, lane_ref, valid_ref, shifts_ref, view_ref, terms_ref, before_ref,
-    new_view_ref, new_terms_ref, own_ref, on_ref, off_ref, inner_ref,
+    chunk_ref, lane_ref, valid_ref, shifts_ref, view_ref, terms_ref, scale_ref, before_ref,
+    new_view_ref, new_terms_ref, own_ref, on_ref, off_ref, inner_ref, new_scale_ref,
     stage_ref, gathered_ref,
 ):
     dom, _ = ids()
-    decode_later(sent_ref, gathered_ref)
-    view = next_view(gathered_ref, chunk_ref, lane_ref, valid_ref, shifts_ref, view_ref, terms_ref)
+    scale = scale_ref[:1, :]
+    base = decode_later(sent_ref, gathered_ref, scale)
+    new_scale_ref[...] = jnp.where(row_iota(8) == 0, scale, base)
+    factor = jnp.exp2(scale - base)
+    view = next_view(factor, gathered_ref, chunk_ref, lane_ref, valid_ref, shifts_ref, view_ref, terms_ref)
     new_view_ref[...] = view
     inner_ref[0] = before_ref[...]
 
@@ -438,12 +457,12 @@
 
     terms = element_operator(inverse_ref, coupling_ref, trace_ref, view, living_ref, keep)
     new_terms_ref[...] = terms
-    put_terms(terms, names_ref, own_ref, on_ref, off_ref, stage_ref, dom)
+    put_terms(terms, base, names_ref, own_ref, on_ref, off_ref, stage_ref, dom)
 
 
 def fourth_kernel(
     inverse_ref, coupling_ref, trace_ref, living_ref, sent_ref,
-    chunk_ref, lane_ref, valid_ref, weight_ref, shifts_ref, first_view_ref, view_ref, terms_ref, before_ref,
+    chunk_ref, lane_ref, valid_ref, weight_ref, shifts_ref, first_view_ref, view_ref, terms_ref, scale_ref, before_ref,
     inner_hbm, sums_hbm,
     inner_ref, sums_ref, gathered_ref, sems,
 ):
@@ -457,18 +476,24 @@
         inner_ref[...] = inner
         copies[1].start()
 
-    decode_later(sent_ref, gathered_ref)
+    scales = [scale_ref[:1, :], scale_ref[1:2, :]]
+    scales.append(decode_later(sent_ref, gathered_ref, scales[1]))
+    factor = jnp.exp2(scales[1] - scales[2])
     first, second = first_view_ref[...], view_ref[...]
-    third = next_view(gathered_ref, chunk_ref, lane_ref, valid_ref, shifts_ref, view_ref, terms_ref)
+    third = next_view(factor, gathered_ref, chunk_ref, lane_ref, valid_ref, shifts_ref, view_ref, terms_ref)
     last = element_operator(inverse_ref, coupling_ref, trace_ref, third, living_ref, keep)
     weight = six_times(weight_ref[...])
     last = last + weight * (shifts_ref[...] * third)
     views = (first, second, third)
-    products = [weight * views[i] * views[j] for i in range(3) for j in range(i, 3)]
+    weighted = [weight * view for view in views]
+    products = [weighted[i] * views[j] for i in range(3) for j in range(i, 3)]
     products += [view * last for view in views]
+    powers = [scales[i] + scales[j] for i in range(3) for j in range(i, 3)]
+    powers += [scale + scales[2] for scale in scales]
     lane = lane_iota(1)
     sums = jnp.zeros((1, LANES), F32)
     for place, product in enumerate(products):
+        sums = sums + jnp.where(lane == SCALE_LANE + place, powers[place], 0.0)
         total = product.reshape(6, 8, LANES).sum(0).sum(0, keepdims=True).sum(1, keepdims=True)
         sums = sums + jnp.where(lane == place, total, 0.0)
     sums_ref[...] = jnp.broadcast_to(sums, sums_ref.shape)
@@ -493,9 +518,9 @@
     ]
     for copy in copies:
         copy.start()
-    decode_first(first_sent_ref, first_ref)
-    decode_later(second_sent_ref, second_ref)
-    decode_later(third_sent_ref, third_ref)
+    scales = [decode_first(first_sent_ref, first_ref)]
+    scales.append(decode_later(second_sent_ref, second_ref, scales[0]))
+    scales.append(decode_later(third_sent_ref, third_ref, scales[1]))
     _, sub = ids()
     wanted = lax.broadcasted_iota(jnp.int32, (2 * RIM, LANES), 0) + (RIM + 2 * RIM * sub)
     sources = (first_ref, second_ref, third_ref)
@@ -530,27 +555,29 @@
         )
         total = total + down
         if v == 0:
-            current = total + trace_load_ref[...]
+            current = total + jnp.exp2(-scales[0][:, :1]) * trace_load_ref[...]
         else:
-            current = total + shift_ref[...] * current
+            factor = jnp.exp2(scales[v - 1] - scales[v])[:, :1]
+            current = total + factor * (shift_ref[...] * current)
         owned_ref[v] = current
 
 
-def coefficients(sums):
+def coefficients(sums, powers, own_powers):
     lane = lane_iota(1)
 
-    def entry(place):
-        return jnp.where(lane == place, sums, 0.0).sum(1, keepdims=True)
-
+    def entry(row, place):
+        return jnp.where(lane == place, row, 0.0).sum(1, keepdims=True)
+
+    pairs = [(i, j) for i in range(3) for j in range(i, 3)]
+    pairs += [(i, 3) for i in range(3)]
+    places = [pairs.index((i, i)) for i in range(3)]
+    scales = [0.5 * entry(powers, place) for place in places]
+    own_scales = [0.5 * entry(own_powers, place) for place in places]
     table = {}
-    place = 0
-    for i in range(3):
-        for j in range(i, 3):
-            table[i, j] = table[j, i] = entry(place)
-            place += 1
-    for i in range(3):
-        table[i, 3] = entry(place)
-        place += 1
+    for place, (i, j) in enumerate(pairs):
+        power = entry(powers, place) - scales[i] - scales[min(j, 2)]
+        table[i, j] = table[j, i] = entry(sums, place) * jnp.exp2(power)
+    steps = [jnp.exp2(scales[1] - scales[0]), jnp.exp2(scales[2] - scales[1]), 1.0]
 
     def form(left, right):
         total = None
@@ -577,7 +604,7 @@
     residual, direction, result = [one], [one], []
     norm = table[0, 0]
     for iteration in range(3):
-        image = [None] + direction
+        image = [None] + [a * b for a, b in zip(direction, steps, strict=False)]
         step = norm / form(direction, image)
         result = combine(result, step, direction)
         if iteration < 2:
@@ -585,15 +612,25 @@
             new_norm = form(residual, residual)
             direction = combine(residual, new_norm / norm, direction)
             norm = new_norm
-    return result
+    return [
+        part * jnp.exp2(scales[0] - scale + own)
+        for part, scale, own in zip(result, scales, own_scales, strict=True)
+    ]
 
 
 def last_kernel(
     living_ref, all_sums_ref, inner_ref, owned_ref,
     traces_ref, interior_ref,
 ):
-    sums = all_sums_ref[...].reshape(-1, 8, LANES).sum(0).sum(0, keepdims=True)
-    a, b, c = coefficients(sums)
+    dom, sub = ids()
+    sums = all_sums_ref[...]
+    powers = pltpu.roll(sums, LANES - SCALE_LANE, 1)
+    own = pltpu.roll(all_sums_ref[pl.ds(dom * SUB + sub, 1), :], LANES - SCALE_LANE, 1)
+    used = lane_iota(1) < SCALE_LANE
+    powers, own = jnp.where(used, powers, 0.0), jnp.where(used, own, 0.0)
+    top = powers.reshape(-1, 8, LANES).max(0).max(0, keepdims=True)
+    sums = (sums * jnp.exp2(powers - top)).reshape(-1, 8, LANES).sum(0).sum(0, keepdims=True)
+    a, b, c = coefficients(sums, top, own)
     traces_ref[...] = a * owned_ref[0] + b * owned_ref[1] + c * owned_ref[2]
     lifted = a * inner_ref[1] + b * inner_ref[2] + c * inner_ref[3]
     living = jnp.broadcast_to(living_ref[:1, :], (NI, LANES)) > 0.0
@@ -607,7 +644,8 @@
         kernel,
         out_shape=[jax.ShapeDtypeStruct(s, d) for s, d in outputs]
         + [pltpu.HBM(s, d) for s, d in to_hbm],
-        in_specs=[near] * len(inputs) + [far] * len(held),
+        in_specs=[near if x.ndim > 1 else pl.BlockSpec(memory_space=pltpu.SMEM) for x in inputs]
+        + [far] * len(held),
         out_specs=[near] * len(outputs) + [far] * len(to_hbm),
         scratch_shapes=list(scratch),
         compiler_params=pltpu.CompilerParams(vmem_limit_bytes=limit * MIB),
@@ -651,33 +689,30 @@
     living, own, on, off, solved = call(
         first_kernel,
         [rows8, ((112, LANES), I16), ((32, LANES), I16), ((32, LANES), I16)],
-        [],
-        from_hbm=[
-            interior_inverse, coupling, interior_load, trace_load, face_shift, element_faces,
-            jnp.pad(block_padding, (0, LANES - 1))[None],
-        ],
+        [block_padding],
+        from_hbm=[interior_inverse, coupling, interior_load, trace_load, face_shift, element_faces],
         to_hbm=[inner],
         scratch=[
             pltpu.VMEM((NI, LANES), F32), pltpu.VMEM((NI, NI, LANES), BF16), pltpu.VMEM((NI, NF, LANES), BF16),
             pltpu.VMEM((NI, LANES), BF16), pltpu.VMEM((FD, 2 * RIM), F32), pltpu.VMEM((FD, 2 * RIM), F32),
-            pltpu.VMEM((4, LANES), jnp.int32), pltpu.VMEM((1, LANES), jnp.int32), pltpu.VMEM((112, LANES), F32),
-            pltpu.SemaphoreType.DMA((PARTS + 7,)),
+            pltpu.VMEM((4, LANES), jnp.int32), pltpu.VMEM((112, LANES), F32),
+            pltpu.SemaphoreType.DMA((PARTS + 6,)),
         ],
         limit=10,
     )
     from_below, from_above = neighbours(on, off)
     first = to_all([own[:UP], from_below[: DOWN - UP], from_above[: FD + 1]], FIRST_ROWS)
-    chunk, lane, valid, weight, shifts, view0, terms, own, on, off, kept = call(
+    chunk, lane, valid, weight, shifts, view0, terms, own, on, off, kept, scale = call(
         second_kernel,
-        [places, places, rows8, rows8, slab, slab, slab, *sent, inner],
+        [places, places, rows8, rows8, slab, slab, slab, *sent, inner, rows8],
         [*matrices, element_faces, living, first],
         scratch=[pltpu.VMEM((NF, LANES), F32), stage, decoded_first],
     )
     second = later(own, on, off)
-    view1, terms1, own, on, off, kept = call(
+    view1, terms1, own, on, off, kept, scale = call(
         third_kernel,
-        [slab, slab, *sent, ((2, NI, LANES), F32)],
-        [*matrices, element_faces, living, second, chunk, lane, valid, shifts, view0, terms, kept],
+        [slab, slab, *sent, ((2, NI, LANES), F32), rows8],
+        [*matrices, element_faces, living, second, chunk, lane, valid, shifts, view0, terms, scale, kept],
         scratch=[stage, decoded],
     )
     third = later(own, on, off)
@@ -685,7 +720,7 @@
     kept, sums = call(
         fourth_kernel,
         [],
-        [*matrices, living, third, chunk, lane, valid, weight, shifts, view0, view1, terms1, kept],
+        [*matrices, living, third, chunk, lane, valid, weight, shifts, view0, view1, terms1, scale, kept],
         to_hbm=[((3, NI, LANES), F32), ((everyone, LANES), F32)],
         scratch=[
             pltpu.VMEM((NI, LANES), F32), pltpu.VMEM((everyone, LANES), F32), decoded,

time: 97.8 us -> 97.6 us (level)
  no operation moved by 1% of the time
where the time goes in v3:
time: 97.6 us; the launch traced here: 97.1 us
  blocking collectives  42 us (43%)
  starting transfers between devices  25.8 us (26%)
  waiting for transfers between devices  13.1 us (13%)
  Pallas kernels  12.3 us (13%)
  local copies, waits for them, and re-layouts  2.1 us (2%)
  between operations  1.54 us (2%)
    all_to_all x3, blocking collectives, to_all(): return lax.all_to_all(copies, 'sub', 0, 0, tiled=True)  42 us
    ppermute x3, starting transfers between devices, neighbours(): from_off = lax.ppermute(off, 'dom', pairs + [(j, i) for i, j in pairs])  13.5 us
    pallas_call x6, Pallas kernels, call(): pl.pallas_call(kernel, out_shape=[jax.ShapeDtypeStruct(s, d) for s, d in...  12.3 us
    all_to_all x1, starting transfers between devices, on_device(): all_sums = lax.all_to_all(sums, ('dom', 'sub'), 0, 0, tiled=True)  11.2 us
    all_to_all x1, waiting for transfers between devices, on_device(): all_sums = lax.all_to_all(sums, ('dom', 'sub'), 0, 0, tiled=True)  8.87 us
    ppermute x3, waiting for transfers between devices, neighbours(): from_off = lax.ppermute(off, 'dom', pairs + [(j, i) for i, j in pairs])  4.22 us
  transfers between devices with their start and end apart: 7, of which 4 were waited for; matrix products, arithmetic and copies ran while one was open for 0% of the time, Pallas kernels for 2%

profile of v3, /device:TPU:1, one launch (start us, length us, event | category | flops | bytes accessed | tf_op | source)
XLA Modules:
  0.0 97.1 jit_solution(2497821079924860331)
XLA Ops:
  1.3 0.0 copy-start
  1.3 2.9 %shard_map.95 = (f32[8,128]{1,0:T(8,128)S(1)}, s16[112,128]{1,0:T(8,128)(2,1)S(1)}, s16[32,128]{1,0:T(8,128)(2,1)S(1)}, s16[32,128]{1,0:T(8,128)(2,1)S(1)}, f32[80,128]{1,0:T(8,128)}) custom-call(s32[1]{0:T(128)S(6)} %copy.11.padding_ref, bf16[80,80,128]{2,1,0:T(8,128)(2,1)} %inverse_ref.5, bf16[80,48,128]{2,1,0:T(8,128)(2,1)} %coupling_ref.5, ...), custom_call_target="tpu_custom_call" | custom-call | tf_op jit(solution)/shard_map/pallas_call | solution.py:643
  4.2 4.5 %collective-permute-start = (s16[32,128]{1,0:T(8,128)(2,1)S(1)}, s16[32,128]{1,0:T(8,128)(2,1)S(1)}, u32[]{:S(2)}, u32[]{:S(2)}) collective-permute-start(s16[32,128]{1,0:T(8,128)(2,1)S(1)} %get-tuple-element.32), channel_id=1, source_target_pairs={{8,16},{24,32},{40,48},{56,64},{72,80},{88,96},{104,112},{120,128}... | collective-permute-start | bytes 24584 | tf_op jit(solution)/shard_map/ppermute | solution.py:665
  8.7 0.1 collective-permute-start.1
  8.9 0.1 pad.11.clone
  9.0 1.1 %collective-permute-done = s16[32,128]{1,0:T(8,128)(2,1)S(1)} collective-permute-done((s16[32,128]{1,0:T(8,128)(2,1)S(1)}, s16[32,128]{1,0:T(8,128)(2,1)S(1)}, u32[]{:S(2)}, u32[]{:S(2)}) %collective-permute-start) | collective-permute-done | bytes 8224 | tf_op jit(solution)/shard_map/ppermute | solution.py:665
  10.1 0.0 collective-permute-done.1
  10.1 0.1 add_add_fusion
  10.2 20.7 %all_to_all.26.sent_ref.first_sent_ref = s16[8,144,128]{2,1,0:T(8,128)(2,1)S(1)} all-to-all(s16[8,144,128]{2,1,0:T(8,128)(2,1)S(1)} %broadcast_in_dim.9), channel_id=1, replica_groups=mesh['dom'=32,'sub'=8] {'sub'}, dimensions={0} | all-to-all | bytes 589824 | tf_op jit(solution)/shard_map/all_to_all | solution.py:659
  30.9 2.4 %shard_map.96 = (s32[8,128]{1,0:T(8,128)S(1)}, s32[8,128]{1,0:T(8,128)S(1)}, f32[8,128]{1,0:T(8,128)S(1)}, f32[8,128]{1,0:T(8,128)S(1)}, f32[48,128]{1,0:T(8,128...) custom-call(bf16[80,80,128]{2,1,0:T(8,128)(2,1)S(1)} %copy-done, ...), custom_call_target="tpu_custom_call" | custom-call | tf_op jit(solution)/shard_map/pallas_call | solution.py:643
  33.3 0.9 collective-permute-start.3
  34.3 3.2 %collective-permute-start.2 = (s16[16,128]{1,0:T(8,128)(2,1)S(1)}, s16[16,128]{1,0:T(8,128)(2,1)S(1)}, u32[]{:S(2)}, u32[]{:S(2)}) collective-permute-start(s16[16,128]{1,0:T(8,128)(2,1)S(1)} %get-tuple-element.35), channel_id=1, source_target_pairs={{8,16},{24,32},{40,48},{56,64},{72,80},{88,96},{104,112},{120,128}... | collective-permute-start | bytes 12296 | tf_op jit(solution)/shard_map/ppermute | solution.py:665
  37.5 0.1 pad.7.clone
  37.6 0.0 collective-permute-done.3
  37.6 1.6 %collective-permute-done.2 = s16[16,128]{1,0:T(8,128)(2,1)S(1)} collective-permute-done((s16[16,128]{1,0:T(8,128)(2,1)S(1)}, s16[16,128]{1,0:T(8,128)(2,1)S(1)}, u32[]{:S(2)}, u32[]{:S(2)}) %collective-permute-start.2) | collective-permute-done | bytes 4128 | tf_op jit(solution)/shard_map/ppermute | solution.py:665
  39.2 0.1 add_add_fusion.1
  39.3 10.7 %all_to_all.27.sent_ref.second_sent_ref = s16[8,80,128]{2,1,0:T(8,128)(2,1)S(1)} all-to-all(s16[8,80,128]{2,1,0:T(8,128)(2,1)S(1)} %broadcast_in_dim.10), channel_id=1, replica_groups=mesh['dom'=32,'sub'=8] {'sub'}, dimensions={0} | all-to-all | bytes 327680 | tf_op jit(solution)/shard_map/all_to_all | solution.py:659
  50.0 1.6 %shard_map.97 = (f32[48,128]{1,0:T(8,128)S(1)}, f32[48,128]{1,0:T(8,128)S(1)}, s16[64,128]{1,0:T(8,128)(2,1)S(1)}, s16[16,128]{1,0:T(8,128)(2,1)S(1)}, s16[16,12...) custom-call(bf16[80,80,128]{2,1,0:T(8,128)(2,1)S(1)} %copy-done, ...), custom_call_target="tpu_custom_call" | custom-call | tf_op jit(solution)/shard_map/pallas_call | solution.py:643
  51.6 0.1 collective-permute-start.5
  51.7 5.7 %collective-permute-start.4 = (s16[16,128]{1,0:T(8,128)(2,1)S(1)}, s16[16,128]{1,0:T(8,128)(2,1)S(1)}, u32[]{:S(2)}, u32[]{:S(2)}) collective-permute-start(s16[16,128]{1,0:T(8,128)(2,1)S(1)} %get-tuple-element.46), channel_id=1, source_target_pairs={{8,16},{24,32},{40,48},{56,64},{72,80},{88,96},{104,112},{120,128}... | collective-permute-start | bytes 12296 | tf_op jit(solution)/shard_map/ppermute | solution.py:665
  57.4 0.0 collective-permute-done.5
  57.4 1.5 %collective-permute-done.4 = s16[16,128]{1,0:T(8,128)(2,1)S(1)} collective-permute-done((s16[16,128]{1,0:T(8,128)(2,1)S(1)}, s16[16,128]{1,0:T(8,128)(2,1)S(1)}, u32[]{:S(2)}, u32[]{:S(2)}) %collective-permute-start.4) | collective-permute-done | bytes 4128 | tf_op jit(solution)/shard_map/ppermute | solution.py:665
  59.0 0.1 add_add_fusion.2
  59.1 10.7 %all_to_all.28.sent_ref.third_sent_ref = s16[8,80,128]{2,1,0:T(8,128)(2,1)S(1)} all-to-all(s16[8,80,128]{2,1,0:T(8,128)(2,1)S(1)} %broadcast_in_dim.11), channel_id=1, replica_groups=mesh['dom'=32,'sub'=8] {'sub'}, dimensions={0} | all-to-all | bytes 327680 | tf_op jit(solution)/shard_map/all_to_all | solution.py:659
  69.8 2.1 %shard_map.98 = (f32[3,80,128]{2,1,0:T(8,128)}, f32[256,128]{1,0:T(8,128)}) custom-call(bf16[80,80,128]{2,1,0:T(8,128)(2,1)S(1)} %copy-done, bf16[80,48,128]{2,1,0:T(8,128)(2,1)S(1)} %copy-done.1, bf16[48,48,128]{2,1,0:T(8,128)(2,1)S(1)} %copy-done.2, f32[8,128]{1,0:T(8,128)S(1)} %get-tuple-element.30.living_ref, ...), custom_call_target="tpu_custom_call" | custom-call | tf_op jit(solution)/shard_map/pallas_call | solution.py:643
  71.9 11.2 %all-to-all-start.3 = ((f32[256,1,128]{2,1,0:T(1,128)}), f32[256,1,128]{2,1,0:T(1,128)S(1)}, u32[]{:S(2)}, u32[]{:S(2)}) async-start(f32[256,1,128]{2,1,0:T(1,128)} %bitcast.5), calls=%async_computation.3 | async-start | bytes 262144 | tf_op jit(solution)/shard_map/all_to_all | solution.py:730
  83.1 0.0 copy-start.4
  83.1 0.9 copy-done.4
  84.0 0.9 copy-done.6
  84.9 2.3 %shard_map.99 = (f32[3,12,256]{2,1,0:T(8,128)S(1)}, f32[4,80,128]{2,1,0:T(8,128)S(1)}) custom-call(s16[8,144,128]{2,1,0:T(8,128)(2,1)S(1)} %all_to_all.26.sent_ref.first_sent_ref, s16[8,80,128]{2,1,0:T(8,128)(2,1)S(1)} %copy-done.6, s16[8,80,128]{2,1,0:T(8,128)(2,1)S(1)} %copy-done.4, f32[12,256]{1,0:T(8,128)} %trace_load_hbm.3, f32[12,256]{1,0:T(8,128)} %shift_hbm.3, ...), custom_call_target="tpu_custom_call" | custom-call | tf_op jit(solution)/shard_map/pallas_call | solution.py:643
  87.2 8.9 %all-to-all-done.3 = f32[256,1,128]{2,1,0:T(1,128)S(1)} async-done(((f32[256,1,128]{2,1,0:T(1,128)}), f32[256,1,128]{2,1,0:T(1,128)S(1)}, u32[]{:S(2)}, u32[]{:S(2)}) %all-to-all-start.3) | async-done | bytes 131104 | tf_op jit(solution)/shard_map/all_to_all | solution.py:730
  96.1 1.0 shard_map.100
  (24 shorter events, 0.1 us)
Async XLA Ops:
  1.3 29.6 %copy-start = (bf16[80,80,128]{2,1,0:T(8,128)(2,1)S(1)}, bf16[80,80,128]{2,1,0:T(8,128)(2,1)}, u32[]{:S(2)}) copy-start(bf16[80,80,128]{2,1,0:T(8,128)(2,1)} %inverse_ref.5) | copy-start | bytes 4915204
  1.3 29.6 %copy-start.1 = (bf16[80,48,128]{2,1,0:T(8,128)(2,1)S(1)}, bf16[80,48,128]{2,1,0:T(8,128)(2,1)}, u32[]{:S(2)}) copy-start(bf16[80,48,128]{2,1,0:T(8,128)(2,1)} %coupling_ref.5) | copy-start | bytes 2949124
  1.3 29.6 %copy-start.2 = (bf16[48,48,128]{2,1,0:T(8,128)(2,1)S(1)}, bf16[48,48,128]{2,1,0:T(8,128)(2,1)}, u32[]{:S(2)}) copy-start(bf16[48,48,128]{2,1,0:T(8,128)(2,1)} %trace_ref.5) | copy-start | bytes 1769476
  1.3 29.6 %copy-start.7 = (s32[4,128]{1,0:T(4,128)S(1)}, s32[4,128]{1,0:T(4,128)}, u32[]{:S(2)}) copy-start(s32[4,128]{1,0:T(4,128)} %names_ref.3) | copy-start | bytes 6148
  4.2 5.8 %collective-permute-start = (s16[32,128]{1,0:T(8,128)(2,1)S(1)}, s16[32,128]{1,0:T(8,128)(2,1)S(1)}, u32[]{:S(2)}, u32[]{:S(2)}) collective-permute-start(s16[32,128]{1,0:T(8,128)(2,1)S(1)} %get-tuple-element.32), channel_id=1, source_target_pairs={{8,16},{24,32},{40,48},{56,64},{72,80},{88,96},{104,112},{120,128}... | collective-permute-start | bytes 24584 | tf_op jit(solution)/shard_map/ppermute | solution.py:665
  8.7 1.3 %collective-permute-start.1 = (s16[32,128]{1,0:T(8,128)(2,1)S(1)}, s16[32,128]{1,0:T(8,128)(2,1)S(1)}, u32[]{:S(2)}, u32[]{:S(2)}) collective-permute-start(s16[32,128]{1,0:T(8,128)(2,1)S(1)} %get-tuple-element.33), channel_id=1, source_target_pairs={{0,8},{8,0},{16,24},{24,16},{32,40},{40,32},{48,56},{56,48},{64,72... | collective-permute-start | bytes 24584 | tf_op jit(solution)/shard_map/ppermute | solution.py:666
  33.3 4.3 %collective-permute-start.3 = (s16[16,128]{1,0:T(8,128)(2,1)S(1)}, s16[16,128]{1,0:T(8,128)(2,1)S(1)}, u32[]{:S(2)}, u32[]{:S(2)}) collective-permute-start(s16[16,128]{1,0:T(8,128)(2,1)S(1)} %get-tuple-element.36), channel_id=1, source_target_pairs={{0,8},{8,0},{16,24},{24,16},{32,40},{40,32},{48,56},{56,48},{64,72... | collective-permute-start | bytes 12296 | tf_op jit(solution)/shard_map/ppermute | solution.py:666
  34.3 4.9 %collective-permute-start.2 = (s16[16,128]{1,0:T(8,128)(2,1)S(1)}, s16[16,128]{1,0:T(8,128)(2,1)S(1)}, u32[]{:S(2)}, u32[]{:S(2)}) collective-permute-start(s16[16,128]{1,0:T(8,128)(2,1)S(1)} %get-tuple-element.35), channel_id=1, source_target_pairs={{8,16},{24,32},{40,48},{56,64},{72,80},{88,96},{104,112},{120,128}... | collective-permute-start | bytes 12296 | tf_op jit(solution)/shard_map/ppermute | solution.py:665
  50.0 1.6 %copy-start.5 = (s16[8,80,128]{2,1,0:T(8,128)(2,1)}, s16[8,80,128]{2,1,0:T(8,128)(2,1)S(1)}, u32[]{:S(2)}) copy-start(s16[8,80,128]{2,1,0:T(8,128)(2,1)S(1)} %all_to_all.27.sent_ref.second_sent_ref) | copy-start | bytes 491524
  51.6 5.8 %collective-permute-start.5 = (s16[16,128]{1,0:T(8,128)(2,1)S(1)}, s16[16,128]{1,0:T(8,128)(2,1)S(1)}, u32[]{:S(2)}, u32[]{:S(2)}) collective-permute-start(s16[16,128]{1,0:T(8,128)(2,1)S(1)} %get-tuple-element.47), channel_id=1, source_target_pairs={{0,8},{8,0},{16,24},{24,16},{32,40},{40,32},{48,56},{56,48},{64,72... | collective-permute-start | bytes 12296 | tf_op jit(solution)/shard_map/ppermute | solution.py:666
  51.7 7.3 %collective-permute-start.4 = (s16[16,128]{1,0:T(8,128)(2,1)S(1)}, s16[16,128]{1,0:T(8,128)(2,1)S(1)}, u32[]{:S(2)}, u32[]{:S(2)}) collective-permute-start(s16[16,128]{1,0:T(8,128)(2,1)S(1)} %get-tuple-element.46), channel_id=1, source_target_pairs={{8,16},{24,32},{40,48},{56,64},{72,80},{88,96},{104,112},{120,128}... | collective-permute-start | bytes 12296 | tf_op jit(solution)/shard_map/ppermute | solution.py:665
  69.8 2.1 %copy-start.3 = (s16[8,80,128]{2,1,0:T(8,128)(2,1)}, s16[8,80,128]{2,1,0:T(8,128)(2,1)S(1)}, u32[]{:S(2)}) copy-start(s16[8,80,128]{2,1,0:T(8,128)(2,1)S(1)} %all_to_all.28.sent_ref.third_sent_ref) | copy-start | bytes 491524
  71.9 24.2 %all-to-all-start.3 = ((f32[256,1,128]{2,1,0:T(1,128)}), f32[256,1,128]{2,1,0:T(1,128)S(1)}, u32[]{:S(2)}, u32[]{:S(2)}) async-start(f32[256,1,128]{2,1,0:T(1,128)} %bitcast.5), calls=%async_computation.3 | async-start | bytes 262144 | tf_op jit(solution)/shard_map/all_to_all | solution.py:730
  83.1 0.9 copy-start.4
  84.0 0.9 copy-start.6

commit v4 on v3

--- a/solution.py
+++ b/solution.py
@@ -23,10 +23,8 @@
 
 BIAS = 16384.0
 SCALE_LANE = 64
-PUSHED, LOADS, SHIFTS, NAMES, SCALES, UP, UP_SHIFT, DOWN, FIRST_END, FIRST_ROWS = (
-    0, 48, 72, 96, 100, 103, 116, 129, 142, 144,
-)
-LATER_UP, LATER_DOWN, LATER_END, LATER_ROWS = 49, 62, 75, 80
+FACES, NAMES, SCALES, UP, UP_SHIFT, DOWN, FIRST_ROWS = 48, 96, 100, 105, 118, 131, 144
+LATER_UP, LATER_DOWN, LATER_ROWS = 54, 67, 80
 
 
 def row_iota(rows):
@@ -137,9 +135,10 @@
         sent_ref,
         terms_ref,
         [
-            (LOADS, SCALES, True), (SHIFTS, SCALES + 1, True), (NAMES, SCALES + 2, False), (UP, None, False),
+            (FACES, SCALES, True), (FACES + FD, SCALES + 1, True), (FACES + 2 * FD, SCALES + 2, False),
+            (FACES + 3 * FD, SCALES + 1, True), (NAMES, SCALES + 2, False), (UP, None, False),
             (UP + FD, UP + FD, True), (UP_SHIFT, None, False), (UP_SHIFT + FD, UP_SHIFT + FD, False),
-            (DOWN, None, False), (FIRST_END, DOWN + FD, True),
+            (DOWN, None, False), (FIRST_ROWS, DOWN + FD, True),
         ],
         (SCALES, SCALES + 1, UP + FD, DOWN + FD),
     )
@@ -151,7 +150,7 @@
         terms_ref,
         [
             (NF, NF, True), (LATER_UP, None, False), (LATER_UP + FD, LATER_UP + FD, True),
-            (LATER_DOWN, None, False), (LATER_END, LATER_DOWN + FD, True),
+            (LATER_DOWN, None, False), (LATER_ROWS, LATER_DOWN + FD, True),
         ],
         (NF, LATER_UP + FD, LATER_DOWN + FD),
         before + 3.0,
@@ -224,7 +223,7 @@
     ]
     for place, (source, target) in enumerate(rest):
         copies.append(pltpu.make_async_copy(source, target, sems.at[1 + PARTS + place]))
-    for copy in copies:
+    for copy in [copies[0], copies[1 + PARTS], *copies[2 + PARTS :], *copies[1 : 1 + PARTS]]:
         copy.start()
     dom, sub = ids()
     for copy in copies[2 + PARTS :]:
@@ -236,8 +235,9 @@
     shifts, shift_exponent = coded(shift_ref[...])
     for half in range(2):
         columns = slice(half * RIM, half * RIM + RIM)
-        stage_ref[LOADS + FD * half : LOADS + FD * half + FD, :] = loads[:, columns]
-        stage_ref[SHIFTS + FD * half : SHIFTS + FD * half + FD, :] = shifts[:, columns]
+        first = FACES + 2 * FD * half
+        stage_ref[first : first + FD, :] = loads[:, columns]
+        stage_ref[first + FD : first + 2 * FD, :] = shifts[:, columns]
     stage_ref[NAMES : NAMES + 4, :] = names_ref[...].astype(F32)
     stage_ref[SCALES + 1 : SCALES + 2, :] = spread_row(load_exponent)
     stage_ref[SCALES + 2 : SCALES + 3, :] = spread_row(shift_exponent)
@@ -372,13 +372,8 @@
         got = jnp.where(high == 0, take_lanes(up_list, low), 0.0)
         for s in range(SUB):
             for half in range(2):
-                source = jnp.concatenate(
-                    [
-                        gathered_ref[s, LOADS + 12 * half : LOADS + 12 * half + 12, :],
-                        gathered_ref[s, SHIFTS + 12 * half : SHIFTS + 12 * half + 12, :],
-                    ],
-                    0,
-                )
+                first = FACES + 2 * FD * half
+                source = gathered_ref[s, first : first + 2 * FD, :]
                 got = jnp.where(high == 2 * s + half + 1, take_lanes(source, low), got)
         loads_ref[pl.ds(j, FD, stride=4), :] = got[:FD]
         shifts_ref[pl.ds(j, FD, stride=4), :] = got[FD:]
@@ -396,7 +391,7 @@
 
 def second_kernel(
     inverse_ref, coupling_ref, trace_ref, names_ref, living_ref, sent_ref,
-    chunk_ref, lane_ref, valid_ref, weight_ref, shifts_ref, view_ref, terms_ref, own_ref, on_ref, off_ref, inner_ref, scale_ref,
+    chunk_ref, lane_ref, valid_ref, weight_ref, shifts_ref, view_ref, terms_ref, inner_ref, scale_ref, own_ref, on_ref, off_ref,
     loads_ref, stage_ref, gathered_ref,
 ):
     dom, sub = ids()
@@ -440,7 +435,7 @@
 def third_kernel(
     inverse_ref, coupling_ref, trace_ref, names_ref, living_ref, sent_ref,
     chunk_ref, lane_ref, valid_ref, shifts_ref, view_ref, terms_ref, scale_ref, before_ref,
-    new_view_ref, new_terms_ref, own_ref, on_ref, off_ref, inner_ref, new_scale_ref,
+    new_view_ref, new_terms_ref, inner_ref, new_scale_ref, own_ref, on_ref, off_ref,
     stage_ref, gathered_ref,
 ):
     dom, _ = ids()
@@ -652,9 +647,8 @@
     )(*inputs, *held)
 
 
-def to_all(blocks, rows):
-    rest = rows - sum(len(block) for block in blocks)
-    value = jnp.concatenate(blocks + [jnp.zeros((rest, LANES), I16)], 0)
+def to_all(blocks):
+    value = jnp.concatenate(blocks, 0)
     copies = jnp.broadcast_to(value[None], (SUB,) + value.shape)
     return lax.all_to_all(copies, "sub", 0, 0, tiled=True)
 
@@ -670,7 +664,7 @@
 
 def later(own, on, off):
     from_below, from_above = neighbours(on, off)
-    return to_all([own[:LATER_UP], from_below[: FD + 1], from_above[: FD + 1]], LATER_ROWS)
+    return to_all([own[:LATER_UP], from_below[: FD + 1], from_above[: FD + 1]])
 
 
 def on_device(
@@ -700,18 +694,19 @@
         ],
         limit=10,
     )
+    *matrices, own = lax.optimization_barrier((*matrices, own))
     from_below, from_above = neighbours(on, off)
-    first = to_all([own[:UP], from_below[: DOWN - UP], from_above[: FD + 1]], FIRST_ROWS)
-    chunk, lane, valid, weight, shifts, view0, terms, own, on, off, kept, scale = call(
+    first = to_all([own[:UP], from_below[: DOWN - UP], from_above[: FIRST_ROWS - DOWN]])
+    chunk, lane, valid, weight, shifts, view0, terms, kept, scale, own, on, off = call(
         second_kernel,
-        [places, places, rows8, rows8, slab, slab, slab, *sent, inner, rows8],
+        [places, places, rows8, rows8, slab, slab, slab, inner, rows8, *sent],
         [*matrices, element_faces, living, first],
         scratch=[pltpu.VMEM((NF, LANES), F32), stage, decoded_first],
     )
     second = later(own, on, off)
-    view1, terms1, own, on, off, kept, scale = call(
+    view1, terms1, kept, scale, own, on, off = call(
         third_kernel,
-        [slab, slab, *sent, ((2, NI, LANES), F32), rows8],
+        [slab, slab, ((2, NI, LANES), F32), rows8, *sent],
         [*matrices, element_faces, living, second, chunk, lane, valid, shifts, view0, terms, scale, kept],
         scratch=[stage, decoded],
     )

time: 97.6 us -> 97 us (level)
  no operation moved by 1% of the time
where the time goes in v4:
time: 97 us; the launch traced here: 96.6 us
  blocking collectives  42 us (43%)
  starting transfers between devices  25.8 us (27%)
  waiting for transfers between devices  13.3 us (14%)
  Pallas kernels  12 us (12%)
  local copies, waits for them, and re-layouts  1.94 us (2%)
  between operations  1.53 us (2%)
    all_to_all x3, blocking collectives, to_all(): return lax.all_to_all(copies, 'sub', 0, 0, tiled=True)  42 us
    ppermute x3, starting transfers between devices, neighbours(): from_off = lax.ppermute(off, 'dom', pairs + [(j, i) for i, j in pairs])  13.5 us
    pallas_call x6, Pallas kernels, call(): pl.pallas_call(kernel, out_shape=[jax.ShapeDtypeStruct(s, d) for s, d in...  12 us
    all_to_all x1, starting transfers between devices, on_device(): all_sums = lax.all_to_all(sums, ('dom', 'sub'), 0, 0, tiled=True)  11.2 us
    all_to_all x1, waiting for transfers between devices, on_device(): all_sums = lax.all_to_all(sums, ('dom', 'sub'), 0, 0, tiled=True)  8.88 us
    ppermute x3, waiting for transfers between devices, neighbours(): from_off = lax.ppermute(off, 'dom', pairs + [(j, i) for i, j in pairs])  4.39 us
  transfers between devices with their start and end apart: 7, of which 4 were waited for; matrix products, arithmetic and copies ran while one was open for 0% of the time, Pallas kernels for 2%

profile of v4, /device:TPU:1, one launch (start us, length us, event | category | flops | bytes accessed | tf_op | source)
XLA Modules:
  0.0 96.6 jit_solution(7630511186057134702)
XLA Ops:
  1.3 0.0 copy-start
  1.3 0.0 copy-start.1
  1.3 0.0 copy-start.2
  1.3 0.0 copy-start.7
  1.3 2.7 %shard_map.95 = (f32[8,128]{1,0:T(8,128)S(1)}, s16[112,128]{1,0:T(8,128)(2,1)S(1)}, s16[32,128]{1,0:T(8,128)(2,1)S(1)}, s16[32,128]{1,0:T(8,128)(2,1)S(1)}, f32[80,128]{1,0:T(8,128)}) custom-call(s32[1]{0:T(128)S(6)} %copy.11.padding_ref, bf16[80,80,128]{2,1,0:T(8,128)(2,1)} %inverse_ref.2, bf16[80,48,128]{2,1,0:T(8,128)(2,1)} %coupling_ref.2, ...), custom_call_target="tpu_custom_call" | custom-call | tf_op jit(solution)/shard_map/pallas_call | solution.py:638
  4.0 4.5 %collective-permute-start = (s16[32,128]{1,0:T(8,128)(2,1)S(1)}, s16[32,128]{1,0:T(8,128)(2,1)S(1)}, u32[]{:S(2)}, u32[]{:S(2)}) collective-permute-start(s16[32,128]{1,0:T(8,128)(2,1)S(1)} %get-tuple-element.40), channel_id=1, source_target_pairs={{8,16},{24,32},{40,48},{56,64},{72,80},{88,96},{104,112},{120,128}... | collective-permute-start | bytes 24584 | tf_op jit(solution)/shard_map/ppermute | solution.py:659
  8.6 0.1 collective-permute-start.1
  8.7 1.2 %collective-permute-done = s16[32,128]{1,0:T(8,128)(2,1)S(1)} collective-permute-done((s16[32,128]{1,0:T(8,128)(2,1)S(1)}, s16[32,128]{1,0:T(8,128)(2,1)S(1)}, u32[]{:S(2)}, u32[]{:S(2)}) %collective-permute-start) | collective-permute-done | bytes 8224 | tf_op jit(solution)/shard_map/ppermute | solution.py:659
  9.9 0.0 collective-permute-done.1
  10.0 20.7 %all_to_all.26.sent_ref.first_sent_ref = s16[8,144,128]{2,1,0:T(8,128)(2,1)S(1)} all-to-all(s16[8,144,128]{2,1,0:T(8,128)(2,1)S(1)} %broadcast_in_dim.6), channel_id=1, replica_groups=mesh['dom'=32,'sub'=8] {'sub'}, dimensions={0} | all-to-all | bytes 589824 | tf_op jit(solution)/shard_map/all_to_all | solution.py:653
  30.6 0.0 copy-done
  30.6 0.0 copy-done.1
  30.7 2.3 %shard_map.96 = (s32[8,128]{1,0:T(8,128)S(1)}, s32[8,128]{1,0:T(8,128)S(1)}, f32[8,128]{1,0:T(8,128)S(1)}, f32[8,128]{1,0:T(8,128)S(1)}, f32[48,128]{1,0:T(8,128...) custom-call(bf16[80,80,128]{2,1,0:T(8,128)(2,1)S(1)} %copy-done, ...), custom_call_target="tpu_custom_call" | custom-call | tf_op jit(solution)/shard_map/pallas_call | solution.py:638
  33.0 0.9 collective-permute-start.3
  33.9 3.2 %collective-permute-start.2 = (s16[16,128]{1,0:T(8,128)(2,1)S(1)}, s16[16,128]{1,0:T(8,128)(2,1)S(1)}, u32[]{:S(2)}, u32[]{:S(2)}) collective-permute-start(s16[16,128]{1,0:T(8,128)(2,1)S(1)} %get-tuple-element.43), channel_id=1, source_target_pairs={{8,16},{24,32},{40,48},{56,64},{72,80},{88,96},{104,112},{120,128}... | collective-permute-start | bytes 12296 | tf_op jit(solution)/shard_map/ppermute | solution.py:659
  37.2 0.0 collective-permute-done.3
  37.2 1.6 %collective-permute-done.2 = s16[16,128]{1,0:T(8,128)(2,1)S(1)} collective-permute-done((s16[16,128]{1,0:T(8,128)(2,1)S(1)}, s16[16,128]{1,0:T(8,128)(2,1)S(1)}, u32[]{:S(2)}, u32[]{:S(2)}) %collective-permute-start.2) | collective-permute-done | bytes 4128 | tf_op jit(solution)/shard_map/ppermute | solution.py:659
  38.9 10.7 %all_to_all.27.sent_ref.second_sent_ref = s16[8,80,128]{2,1,0:T(8,128)(2,1)S(1)} all-to-all(s16[8,80,128]{2,1,0:T(8,128)(2,1)S(1)} %broadcast_in_dim.7), channel_id=1, replica_groups=mesh['dom'=32,'sub'=8] {'sub'}, dimensions={0} | all-to-all | bytes 327680 | tf_op jit(solution)/shard_map/all_to_all | solution.py:653
  49.6 1.6 %shard_map.97 = (f32[48,128]{1,0:T(8,128)S(1)}, f32[48,128]{1,0:T(8,128)S(1)}, f32[2,80,128]{2,1,0:T(8,128)S(1)}, f32[8,128]{1,0:T(8,128)S(1)}, s16[64,128]{1,0:...) custom-call(bf16[80,80,128]{2,1,0:T(8,128)(2,1)S(1)} %copy-done, ...), custom_call_target="tpu_custom_call" | custom-call | tf_op jit(solution)/shard_map/pallas_call | solution.py:638
  51.2 0.1 collective-permute-start.5
  51.3 5.7 %collective-permute-start.4 = (s16[16,128]{1,0:T(8,128)(2,1)S(1)}, s16[16,128]{1,0:T(8,128)(2,1)S(1)}, u32[]{:S(2)}, u32[]{:S(2)}) collective-permute-start(s16[16,128]{1,0:T(8,128)(2,1)S(1)} %get-tuple-element.54), channel_id=1, source_target_pairs={{8,16},{24,32},{40,48},{56,64},{72,80},{88,96},{104,112},{120,128}... | collective-permute-start | bytes 12296 | tf_op jit(solution)/shard_map/ppermute | solution.py:659
  57.0 0.0 collective-permute-done.5
  57.1 1.5 %collective-permute-done.4 = s16[16,128]{1,0:T(8,128)(2,1)S(1)} collective-permute-done((s16[16,128]{1,0:T(8,128)(2,1)S(1)}, s16[16,128]{1,0:T(8,128)(2,1)S(1)}, u32[]{:S(2)}, u32[]{:S(2)}) %collective-permute-start.4) | collective-permute-done | bytes 4128 | tf_op jit(solution)/shard_map/ppermute | solution.py:659
  58.7 10.7 %all_to_all.28.sent_ref.third_sent_ref = s16[8,80,128]{2,1,0:T(8,128)(2,1)S(1)} all-to-all(s16[8,80,128]{2,1,0:T(8,128)(2,1)S(1)} %broadcast_in_dim.8), channel_id=1, replica_groups=mesh['dom'=32,'sub'=8] {'sub'}, dimensions={0} | all-to-all | bytes 327680 | tf_op jit(solution)/shard_map/all_to_all | solution.py:653
  69.3 2.1 %shard_map.98 = (f32[3,80,128]{2,1,0:T(8,128)}, f32[256,128]{1,0:T(8,128)}) custom-call(bf16[80,80,128]{2,1,0:T(8,128)(2,1)S(1)} %copy-done, bf16[80,48,128]{2,1,0:T(8,128)(2,1)S(1)} %copy-done.1, bf16[48,48,128]{2,1,0:T(8,128)(2,1)S(1)} %copy-done.2, f32[8,128]{1,0:T(8,128)S(1)} %get-tuple-element.34.living_ref, ...), custom_call_target="tpu_custom_call" | custom-call | tf_op jit(solution)/shard_map/pallas_call | solution.py:638
  71.4 0.0 copy-done.3
  71.4 11.2 %all-to-all-start.3 = ((f32[256,1,128]{2,1,0:T(1,128)}), f32[256,1,128]{2,1,0:T(1,128)S(1)}, u32[]{:S(2)}, u32[]{:S(2)}) async-start(f32[256,1,128]{2,1,0:T(1,128)} %bitcast.7), calls=%async_computation.3 | async-start | bytes 262144 | tf_op jit(solution)/shard_map/all_to_all | solution.py:725
  82.6 0.9 copy-done.4
  83.5 0.9 copy-done.6
  84.4 2.3 %shard_map.99 = (f32[3,12,256]{2,1,0:T(8,128)S(1)}, f32[4,80,128]{2,1,0:T(8,128)S(1)}) custom-call(s16[8,144,128]{2,1,0:T(8,128)(2,1)S(1)} %all_to_all.26.sent_ref.first_sent_ref, s16[8,80,128]{2,1,0:T(8,128)(2,1)S(1)} %copy-done.6, s16[8,80,128]{2,1,0:T(8,128)(2,1)S(1)} %copy-done.4, f32[12,256]{1,0:T(8,128)} %trace_load_hbm.3, f32[12,256]{1,0:T(8,128)} %shift_hbm.3, ...), custom_call_target="tpu_custom_call" | custom-call | tf_op jit(solution)/shard_map/pallas_call | solution.py:638
  86.8 8.9 %all-to-all-done.3 = f32[256,1,128]{2,1,0:T(1,128)S(1)} async-done(((f32[256,1,128]{2,1,0:T(1,128)}), f32[256,1,128]{2,1,0:T(1,128)S(1)}, u32[]{:S(2)}, u32[]{:S(2)}) %all-to-all-start.3) | async-done | bytes 131104 | tf_op jit(solution)/shard_map/all_to_all | solution.py:725
  95.6 1.0 shard_map.100
  (19 shorter events, 0.2 us)
Async XLA Ops:
  1.3 29.4 %copy-start = (bf16[80,80,128]{2,1,0:T(8,128)(2,1)S(1)}, bf16[80,80,128]{2,1,0:T(8,128)(2,1)}, u32[]{:S(2)}) copy-start(bf16[80,80,128]{2,1,0:T(8,128)(2,1)} %inverse_ref.2) | copy-start | bytes 4915204
  1.3 29.4 %copy-start.1 = (bf16[80,48,128]{2,1,0:T(8,128)(2,1)S(1)}, bf16[80,48,128]{2,1,0:T(8,128)(2,1)}, u32[]{:S(2)}) copy-start(bf16[80,48,128]{2,1,0:T(8,128)(2,1)} %coupling_ref.2) | copy-start | bytes 2949124
  1.3 29.3 %copy-start.2 = (bf16[48,48,128]{2,1,0:T(8,128)(2,1)S(1)}, bf16[48,48,128]{2,1,0:T(8,128)(2,1)}, u32[]{:S(2)}) copy-start(bf16[48,48,128]{2,1,0:T(8,128)(2,1)} %trace_ref.2) | copy-start | bytes 1769476
  1.3 29.3 %copy-start.7 = (s32[4,128]{1,0:T(4,128)S(1)}, s32[4,128]{1,0:T(4,128)}, u32[]{:S(2)}) copy-start(s32[4,128]{1,0:T(4,128)} %names_ref.3) | copy-start | bytes 6148
  4.0 5.8 %collective-permute-start = (s16[32,128]{1,0:T(8,128)(2,1)S(1)}, s16[32,128]{1,0:T(8,128)(2,1)S(1)}, u32[]{:S(2)}, u32[]{:S(2)}) collective-permute-start(s16[32,128]{1,0:T(8,128)(2,1)S(1)} %get-tuple-element.40), channel_id=1, source_target_pairs={{8,16},{24,32},{40,48},{56,64},{72,80},{88,96},{104,112},{120,128}... | collective-permute-start | bytes 24584 | tf_op jit(solution)/shard_map/ppermute | solution.py:659
  8.6 1.3 %collective-permute-start.1 = (s16[32,128]{1,0:T(8,128)(2,1)S(1)}, s16[32,128]{1,0:T(8,128)(2,1)S(1)}, u32[]{:S(2)}, u32[]{:S(2)}) collective-permute-start(s16[32,128]{1,0:T(8,128)(2,1)S(1)} %get-tuple-element.41), channel_id=1, source_target_pairs={{0,8},{8,0},{16,24},{24,16},{32,40},{40,32},{48,56},{56,48},{64,72... | collective-permute-start | bytes 24584 | tf_op jit(solution)/shard_map/ppermute | solution.py:660
  33.0 4.2 %collective-permute-start.3 = (s16[16,128]{1,0:T(8,128)(2,1)S(1)}, s16[16,128]{1,0:T(8,128)(2,1)S(1)}, u32[]{:S(2)}, u32[]{:S(2)}) collective-permute-start(s16[16,128]{1,0:T(8,128)(2,1)S(1)} %get-tuple-element.44), channel_id=1, source_target_pairs={{0,8},{8,0},{16,24},{24,16},{32,40},{40,32},{48,56},{56,48},{64,72... | collective-permute-start | bytes 12296 | tf_op jit(solution)/shard_map/ppermute | solution.py:660
  33.9 4.9 %collective-permute-start.2 = (s16[16,128]{1,0:T(8,128)(2,1)S(1)}, s16[16,128]{1,0:T(8,128)(2,1)S(1)}, u32[]{:S(2)}, u32[]{:S(2)}) collective-permute-start(s16[16,128]{1,0:T(8,128)(2,1)S(1)} %get-tuple-element.43), channel_id=1, source_target_pairs={{8,16},{24,32},{40,48},{56,64},{72,80},{88,96},{104,112},{120,128}... | collective-permute-start | bytes 12296 | tf_op jit(solution)/shard_map/ppermute | solution.py:659
  49.6 1.6 %copy-start.5 = (s16[8,80,128]{2,1,0:T(8,128)(2,1)}, s16[8,80,128]{2,1,0:T(8,128)(2,1)S(1)}, u32[]{:S(2)}) copy-start(s16[8,80,128]{2,1,0:T(8,128)(2,1)S(1)} %all_to_all.27.sent_ref.second_sent_ref) | copy-start | bytes 491524
  51.2 5.8 %collective-permute-start.5 = (s16[16,128]{1,0:T(8,128)(2,1)S(1)}, s16[16,128]{1,0:T(8,128)(2,1)S(1)}, u32[]{:S(2)}, u32[]{:S(2)}) collective-permute-start(s16[16,128]{1,0:T(8,128)(2,1)S(1)} %get-tuple-element.55), channel_id=1, source_target_pairs={{0,8},{8,0},{16,24},{24,16},{32,40},{40,32},{48,56},{56,48},{64,72... | collective-permute-start | bytes 12296 | tf_op jit(solution)/shard_map/ppermute | solution.py:660
  51.3 7.3 %collective-permute-start.4 = (s16[16,128]{1,0:T(8,128)(2,1)S(1)}, s16[16,128]{1,0:T(8,128)(2,1)S(1)}, u32[]{:S(2)}, u32[]{:S(2)}) collective-permute-start(s16[16,128]{1,0:T(8,128)(2,1)S(1)} %get-tuple-element.54), channel_id=1, source_target_pairs={{8,16},{24,32},{40,48},{56,64},{72,80},{88,96},{104,112},{120,128}... | collective-permute-start | bytes 12296 | tf_op jit(solution)/shard_map/ppermute | solution.py:659
  69.3 2.1 %copy-start.3 = (s16[8,80,128]{2,1,0:T(8,128)(2,1)}, s16[8,80,128]{2,1,0:T(8,128)(2,1)S(1)}, u32[]{:S(2)}) copy-start(s16[8,80,128]{2,1,0:T(8,128)(2,1)S(1)} %all_to_all.28.sent_ref.third_sent_ref) | copy-start | bytes 491524
  71.4 24.2 %all-to-all-start.3 = ((f32[256,1,128]{2,1,0:T(1,128)}), f32[256,1,128]{2,1,0:T(1,128)S(1)}, u32[]{:S(2)}, u32[]{:S(2)}) async-start(f32[256,1,128]{2,1,0:T(1,128)} %bitcast.7), calls=%async_computation.3 | async-start | bytes 262144 | tf_op jit(solution)/shard_map/all_to_all | solution.py:725
  82.6 0.9 copy-start.4
  83.5 0.9 copy-start.6

commit v5 on v4

--- a/solution.py
+++ b/solution.py
@@ -23,6 +23,7 @@
 
 BIAS = 16384.0
 SCALE_LANE = 64
+MATE_LANE = 16
 FACES, NAMES, SCALES, UP, UP_SHIFT, DOWN, FIRST_ROWS = 48, 96, 100, 105, 118, 131, 144
 LATER_UP, LATER_DOWN, LATER_ROWS = 54, 67, 80
 
@@ -458,8 +459,8 @@
 def fourth_kernel(
     inverse_ref, coupling_ref, trace_ref, living_ref, sent_ref,
     chunk_ref, lane_ref, valid_ref, weight_ref, shifts_ref, first_view_ref, view_ref, terms_ref, scale_ref, before_ref,
-    inner_hbm, sums_hbm,
-    inner_ref, sums_ref, gathered_ref, sems,
+    sums_ref, for_mate_ref, inner_hbm,
+    inner_ref, gathered_ref, sems,
 ):
     copies = [
         pltpu.make_async_copy(before_ref, inner_hbm.at[pl.ds(0, 2)], sems.at[0]),
@@ -491,12 +492,10 @@
         sums = sums + jnp.where(lane == SCALE_LANE + place, powers[place], 0.0)
         total = product.reshape(6, 8, LANES).sum(0).sum(0, keepdims=True).sum(1, keepdims=True)
         sums = sums + jnp.where(lane == place, total, 0.0)
-    sums_ref[...] = jnp.broadcast_to(sums, sums_ref.shape)
-    send = pltpu.make_async_copy(sums_ref, sums_hbm, sems.at[2])
-    send.start()
+    sums_ref[...] = sums
+    for_mate_ref[...] = pltpu.roll(sums, MATE_LANE, 1)
     for copy in copies:
         copy.wait()
-    send.wait()
 
 
 def owner_kernel(
@@ -619,9 +618,10 @@
 ):
     dom, sub = ids()
     sums = all_sums_ref[...]
+    sums = jnp.concatenate([sums, pltpu.roll(sums, LANES - MATE_LANE, 1)], 0)
     powers = pltpu.roll(sums, LANES - SCALE_LANE, 1)
-    own = pltpu.roll(all_sums_ref[pl.ds(dom * SUB + sub, 1), :], LANES - SCALE_LANE, 1)
-    used = lane_iota(1) < SCALE_LANE
+    own = pltpu.roll(all_sums_ref[pl.ds((dom // 2) * SUB + sub, 1), :], LANES - SCALE_LANE, 1)
+    used = lane_iota(1) < MATE_LANE
     powers, own = jnp.where(used, powers, 0.0), jnp.where(used, own, 0.0)
     top = powers.reshape(-1, 8, LANES).max(0).max(0, keepdims=True)
     sums = (sums * jnp.exp2(powers - top)).reshape(-1, 8, LANES).sum(0).sum(0, keepdims=True)
@@ -711,18 +711,22 @@
         scratch=[stage, decoded],
     )
     third = later(own, on, off)
-    everyone = lax.axis_size("dom") * SUB
-    kept, sums = call(
+    partitions = lax.axis_size("dom")
+    sums, for_mate, kept = call(
         fourth_kernel,
-        [],
+        [((1, LANES), F32), ((1, LANES), F32)],
         [*matrices, living, third, chunk, lane, valid, weight, shifts, view0, view1, terms1, scale, kept],
-        to_hbm=[((3, NI, LANES), F32), ((everyone, LANES), F32)],
+        to_hbm=[((3, NI, LANES), F32)],
         scratch=[
-            pltpu.VMEM((NI, LANES), F32), pltpu.VMEM((everyone, LANES), F32), decoded,
-            pltpu.SemaphoreType.DMA((3,)),
+            pltpu.VMEM((NI, LANES), F32), decoded, pltpu.SemaphoreType.DMA((2,)),
         ],
     )
-    all_sums = lax.all_to_all(sums, ("dom", "sub"), 0, 0, tiled=True)
+    sums = sums + lax.ppermute(for_mate, "dom", [(i, i ^ 1) for i in range(partitions)])
+    members = [[d * SUB + s for d in range(core, partitions, 2) for s in range(SUB)] for core in range(2)]
+    all_sums = lax.all_to_all(
+        jnp.broadcast_to(sums, (len(members[0]), LANES)), ("dom", "sub"), 0, 0, tiled=True,
+        axis_index_groups=members,
+    )
     owned, kept = call(
         owner_kernel,
         [((3, FD, 2 * RIM), F32), ((4, NI, LANES), F32)],

time: 97 us -> 96.8 us (level)
  blocking collectives: 42 us -> 45.8 us
  waiting for transfers between devices: 13.3 us -> 10.8 us
  starting transfers between devices: 25.8 us -> 23.7 us
    all_to_all x3, blocking collectives: 42 us -> 45.8 us  [to_all(): return lax.all_to_all(copies, 'sub', 0, 0, tiled=True)]
    all_to_all x1, waiting for transfers between devices: 8.88 us -> 6.43 us  [on_device(): lax.all_to_all(jnp.broadcast_to(sums, (len(members[0]), LANES)), ('dom',...]
    ppermute x3, starting transfers between devices: 13.5 us -> 12.4 us  [neighbours(): from_off = lax.ppermute(off, 'dom', pairs + [(j, i) for i, j in pairs])]
  transfers between devices with their start and end apart: 7 -> 8, of which waited for: 4 -> 5; matrix products, arithmetic and copies ran while one was open for 0% -> 0% of each run, Pallas kernels for 2% -> 2%
where the time goes in v5:
time: 96.8 us; the launch traced here: 96.3 us
  blocking collectives  45.8 us (47%)
  starting transfers between devices  23.7 us (24%)
  Pallas kernels  11.8 us (12%)
  waiting for transfers between devices  10.8 us (11%)
  local copies, waits for them, and re-layouts  2.6 us (3%)
  between operations  1.54 us (2%)
    all_to_all x3, blocking collectives, to_all(): return lax.all_to_all(copies, 'sub', 0, 0, tiled=True)  45.8 us
    ppermute x3, starting transfers between devices, neighbours(): from_off = lax.ppermute(off, 'dom', pairs + [(j, i) for i, j in pairs])  12.4 us
    pallas_call x6, Pallas kernels, call(): pl.pallas_call(kernel, out_shape=[jax.ShapeDtypeStruct(s, d) for s, d in...  11.8 us
    all_to_all x1, starting transfers between devices, on_device(): lax.all_to_all(jnp.broadcast_to(sums, (len(members[0]), LANES)), ('dom',...  10.4 us
    all_to_all x1, waiting for transfers between devices, on_device(): lax.all_to_all(jnp.broadcast_to(sums, (len(members[0]), LANES)), ('dom',...  6.43 us
    ppermute x3, waiting for transfers between devices, neighbours(): from_off = lax.ppermute(off, 'dom', pairs + [(j, i) for i, j in pairs])  3.54 us
  transfers between devices with their start and end apart: 8, of which 5 were waited for; matrix products, arithmetic and copies ran while one was open for 0% of the time, Pallas kernels for 2%

profile of v5, /device:TPU:1, one launch (start us, length us, event | category | flops | bytes accessed | tf_op | source)
XLA Modules:
  0.0 96.3 jit_solution(10526920182962125899)
XLA Ops:
  1.3 0.0 copy-start
  1.3 0.0 copy-start.1
  1.3 0.0 copy-start.2
  1.3 2.7 %shard_map.95 = (f32[8,128]{1,0:T(8,128)S(1)}, s16[112,128]{1,0:T(8,128)(2,1)S(1)}, s16[32,128]{1,0:T(8,128)(2,1)S(1)}, s16[32,128]{1,0:T(8,128)(2,1)S(1)}, f32[80,128]{1,0:T(8,128)}) custom-call(s32[1]{0:T(128)S(6)} %copy.10.padding_ref, bf16[80,80,128]{2,1,0:T(8,128)(2,1)} %inverse_ref.2, bf16[80,48,128]{2,1,0:T(8,128)(2,1)} %coupling_ref.2, ...), custom_call_target="tpu_custom_call" | custom-call | tf_op jit(solution)/shard_map/pallas_call | solution.py:638
  4.0 4.5 %collective-permute-start = (s16[32,128]{1,0:T(8,128)(2,1)S(1)}, s16[32,128]{1,0:T(8,128)(2,1)S(1)}, u32[]{:S(2)}, u32[]{:S(2)}) collective-permute-start(s16[32,128]{1,0:T(8,128)(2,1)S(1)} %get-tuple-element.41), channel_id=1, source_target_pairs={{8,16},{24,32},{40,48},{56,64},{72,80},{88,96},{104,112},{120,128}... | collective-permute-start | bytes 24584 | tf_op jit(solution)/shard_map/ppermute | solution.py:659
  8.6 0.1 collective-permute-start.1
  8.7 1.2 %collective-permute-done = s16[32,128]{1,0:T(8,128)(2,1)S(1)} collective-permute-done((s16[32,128]{1,0:T(8,128)(2,1)S(1)}, s16[32,128]{1,0:T(8,128)(2,1)S(1)}, u32[]{:S(2)}, u32[]{:S(2)}) %collective-permute-start) | collective-permute-done | bytes 8224 | tf_op jit(solution)/shard_map/ppermute | solution.py:659
  9.9 0.0 collective-permute-done.1
  10.0 20.7 %all_to_all.23.sent_ref.first_sent_ref = s16[8,144,128]{2,1,0:T(8,128)(2,1)S(1)} all-to-all(s16[8,144,128]{2,1,0:T(8,128)(2,1)S(1)} %broadcast_in_dim.8), channel_id=1, replica_groups=mesh['dom'=32,'sub'=8] {'sub'}, dimensions={0} | all-to-all | bytes 589824 | tf_op jit(solution)/shard_map/all_to_all | solution.py:653
  30.7 2.3 %shard_map.96 = (s32[8,128]{1,0:T(8,128)S(1)}, s32[8,128]{1,0:T(8,128)S(1)}, f32[8,128]{1,0:T(8,128)S(1)}, f32[8,128]{1,0:T(8,128)S(1)}, f32[48,128]{1,0:T(8,128...) custom-call(bf16[80,80,128]{2,1,0:T(8,128)(2,1)S(1)} %copy-done, ...), custom_call_target="tpu_custom_call" | custom-call | tf_op jit(solution)/shard_map/pallas_call | solution.py:638
  33.0 4.1 %collective-permute-start.2 = (s16[16,128]{1,0:T(8,128)(2,1)S(1)}, s16[16,128]{1,0:T(8,128)(2,1)S(1)}, u32[]{:S(2)}, u32[]{:S(2)}) collective-permute-start(s16[16,128]{1,0:T(8,128)(2,1)S(1)} %get-tuple-element.44), channel_id=1, source_target_pairs={{8,16},{24,32},{40,48},{56,64},{72,80},{88,96},{104,112},{120,128}... | collective-permute-start | bytes 12296 | tf_op jit(solution)/shard_map/ppermute | solution.py:659
  37.1 0.1 collective-permute-start.3
  37.2 1.2 %collective-permute-done.2 = s16[16,128]{1,0:T(8,128)(2,1)S(1)} collective-permute-done((s16[16,128]{1,0:T(8,128)(2,1)S(1)}, s16[16,128]{1,0:T(8,128)(2,1)S(1)}, u32[]{:S(2)}, u32[]{:S(2)}) %collective-permute-start.2) | collective-permute-done | bytes 4128 | tf_op jit(solution)/shard_map/ppermute | solution.py:659
  38.3 0.0 collective-permute-done.3
  38.4 12.5 %all_to_all.24.sent_ref.second_sent_ref = s16[8,80,128]{2,1,0:T(8,128)(2,1)S(1)} all-to-all(s16[8,80,128]{2,1,0:T(8,128)(2,1)S(1)} %broadcast_in_dim.9), channel_id=1, replica_groups=mesh['dom'=32,'sub'=8] {'sub'}, dimensions={0} | all-to-all | bytes 327680 | tf_op jit(solution)/shard_map/all_to_all | solution.py:653
  50.9 1.6 %shard_map.97 = (f32[48,128]{1,0:T(8,128)S(1)}, f32[48,128]{1,0:T(8,128)S(1)}, f32[2,80,128]{2,1,0:T(8,128)S(1)}, f32[8,128]{1,0:T(8,128)S(1)}, s16[64,128]{1,0:...) custom-call(bf16[80,80,128]{2,1,0:T(8,128)(2,1)S(1)} %copy-done, ...), custom_call_target="tpu_custom_call" | custom-call | tf_op jit(solution)/shard_map/pallas_call | solution.py:638
  52.6 3.8 %collective-permute-start.4 = (s16[16,128]{1,0:T(8,128)(2,1)S(1)}, s16[16,128]{1,0:T(8,128)(2,1)S(1)}, u32[]{:S(2)}, u32[]{:S(2)}) collective-permute-start(s16[16,128]{1,0:T(8,128)(2,1)S(1)} %get-tuple-element.55), channel_id=1, source_target_pairs={{8,16},{24,32},{40,48},{56,64},{72,80},{88,96},{104,112},{120,128}... | collective-permute-start | bytes 12296 | tf_op jit(solution)/shard_map/ppermute | solution.py:659
  56.4 0.1 collective-permute-start.5
  56.5 1.2 %collective-permute-done.4 = s16[16,128]{1,0:T(8,128)(2,1)S(1)} collective-permute-done((s16[16,128]{1,0:T(8,128)(2,1)S(1)}, s16[16,128]{1,0:T(8,128)(2,1)S(1)}, u32[]{:S(2)}, u32[]{:S(2)}) %collective-permute-start.4) | collective-permute-done | bytes 4128 | tf_op jit(solution)/shard_map/ppermute | solution.py:659
  57.7 0.0 collective-permute-done.5
  57.7 12.5 %all_to_all.25.sent_ref.third_sent_ref = s16[8,80,128]{2,1,0:T(8,128)(2,1)S(1)} all-to-all(s16[8,80,128]{2,1,0:T(8,128)(2,1)S(1)} %broadcast_in_dim.10), channel_id=1, replica_groups=mesh['dom'=32,'sub'=8] {'sub'}, dimensions={0} | all-to-all | bytes 327680 | tf_op jit(solution)/shard_map/all_to_all | solution.py:653
  70.3 1.9 %shard_map.98 = (f32[1,128]{1,0:T(1,128)S(1)}, f32[1,128]{1,0:T(1,128)S(1)}, f32[3,80,128]{2,1,0:T(8,128)}) custom-call(bf16[80,80,128]{2,1,0:T(8,128)(2,1)S(1)} %copy-done, bf16[80,48,128]{2,1,0:T(8,128)(2,1)S(1)} %copy-done.1, bf16[48,48,128]{2,1,0:T(8,128)(2,1)S(1)} %copy-done.2, f32[8,128]{1,0:T(8,128)S(1)} %get-tuple-element.35.living_ref, ...), custom_call_target="tpu_custom_call" | custom-call | tf_op jit(solution)/shard_map/pallas_call | solution.py:638
  72.2 0.0 copy-done.3
  72.2 0.7 collective-permute-start.6
  72.9 0.8 collective-permute-done.6
  73.7 0.7 broadcast_in_dim.11
  74.4 10.4 %all-to-all-start.3 = ((f32[128,1,128]{2,1,0:T(1,128)}), f32[128,1,128]{2,1,0:T(1,128)S(1)}, u32[]{:S(2)}, u32[]{:S(2)}) async-start(f32[128,1,128]{2,1,0:T(1,128)} %broadcast_in_dim.11), calls=%async_computation.3 | async-start | bytes 131072 | tf_op jit(solution)/shard_map/all_to_all | solution.py:726
  84.7 0.9 copy-done.4
  85.7 0.9 copy-done.6
  86.6 2.3 %shard_map.99 = (f32[3,12,256]{2,1,0:T(8,128)S(1)}, f32[4,80,128]{2,1,0:T(8,128)S(1)}) custom-call(s16[8,144,128]{2,1,0:T(8,128)(2,1)S(1)} %all_to_all.23.sent_ref.first_sent_ref, s16[8,80,128]{2,1,0:T(8,128)(2,1)S(1)} %copy-done.6, s16[8,80,128]{2,1,0:T(8,128)(2,1)S(1)} %copy-done.4, f32[12,256]{1,0:T(8,128)} %trace_load_hbm.3, f32[12,256]{1,0:T(8,128)} %shift_hbm.3, ...), custom_call_target="tpu_custom_call" | custom-call | tf_op jit(solution)/shard_map/pallas_call | solution.py:638
  88.9 6.4 %all-to-all-done.3 = f32[128,1,128]{2,1,0:T(1,128)S(1)} async-done(((f32[128,1,128]{2,1,0:T(1,128)}), f32[128,1,128]{2,1,0:T(1,128)S(1)}, u32[]{:S(2)}, u32[]{:S(2)}) %all-to-all-start.3) | async-done | bytes 65568 | tf_op jit(solution)/shard_map/all_to_all | solution.py:726
  95.3 1.0 %shard_map.100 = (f32[12,256]{1,0:T(8,128)}, f32[80,128]{1,0:T(8,128)}) custom-call(f32[8,128]{1,0:T(8,128)S(1)} %get-tuple-element.35.living_ref, f32[128,128]{1,0:T(8,128)S(1)} %bitcast.4, f32[4,80,128]{2,1,0:T(8,128)S(1)} %get-tuple-element.66.inner_ref, f32[3,12,256]{2,1,0:T(8,128)S(1)} %get-tuple-element.67.owned_ref), custom_call_target="tpu_custom_call" | custom-call | tf_op jit(solution)/shard_map/pallas_call | solution.py:638
  (23 shorter events, 0.2 us)
Async XLA Ops:
  1.3 29.4 %copy-start = (bf16[80,80,128]{2,1,0:T(8,128)(2,1)S(1)}, bf16[80,80,128]{2,1,0:T(8,128)(2,1)}, u32[]{:S(2)}) copy-start(bf16[80,80,128]{2,1,0:T(8,128)(2,1)} %inverse_ref.2) | copy-start | bytes 4915204
  1.3 29.4 %copy-start.1 = (bf16[80,48,128]{2,1,0:T(8,128)(2,1)S(1)}, bf16[80,48,128]{2,1,0:T(8,128)(2,1)}, u32[]{:S(2)}) copy-start(bf16[80,48,128]{2,1,0:T(8,128)(2,1)} %coupling_ref.2) | copy-start | bytes 2949124
  1.3 29.3 %copy-start.2 = (bf16[48,48,128]{2,1,0:T(8,128)(2,1)S(1)}, bf16[48,48,128]{2,1,0:T(8,128)(2,1)}, u32[]{:S(2)}) copy-start(bf16[48,48,128]{2,1,0:T(8,128)(2,1)} %trace_ref.2) | copy-start | bytes 1769476
  1.3 29.3 %copy-start.7 = (s32[4,128]{1,0:T(4,128)S(1)}, s32[4,128]{1,0:T(4,128)}, u32[]{:S(2)}) copy-start(s32[4,128]{1,0:T(4,128)} %names_ref.3) | copy-start | bytes 6148
  4.0 5.8 %collective-permute-start = (s16[32,128]{1,0:T(8,128)(2,1)S(1)}, s16[32,128]{1,0:T(8,128)(2,1)S(1)}, u32[]{:S(2)}, u32[]{:S(2)}) collective-permute-start(s16[32,128]{1,0:T(8,128)(2,1)S(1)} %get-tuple-element.41), channel_id=1, source_target_pairs={{8,16},{24,32},{40,48},{56,64},{72,80},{88,96},{104,112},{120,128}... | collective-permute-start | bytes 24584 | tf_op jit(solution)/shard_map/ppermute | solution.py:659
  8.6 1.3 %collective-permute-start.1 = (s16[32,128]{1,0:T(8,128)(2,1)S(1)}, s16[32,128]{1,0:T(8,128)(2,1)S(1)}, u32[]{:S(2)}, u32[]{:S(2)}) collective-permute-start(s16[32,128]{1,0:T(8,128)(2,1)S(1)} %get-tuple-element.42), channel_id=1, source_target_pairs={{0,8},{8,0},{16,24},{24,16},{32,40},{40,32},{48,56},{56,48},{64,72... | collective-permute-start | bytes 24584 | tf_op jit(solution)/shard_map/ppermute | solution.py:660
  33.0 5.4 %collective-permute-start.2 = (s16[16,128]{1,0:T(8,128)(2,1)S(1)}, s16[16,128]{1,0:T(8,128)(2,1)S(1)}, u32[]{:S(2)}, u32[]{:S(2)}) collective-permute-start(s16[16,128]{1,0:T(8,128)(2,1)S(1)} %get-tuple-element.44), channel_id=1, source_target_pairs={{8,16},{24,32},{40,48},{56,64},{72,80},{88,96},{104,112},{120,128}... | collective-permute-start | bytes 12296 | tf_op jit(solution)/shard_map/ppermute | solution.py:659
  37.1 1.3 %collective-permute-start.3 = (s16[16,128]{1,0:T(8,128)(2,1)S(1)}, s16[16,128]{1,0:T(8,128)(2,1)S(1)}, u32[]{:S(2)}, u32[]{:S(2)}) collective-permute-start(s16[16,128]{1,0:T(8,128)(2,1)S(1)} %get-tuple-element.45), channel_id=1, source_target_pairs={{0,8},{8,0},{16,24},{24,16},{32,40},{40,32},{48,56},{56,48},{64,72... | collective-permute-start | bytes 12296 | tf_op jit(solution)/shard_map/ppermute | solution.py:660
  50.9 1.6 %copy-start.5 = (s16[8,80,128]{2,1,0:T(8,128)(2,1)}, s16[8,80,128]{2,1,0:T(8,128)(2,1)S(1)}, u32[]{:S(2)}) copy-start(s16[8,80,128]{2,1,0:T(8,128)(2,1)S(1)} %all_to_all.24.sent_ref.second_sent_ref) | copy-start | bytes 491524
  52.6 5.1 %collective-permute-start.4 = (s16[16,128]{1,0:T(8,128)(2,1)S(1)}, s16[16,128]{1,0:T(8,128)(2,1)S(1)}, u32[]{:S(2)}, u32[]{:S(2)}) collective-permute-start(s16[16,128]{1,0:T(8,128)(2,1)S(1)} %get-tuple-element.55), channel_id=1, source_target_pairs={{8,16},{24,32},{40,48},{56,64},{72,80},{88,96},{104,112},{120,128}... | collective-permute-start | bytes 12296 | tf_op jit(solution)/shard_map/ppermute | solution.py:659
  56.4 1.3 %collective-permute-start.5 = (s16[16,128]{1,0:T(8,128)(2,1)S(1)}, s16[16,128]{1,0:T(8,128)(2,1)S(1)}, u32[]{:S(2)}, u32[]{:S(2)}) collective-permute-start(s16[16,128]{1,0:T(8,128)(2,1)S(1)} %get-tuple-element.56), channel_id=1, source_target_pairs={{0,8},{8,0},{16,24},{24,16},{32,40},{40,32},{48,56},{56,48},{64,72... | collective-permute-start | bytes 12296 | tf_op jit(solution)/shard_map/ppermute | solution.py:660
  70.3 1.9 %copy-start.3 = (s16[8,80,128]{2,1,0:T(8,128)(2,1)}, s16[8,80,128]{2,1,0:T(8,128)(2,1)S(1)}, u32[]{:S(2)}) copy-start(s16[8,80,128]{2,1,0:T(8,128)(2,1)S(1)} %all_to_all.25.sent_ref.third_sent_ref) | copy-start | bytes 491524
  72.2 1.5 %collective-permute-start.6 = (f32[1,128]{1,0:T(1,128)S(1)}, f32[1,128]{1,0:T(1,128)S(1)}, u32[]{:S(2)}, u32[]{:S(2)}) collective-permute-start(f32[1,128]{1,0:T(1,128)S(1)} %get-tuple-element.63), channel_id=1, source_target_pairs={{0,8},{8,0},{16,24},{24,16},{32,40},{40,32},{48,56},{56,48},{64,72... | collective-permute-start | bytes 1544 | tf_op jit(solution)/shard_map/ppermute | solution.py:724
  74.4 20.9 %all-to-all-start.3 = ((f32[128,1,128]{2,1,0:T(1,128)}), f32[128,1,128]{2,1,0:T(1,128)S(1)}, u32[]{:S(2)}, u32[]{:S(2)}) async-start(f32[128,1,128]{2,1,0:T(1,128)} %broadcast_in_dim.11), calls=%async_computation.3 | async-start | bytes 131072 | tf_op jit(solution)/shard_map/all_to_all | solution.py:726
  84.7 0.9 copy-start.4
  85.7 0.9 copy-start.6

commit v6 on v4

--- a/solution.py
+++ b/solution.py
@@ -72,11 +72,11 @@
 
 def transposed_times(matrix_ref, vector):
     depth = matrix_ref.shape[0]
-    totals = [None, None]
+    totals = [None] * 4
     for i in range(depth):
         term = matrix_ref[i].astype(F32) * vector[i : i + 1]
-        totals[i % 2] = term if totals[i % 2] is None else totals[i % 2] + term
-    return totals[0] + totals[1]
+        totals[i % 4] = term if totals[i % 4] is None else totals[i % 4] + term
+    return (totals[0] + totals[1]) + (totals[2] + totals[3])
 
 
 def coded(value):
@@ -179,11 +179,14 @@
 def whole_pick(values, chosen):
     high = jnp.floor(values * (1.0 / 256.0))
     stacked = jnp.concatenate([high, values - 256.0 * high], 0).astype(BF16)
-    sums = lax.dot_general(
-        stacked, chosen, (((1,), (1,)), ((), ())), preferred_element_type=F32
-    )
+    sums = jnp.dot(stacked, chosen, preferred_element_type=F32)
     rows = values.shape[0]
     return 256.0 * sums[:rows] + sums[rows:]
+
+
+def as_columns(rows):
+    rest = jnp.zeros((LANES - len(rows), LANES), F32)
+    return jnp.concatenate([rows, rest], 0).T.astype(jnp.int32)
 
 
 def face_major(terms_ref):
@@ -195,13 +198,14 @@
 
 
 def rim_lists(terms_ref, names_ref):
-    wanted = lax.broadcasted_iota(jnp.int32, (2 * RIM, LANES), 0)
-    wanted = jnp.where(wanted < RIM, wanted, wanted + FACES_PART - RIM)
-    chosen = [
-        jnp.where(wanted == names_ref[j : j + 1, :], 1.0, 0.0).astype(BF16)
-        for j in range(4)
-    ]
-    lists = whole_pick(face_major(terms_ref), jnp.concatenate(chosen, 1))
+    turned = as_columns(names_ref[...].astype(F32))
+    wanted = lane_iota(LANES)
+    chosen = []
+    for j in range(4):
+        name = jnp.broadcast_to(turned[:, j : j + 1], (LANES, LANES))
+        hits = [name == wanted, name == wanted + FACES_PART]
+        chosen.append(jnp.concatenate([jnp.where(hit, 1.0, 0.0).astype(BF16) for hit in hits], 1))
+    lists = whole_pick(face_major(terms_ref), jnp.concatenate(chosen, 0))
     return lists[:FD, :RIM], lists[:FD, RIM:]
 
 

time: 97 us -> 96.8 us (level)
  no operation moved by 1% of the time
where the time goes in v6:
time: 96.8 us; the launch traced here: 96.4 us
  blocking collectives  42 us (43%)
  starting transfers between devices  25.8 us (27%)
  waiting for transfers between devices  13.3 us (14%)
  Pallas kernels  11.8 us (12%)
  local copies, waits for them, and re-layouts  1.94 us (2%)
  between operations  1.52 us (2%)
    all_to_all x3, blocking collectives, to_all(): return lax.all_to_all(copies, 'sub', 0, 0, tiled=True)  42 us
    ppermute x3, starting transfers between devices, neighbours(): from_off = lax.ppermute(off, 'dom', pairs + [(j, i) for i, j in pairs])  13.5 us
    pallas_call x6, Pallas kernels, call(): pl.pallas_call(kernel, out_shape=[jax.ShapeDtypeStruct(s, d) for s, d in...  11.8 us
    all_to_all x1, starting transfers between devices, on_device(): all_sums = lax.all_to_all(sums, ('dom', 'sub'), 0, 0, tiled=True)  11.2 us
    all_to_all x1, waiting for transfers between devices, on_device(): all_sums = lax.all_to_all(sums, ('dom', 'sub'), 0, 0, tiled=True)  8.89 us
    ppermute x3, waiting for transfers between devices, neighbours(): from_off = lax.ppermute(off, 'dom', pairs + [(j, i) for i, j in pairs])  4.39 us
  transfers between devices with their start and end apart: 7, of which 4 were waited for; matrix products, arithmetic and copies ran while one was open for 0% of the time, Pallas kernels for 2%

profile of v6, /device:TPU:1, one launch (start us, length us, event | category | flops | bytes accessed | tf_op | source)
XLA Modules:
  0.0 96.4 jit_solution(5503949257288961704)
XLA Ops:
  1.3 0.0 copy-start
  1.3 0.0 copy-start.1
  1.3 0.0 copy-start.2
  1.3 0.0 copy-start.7
  1.3 2.7 %shard_map.95 = (f32[8,128]{1,0:T(8,128)S(1)}, s16[112,128]{1,0:T(8,128)(2,1)S(1)}, s16[32,128]{1,0:T(8,128)(2,1)S(1)}, s16[32,128]{1,0:T(8,128)(2,1)S(1)}, f32[80,128]{1,0:T(8,128)}) custom-call(s32[1]{0:T(128)S(6)} %copy.11.padding_ref, bf16[80,80,128]{2,1,0:T(8,128)(2,1)} %inverse_ref.2, bf16[80,48,128]{2,1,0:T(8,128)(2,1)} %coupling_ref.2, ...), custom_call_target="tpu_custom_call" | custom-call | tf_op jit(solution)/shard_map/pallas_call | solution.py:642
  4.1 4.5 %collective-permute-start = (s16[32,128]{1,0:T(8,128)(2,1)S(1)}, s16[32,128]{1,0:T(8,128)(2,1)S(1)}, u32[]{:S(2)}, u32[]{:S(2)}) collective-permute-start(s16[32,128]{1,0:T(8,128)(2,1)S(1)} %get-tuple-element.40), channel_id=1, source_target_pairs={{8,16},{24,32},{40,48},{56,64},{72,80},{88,96},{104,112},{120,128}... | collective-permute-start | bytes 24584 | tf_op jit(solution)/shard_map/ppermute | solution.py:663
  8.6 0.1 collective-permute-start.1
  8.7 1.2 %collective-permute-done = s16[32,128]{1,0:T(8,128)(2,1)S(1)} collective-permute-done((s16[32,128]{1,0:T(8,128)(2,1)S(1)}, s16[32,128]{1,0:T(8,128)(2,1)S(1)}, u32[]{:S(2)}, u32[]{:S(2)}) %collective-permute-start) | collective-permute-done | bytes 8224 | tf_op jit(solution)/shard_map/ppermute | solution.py:663
  9.9 0.0 collective-permute-done.1
  10.0 20.7 %all_to_all.26.sent_ref.first_sent_ref = s16[8,144,128]{2,1,0:T(8,128)(2,1)S(1)} all-to-all(s16[8,144,128]{2,1,0:T(8,128)(2,1)S(1)} %broadcast_in_dim.6), channel_id=1, replica_groups=mesh['dom'=32,'sub'=8] {'sub'}, dimensions={0} | all-to-all | bytes 589824 | tf_op jit(solution)/shard_map/all_to_all | solution.py:657
  30.7 0.0 copy-done
  30.7 0.0 copy-done.1
  30.7 2.2 %shard_map.96 = (s32[8,128]{1,0:T(8,128)S(1)}, s32[8,128]{1,0:T(8,128)S(1)}, f32[8,128]{1,0:T(8,128)S(1)}, f32[8,128]{1,0:T(8,128)S(1)}, f32[48,128]{1,0:T(8,128...) custom-call(bf16[80,80,128]{2,1,0:T(8,128)(2,1)S(1)} %copy-done, ...), custom_call_target="tpu_custom_call" | custom-call | tf_op jit(solution)/shard_map/pallas_call | solution.py:642
  32.9 0.9 collective-permute-start.3
  33.9 3.2 %collective-permute-start.2 = (s16[16,128]{1,0:T(8,128)(2,1)S(1)}, s16[16,128]{1,0:T(8,128)(2,1)S(1)}, u32[]{:S(2)}, u32[]{:S(2)}) collective-permute-start(s16[16,128]{1,0:T(8,128)(2,1)S(1)} %get-tuple-element.43), channel_id=1, source_target_pairs={{8,16},{24,32},{40,48},{56,64},{72,80},{88,96},{104,112},{120,128}... | collective-permute-start | bytes 12296 | tf_op jit(solution)/shard_map/ppermute | solution.py:663
  37.2 0.0 collective-permute-done.3
  37.2 1.6 %collective-permute-done.2 = s16[16,128]{1,0:T(8,128)(2,1)S(1)} collective-permute-done((s16[16,128]{1,0:T(8,128)(2,1)S(1)}, s16[16,128]{1,0:T(8,128)(2,1)S(1)}, u32[]{:S(2)}, u32[]{:S(2)}) %collective-permute-start.2) | collective-permute-done | bytes 4128 | tf_op jit(solution)/shard_map/ppermute | solution.py:663
  38.9 10.7 %all_to_all.27.sent_ref.second_sent_ref = s16[8,80,128]{2,1,0:T(8,128)(2,1)S(1)} all-to-all(s16[8,80,128]{2,1,0:T(8,128)(2,1)S(1)} %broadcast_in_dim.7), channel_id=1, replica_groups=mesh['dom'=32,'sub'=8] {'sub'}, dimensions={0} | all-to-all | bytes 327680 | tf_op jit(solution)/shard_map/all_to_all | solution.py:657
  49.5 1.5 %shard_map.97 = (f32[48,128]{1,0:T(8,128)S(1)}, f32[48,128]{1,0:T(8,128)S(1)}, f32[2,80,128]{2,1,0:T(8,128)S(1)}, f32[8,128]{1,0:T(8,128)S(1)}, s16[64,128]{1,0:...) custom-call(bf16[80,80,128]{2,1,0:T(8,128)(2,1)S(1)} %copy-done, ...), custom_call_target="tpu_custom_call" | custom-call | tf_op jit(solution)/shard_map/pallas_call | solution.py:642
  51.1 0.1 collective-permute-start.5
  51.2 5.7 %collective-permute-start.4 = (s16[16,128]{1,0:T(8,128)(2,1)S(1)}, s16[16,128]{1,0:T(8,128)(2,1)S(1)}, u32[]{:S(2)}, u32[]{:S(2)}) collective-permute-start(s16[16,128]{1,0:T(8,128)(2,1)S(1)} %get-tuple-element.54), channel_id=1, source_target_pairs={{8,16},{24,32},{40,48},{56,64},{72,80},{88,96},{104,112},{120,128}... | collective-permute-start | bytes 12296 | tf_op jit(solution)/shard_map/ppermute | solution.py:663
  56.9 0.0 collective-permute-done.5
  56.9 1.5 %collective-permute-done.4 = s16[16,128]{1,0:T(8,128)(2,1)S(1)} collective-permute-done((s16[16,128]{1,0:T(8,128)(2,1)S(1)}, s16[16,128]{1,0:T(8,128)(2,1)S(1)}, u32[]{:S(2)}, u32[]{:S(2)}) %collective-permute-start.4) | collective-permute-done | bytes 4128 | tf_op jit(solution)/shard_map/ppermute | solution.py:663
  58.5 10.7 %all_to_all.28.sent_ref.third_sent_ref = s16[8,80,128]{2,1,0:T(8,128)(2,1)S(1)} all-to-all(s16[8,80,128]{2,1,0:T(8,128)(2,1)S(1)} %broadcast_in_dim.8), channel_id=1, replica_groups=mesh['dom'=32,'sub'=8] {'sub'}, dimensions={0} | all-to-all | bytes 327680 | tf_op jit(solution)/shard_map/all_to_all | solution.py:657
  69.2 2.0 %shard_map.98 = (f32[3,80,128]{2,1,0:T(8,128)}, f32[256,128]{1,0:T(8,128)}) custom-call(bf16[80,80,128]{2,1,0:T(8,128)(2,1)S(1)} %copy-done, bf16[80,48,128]{2,1,0:T(8,128)(2,1)S(1)} %copy-done.1, bf16[48,48,128]{2,1,0:T(8,128)(2,1)S(1)} %copy-done.2, f32[8,128]{1,0:T(8,128)S(1)} %get-tuple-element.34.living_ref, ...), custom_call_target="tpu_custom_call" | custom-call | tf_op jit(solution)/shard_map/pallas_call | solution.py:642
  71.2 0.0 copy-done.3
  71.2 11.2 %all-to-all-start.3 = ((f32[256,1,128]{2,1,0:T(1,128)}), f32[256,1,128]{2,1,0:T(1,128)S(1)}, u32[]{:S(2)}, u32[]{:S(2)}) async-start(f32[256,1,128]{2,1,0:T(1,128)} %bitcast.7), calls=%async_computation.3 | async-start | bytes 262144 | tf_op jit(solution)/shard_map/all_to_all | solution.py:729
  82.5 0.9 copy-done.4
  83.4 0.9 copy-done.6
  84.3 2.3 %shard_map.99 = (f32[3,12,256]{2,1,0:T(8,128)S(1)}, f32[4,80,128]{2,1,0:T(8,128)S(1)}) custom-call(s16[8,144,128]{2,1,0:T(8,128)(2,1)S(1)} %all_to_all.26.sent_ref.first_sent_ref, s16[8,80,128]{2,1,0:T(8,128)(2,1)S(1)} %copy-done.6, s16[8,80,128]{2,1,0:T(8,128)(2,1)S(1)} %copy-done.4, f32[12,256]{1,0:T(8,128)} %trace_load_hbm.3, f32[12,256]{1,0:T(8,128)} %shift_hbm.3, ...), custom_call_target="tpu_custom_call" | custom-call | tf_op jit(solution)/shard_map/pallas_call | solution.py:642
  86.6 8.9 %all-to-all-done.3 = f32[256,1,128]{2,1,0:T(1,128)S(1)} async-done(((f32[256,1,128]{2,1,0:T(1,128)}), f32[256,1,128]{2,1,0:T(1,128)S(1)}, u32[]{:S(2)}, u32[]{:S(2)}) %all-to-all-start.3) | async-done | bytes 131104 | tf_op jit(solution)/shard_map/all_to_all | solution.py:729
  95.5 1.0 shard_map.100
  (19 shorter events, 0.2 us)
Async XLA Ops:
  1.3 29.4 %copy-start = (bf16[80,80,128]{2,1,0:T(8,128)(2,1)S(1)}, bf16[80,80,128]{2,1,0:T(8,128)(2,1)}, u32[]{:S(2)}) copy-start(bf16[80,80,128]{2,1,0:T(8,128)(2,1)} %inverse_ref.2) | copy-start | bytes 4915204
  1.3 29.4 %copy-start.1 = (bf16[80,48,128]{2,1,0:T(8,128)(2,1)S(1)}, bf16[80,48,128]{2,1,0:T(8,128)(2,1)}, u32[]{:S(2)}) copy-start(bf16[80,48,128]{2,1,0:T(8,128)(2,1)} %coupling_ref.2) | copy-start | bytes 2949124
  1.3 29.4 %copy-start.2 = (bf16[48,48,128]{2,1,0:T(8,128)(2,1)S(1)}, bf16[48,48,128]{2,1,0:T(8,128)(2,1)}, u32[]{:S(2)}) copy-start(bf16[48,48,128]{2,1,0:T(8,128)(2,1)} %trace_ref.2) | copy-start | bytes 1769476
  1.3 29.4 %copy-start.7 = (s32[4,128]{1,0:T(4,128)S(1)}, s32[4,128]{1,0:T(4,128)}, u32[]{:S(2)}) copy-start(s32[4,128]{1,0:T(4,128)} %names_ref.3) | copy-start | bytes 6148
  4.1 5.8 %collective-permute-start = (s16[32,128]{1,0:T(8,128)(2,1)S(1)}, s16[32,128]{1,0:T(8,128)(2,1)S(1)}, u32[]{:S(2)}, u32[]{:S(2)}) collective-permute-start(s16[32,128]{1,0:T(8,128)(2,1)S(1)} %get-tuple-element.40), channel_id=1, source_target_pairs={{8,16},{24,32},{40,48},{56,64},{72,80},{88,96},{104,112},{120,128}... | collective-permute-start | bytes 24584 | tf_op jit(solution)/shard_map/ppermute | solution.py:663
  8.6 1.3 %collective-permute-start.1 = (s16[32,128]{1,0:T(8,128)(2,1)S(1)}, s16[32,128]{1,0:T(8,128)(2,1)S(1)}, u32[]{:S(2)}, u32[]{:S(2)}) collective-permute-start(s16[32,128]{1,0:T(8,128)(2,1)S(1)} %get-tuple-element.41), channel_id=1, source_target_pairs={{0,8},{8,0},{16,24},{24,16},{32,40},{40,32},{48,56},{56,48},{64,72... | collective-permute-start | bytes 24584 | tf_op jit(solution)/shard_map/ppermute | solution.py:664
  32.9 4.2 %collective-permute-start.3 = (s16[16,128]{1,0:T(8,128)(2,1)S(1)}, s16[16,128]{1,0:T(8,128)(2,1)S(1)}, u32[]{:S(2)}, u32[]{:S(2)}) collective-permute-start(s16[16,128]{1,0:T(8,128)(2,1)S(1)} %get-tuple-element.44), channel_id=1, source_target_pairs={{0,8},{8,0},{16,24},{24,16},{32,40},{40,32},{48,56},{56,48},{64,72... | collective-permute-start | bytes 12296 | tf_op jit(solution)/shard_map/ppermute | solution.py:664
  33.9 4.9 %collective-permute-start.2 = (s16[16,128]{1,0:T(8,128)(2,1)S(1)}, s16[16,128]{1,0:T(8,128)(2,1)S(1)}, u32[]{:S(2)}, u32[]{:S(2)}) collective-permute-start(s16[16,128]{1,0:T(8,128)(2,1)S(1)} %get-tuple-element.43), channel_id=1, source_target_pairs={{8,16},{24,32},{40,48},{56,64},{72,80},{88,96},{104,112},{120,128}... | collective-permute-start | bytes 12296 | tf_op jit(solution)/shard_map/ppermute | solution.py:663
  49.5 1.5 %copy-start.5 = (s16[8,80,128]{2,1,0:T(8,128)(2,1)}, s16[8,80,128]{2,1,0:T(8,128)(2,1)S(1)}, u32[]{:S(2)}) copy-start(s16[8,80,128]{2,1,0:T(8,128)(2,1)S(1)} %all_to_all.27.sent_ref.second_sent_ref) | copy-start | bytes 491524
  51.1 5.8 %collective-permute-start.5 = (s16[16,128]{1,0:T(8,128)(2,1)S(1)}, s16[16,128]{1,0:T(8,128)(2,1)S(1)}, u32[]{:S(2)}, u32[]{:S(2)}) collective-permute-start(s16[16,128]{1,0:T(8,128)(2,1)S(1)} %get-tuple-element.55), channel_id=1, source_target_pairs={{0,8},{8,0},{16,24},{24,16},{32,40},{40,32},{48,56},{56,48},{64,72... | collective-permute-start | bytes 12296 | tf_op jit(solution)/shard_map/ppermute | solution.py:664
  51.2 7.3 %collective-permute-start.4 = (s16[16,128]{1,0:T(8,128)(2,1)S(1)}, s16[16,128]{1,0:T(8,128)(2,1)S(1)}, u32[]{:S(2)}, u32[]{:S(2)}) collective-permute-start(s16[16,128]{1,0:T(8,128)(2,1)S(1)} %get-tuple-element.54), channel_id=1, source_target_pairs={{8,16},{24,32},{40,48},{56,64},{72,80},{88,96},{104,112},{120,128}... | collective-permute-start | bytes 12296 | tf_op jit(solution)/shard_map/ppermute | solution.py:663
  69.2 2.1 %copy-start.3 = (s16[8,80,128]{2,1,0:T(8,128)(2,1)}, s16[8,80,128]{2,1,0:T(8,128)(2,1)S(1)}, u32[]{:S(2)}) copy-start(s16[8,80,128]{2,1,0:T(8,128)(2,1)S(1)} %all_to_all.28.sent_ref.third_sent_ref) | copy-start | bytes 491524
  71.2 24.2 %all-to-all-start.3 = ((f32[256,1,128]{2,1,0:T(1,128)}), f32[256,1,128]{2,1,0:T(1,128)S(1)}, u32[]{:S(2)}, u32[]{:S(2)}) async-start(f32[256,1,128]{2,1,0:T(1,128)} %bitcast.7), calls=%async_computation.3 | async-start | bytes 262144 | tf_op jit(solution)/shard_map/all_to_all | solution.py:729
  82.4 0.9 copy-start.4
  83.4 0.9 copy-start.6
